TPU v7x, 256 devices: a whole 4x4x8 slice. The times are simulated.
256 devices in a mesh: slab: 64 (over z, x, core), own: 4 (over y).
Axes of the slice: x: 4, y: 4, z: 8, core: 2. Of those that a mesh axis runs over, the one named last changes fastest.
Arguments:
- src_factor: float32 [256, 131072], P('own', 'slab'), may hold values from -5 to 5
- dst_factor: float32 [256, 131072], P('own', 'slab'), may hold values from -5 to 5
- hour_factor: float32 [512, 256], P('slab', 'own'), may hold values from 0.5 to 2
- tile_src: int32 [1920], P('slab'), may hold values from 0 to 1023, as said below
- tile_dst: int32 [1920], P('slab'), may hold values from 0 to 1023, as said below
- tile_hour: int32 [1920], P('slab'), may hold values from 0 to 511, as said below
- tile_count: int32 [64], P('slab'), may hold values from 2 to 30, as said below
- src_place: int32 [1024], replicated, may hold values from 0 to 1023, as said below
- dst_place: int32 [1024], replicated, may hold values from 0 to 1023, as said below
- tile_bits: int32 [1920, 8, 128], P('slab'), may hold values from 0 to 65535
Outputs:
- grad_src: float32 [256, 131072], P('own', 'slab')
- grad_dst: float32 [256, 131072], P('own', 'slab')
- grad_hour: float32 [512, 256], P('slab', 'own')
Inputs may be any that keep to these rules, and one draw needn't show every extreme that they name: `tile_src`: slots s * 30 to s * 30 + 29 form slab group s. Among one group's slots, padded ones included, the source blocks whose storage position lies on one storage slab index (src_place[id] // 16) are at most 2 different ones; every group has a storage slab index with 2. `tile_dst`: the same holds for destination blocks with dst_place. `tile_hour`: A tile of slab group s has an hour of s * 8 to s * 8 + 7. `tile_count`: some group fills all 30 slots, some has 2 live tiles. `src_place`: A permutation of the block ids. `dst_place`: A permutation of the block ids.
All inputs are finite; a program needn't handle non-finite values.
Results may differ from a plain program's by a relative error of at most 0.0003.
Values sent between devices are 32-bit elements; how exact they have to be, the bound alone decides.
No kernel may reach another device: no remote copies, remote signals or barrier semaphores. Data moves between devices by JAX's collectives and lax.ppermute only.
A program may use at most 64 MiB of HBM per device.

v0:
```python
import jax
import jax.numpy as jnp
from jax import lax
from jax.experimental import pallas as pl
from jax.experimental.pallas import tpu as pltpu
from jax.sharding import Mesh, PartitionSpec as P

NZ, NX, NC, NO = 8, 4, 2, 4
SLAB = ("z", "x", "c")
GROUPS = 64
TILE_CAP = 30
SIDE = 128
RK = 64
STORED = 16
SLOTS = 5
ROWS = 3 * SLOTS + 1
PER = 10
ROUND = PER * NO
VMEM = pl.BlockSpec(memory_space=pltpu.VMEM)
SMEM = pl.BlockSpec(memory_space=pltpu.SMEM)
ANY = pl.BlockSpec(memory_space=pl.ANY)
f32, bf16, i32 = jnp.float32, jnp.bfloat16, jnp.int32
PARAMS = pltpu.CompilerParams(vmem_limit_bytes=48 * 1024 * 1024)


def lane_block(within):
    return pl.ds(pl.multiple_of(within * SIDE, SIDE), SIDE)


def split(x):
    hi = x.astype(bf16)
    return hi, (x - hi.astype(f32)).astype(bf16)


def dot3(a, b, dims):
    dg = lambda p, q: lax.dot_general(p, q, (dims, ((), ())), preferred_element_type=f32)
    return dg(a[0], b[0]) + (dg(a[0], b[1]) + dg(a[1], b[0]))


def as_column(row):
    return jnp.broadcast_to(row, (SIDE, RK)).T


def send_kernel(scal, src_ids, dst_ids, hours, src_place, dst_place, bits, hour_rows, out, where, count):
    own, first_hour, live, pair_round = scal[0], scal[1], scal[2], scal[3]

    @pl.loop(0, GROUPS)
    def _(g):
        count[g] = 0

    out[...] = jnp.zeros_like(out)
    lane = lax.broadcasted_iota(i32, (1, SIDE), 1)

    def step(t, hist):
        src_at = src_place[src_ids[t]]
        dst_at = dst_place[dst_ids[t]]
        to = (src_at // 128) * 8 + (dst_at // STORED) % 8
        rank = count[to]
        slot = rank - pair_round * SLOTS
        here = (t < live) & (slot >= 0) & (slot < SLOTS)
        where[t] = jnp.where(here, to * 8 + slot, -1)

        @pl.when(t < live)
        def _():
            count[to] = rank + 1

        @pl.when(here)
        def _():
            for i in range(2):
                out[to, pl.ds(3 * slot + i, 1), :] = bits[t, pl.ds(2 * own + i, 1), :].astype(f32)
            c = hour_rows[pl.ds(hours[t] - first_hour, 1), :]
            row = jnp.concatenate([c, jnp.zeros_like(c)], axis=1)
            row = jnp.where(lane == 64, 1.0, row)
            row = jnp.where(lane == 65, src_at.astype(f32), row)
            row = jnp.where(lane == 66, dst_at.astype(f32), row)
            out[to, pl.ds(3 * slot + 2, 1), :] = row

        return hist + jnp.where((lane == to) & (t < live), 1.0, 0.0)

    hist = lax.fori_loop(0, TILE_CAP, step, jnp.zeros((1, SIDE), f32))
    out[:, ROWS - 1 : ROWS, :] = jnp.broadcast_to(hist[None], (GROUPS, 1, SIDE))


def list_kernel(scal, meta, lst):
    base = scal[3]

    def scan(i, n):
        pos = n - base
        valid = meta[3 * i]

        @pl.when((valid == 1) & (pos >= 0) & (pos < ROUND))
        def _():
            lst[pos] = meta[3 * i + 1]
            lst[ROUND + pos] = meta[3 * i + 2]
            lst[2 * ROUND + pos] = i

        return n + valid

    total = lax.fori_loop(0, GROUPS * SLOTS, scan, 0)
    lst[3 * ROUND] = jnp.clip(total - base, 0, ROUND)


def each_tile(own, n, d, work):
    to = jnp.bitwise_and(own + d, NO - 1)

    @pl.loop(0, jnp.right_shift(n - to + NO - 1, 2))
    def _(j):
        work(j, NO * j + to)


def slot_row(slot):
    return (slot // SLOTS) * ROWS + 3 * (slot % SLOTS)


def src_pack_kernel(scal, lst, a00, a10, a30, a2t0, a2b0, a01, a11, a31, a2t1, a2b1, *outs):
    own, x_at, c_at = scal[0], scal[1], scal[2]
    sources = (
        ((a00,), (a01,)), ((a10,), (a11,)), ((a2t0, a2b0), (a2t1, a2b1)), ((a30,), (a31,)),
    )
    for d in range(NO):

        def work(j, k):
            src_at = lst[k]
            cols = lane_block(jnp.bitwise_and(src_at, STORED - 1))
            dx = jnp.bitwise_and(jnp.right_shift(src_at, 5) - x_at, NX - 1)
            dc = jnp.bitwise_and(jnp.right_shift(src_at, 4) + c_at, NC - 1)
            for sx in range(NX):
                for sc in range(NC):

                    @pl.when((dx == sx) & (dc == sc))
                    def _():
                        refs = sources[sx][sc]
                        step = RK // len(refs)
                        for h, ref in enumerate(refs):
                            outs[d][j, h * step : (h + 1) * step, :] = ref[:, cols]

        each_tile(own, lst[3 * ROUND], d, work)


def dst_pack_kernel(scal, lst, recv, b, *rest):
    outs = rest[-NO:]
    for d in range(NO):

        def work(j, k):
            dst_at = lst[ROUND + k]
            row = slot_row(lst[2 * ROUND + k])
            c = as_column(recv[pl.ds(row + 2, 1), :RK])
            cols = lane_block(jnp.bitwise_and(dst_at, STORED - 1))
            outs[d][j, :RK, :] = b[jnp.right_shift(dst_at, 7), :, cols] * c
            for i in range(2):
                outs[d][j, RK + i : RK + i + 1, :] = recv[pl.ds(row + i, 1), :]

        each_tile(scal[0], lst[3 * ROUND], d, work)


def tile_kernel(scal, lst, a0, a1, a2, a3, b0, b1, b2, b3, u0, u1, u2, u3, g0, g1, g2, g3, res):
    own = scal[0]
    n = lst[3 * ROUND]
    a_in, b_in, u_out, g_out = (a0, a1, a2, a3), (b0, b1, b2, b3), (u0, u1, u2, u3), (g0, g1, g2, g3)
    shift = lax.broadcasted_iota(i32, (32, SIDE), 0) % 16

    @pl.loop(0, jnp.right_shift(n - own + NO - 1, 2))
    def _(j):
        a = split(jnp.concatenate([r[j] for r in a_in], axis=0))
        b = split(jnp.concatenate([r[j, :RK] for r in b_in], axis=0))
        res[...] = dot3(a, b, ((0,), (0,)))
        for d in range(NO):
            rows = pl.ds(pl.multiple_of(jnp.bitwise_and(own - d, NO - 1) * 32, 32), 32)
            words = jnp.concatenate(
                [jnp.broadcast_to(b_in[d][j, RK + i : RK + i + 1, :], (16, SIDE)) for i in range(2)], axis=0
            ).astype(i32)
            entries = (jnp.right_shift(words, shift) & 1).astype(f32)
            res[rows, :] = jax.nn.sigmoid(res[rows, :]) - entries
        r = split(res[...])
        u = dot3(b, r, ((1,), (1,)))
        g = dot3(a, r, ((1,), (0,)))
        for d in range(NO):
            u_out[d][j] = u[RK * d : RK * (d + 1)]
            g_out[d][j] = g[RK * d : RK * (d + 1)]


def dst_sum_kernel(scal, lst, recv, b, g0, g1, g2, g3, out, hour):
    out[...] = jnp.zeros_like(out)
    hour[...] = jnp.zeros_like(hour)
    ones = jnp.ones((8, SIDE), f32)
    for d, g in enumerate((g0, g1, g2, g3)):

        def work(j, k):
            dst_at = lst[ROUND + k]
            slot = lst[2 * ROUND + k]
            c = as_column(recv[pl.ds(slot_row(slot) + 2, 1), :RK])
            z = jnp.right_shift(dst_at, 7)
            cols = lane_block(jnp.bitwise_and(dst_at, STORED - 1))
            part = g[j]
            out[z, :, cols] += part * c
            row = lax.dot_general(
                ones, b[z, :, cols] * part, (((1,), (1,)), ((), ())),
                precision=lax.Precision.HIGHEST, preferred_element_type=f32,
            )
            hour[slot // SLOTS, pl.ds(slot % SLOTS, 1), :RK] = row[:1]

        each_tile(scal[0], lst[3 * ROUND], d, work)


def src_sum_kernel(scal, lst, u0, u1, u2, u3, back, keep, give):
    own, x_at, c_at = scal[0], scal[1], scal[2]
    keep[...] = jnp.zeros_like(keep)
    give[...] = jnp.zeros_like(give)
    for d, u in enumerate((u0, u1, u2, u3)):

        def work(j, k):
            src_at = lst[k]
            cols = lane_block(jnp.bitwise_and(src_at, STORED - 1))
            dx = jnp.bitwise_and(jnp.right_shift(src_at, 5) - x_at, NX - 1)
            dc = jnp.bitwise_and(jnp.right_shift(src_at, 4) + c_at, NC - 1)
            for sc, total in enumerate((keep, give)):

                @pl.when(dc == sc)
                def _():
                    total[dx, :, cols] += u[j]

        each_tile(own, lst[3 * ROUND], d, work)


def hour_kernel(scal, hours, where, back, out):
    first_hour = scal[1]
    out[...] = jnp.zeros_like(out)

    @pl.loop(0, TILE_CAP)
    def _(t):
        at = where[t]

        @pl.when(at >= 0)
        def _():
            h = hours[t] - first_hour
            out[pl.ds(h, 1), :] += back[at // 8, pl.ds(at % 8, 1), :RK]


def shape(*dims, dtype=f32):
    return jax.ShapeDtypeStruct(dims, dtype)


def call(kernel, out_shape, in_specs, args, out_specs=None, scratch=()):
    if out_specs is None:
        out_specs = jax.tree.map(lambda _: VMEM, out_shape)
    return pl.pallas_call(
        kernel, out_shape=out_shape, in_specs=in_specs, out_specs=out_specs,
        scratch_shapes=scratch, compiler_params=PARAMS,
    )(*args)


def hop(value, axis, size, by):
    return lax.ppermute(value, axis, [(i, (i + by) % size) for i in range(size)])


def per_device(
    src_factor, dst_factor, hour_factor, tile_src, tile_dst, tile_hour, tile_count, src_place, dst_place, tile_bits
):
    z_at, x_at, c_at, own = (lax.axis_index(n).astype(i32) for n in ("z", "x", "c", "own"))
    first_hour = ((z_at * NX + x_at) * NC + c_at) * hour_factor.shape[0]
    live = tile_count[0]
    half = RK // 2

    with jax.named_scope("gather_dst"):
        b_all = lax.all_gather(dst_factor, "z", axis=0)
    with jax.named_scope("gather_src"):
        up = hop(src_factor, "x", NX, 1)
        down = hop(src_factor, "x", NX, -1)
        far_top = hop(up[:half], "x", NX, 1)
        far_bottom = hop(down[half:], "x", NX, -1)
        mine = (src_factor, down, up, far_top, far_bottom)
        a_all = mine + tuple(hop(v, "c", NC, 1) for v in mine)

    def one_round(pair_round, base):
        with jax.named_scope("slots"):
            scal = jnp.stack([own, first_hour, live, pair_round])
            sent, where = call(
                send_kernel, (shape(GROUPS, ROWS, SIDE), shape(TILE_CAP, dtype=i32)),
                [SMEM] * 6 + [VMEM] * 2,
                (scal, tile_src, tile_dst, tile_hour, src_place, dst_place, tile_bits, hour_factor),
                out_specs=(VMEM, SMEM), scratch=[pltpu.SMEM((GROUPS,), i32)],
            )
            got = lax.all_to_all(sent, SLAB, 0, 0)
            meta = got[:, 2 : ROWS - 1 : 3, RK : RK + 3].astype(i32).reshape(-1)
            rows = got.reshape(GROUPS * ROWS, SIDE)
            hist = got[:, ROWS - 1, :GROUPS].astype(i32)
        at = jnp.stack([own, x_at, c_at, base])
        with jax.named_scope("list"):
            lst = call(list_kernel, shape(3 * ROUND + 8, dtype=i32), [SMEM] * 2, (at, meta), out_specs=SMEM)
        with jax.named_scope("src_exchange"):
            a_out = call(
                src_pack_kernel, (shape(PER, RK, SIDE),) * NO, [SMEM] * 2 + [VMEM] * 10, (at, lst) + a_all
            )
            a_in = [v if d == 0 else hop(v, "own", NO, d) for d, v in enumerate(a_out)]
        with jax.named_scope("dst_exchange"):
            b_out = call(
                dst_pack_kernel, (shape(PER, RK + 8, SIDE),) * NO, [SMEM] * 2 + [VMEM] * 2 + [ANY] * NO,
                (at, lst, rows, b_all, *a_in),
            )
            b_in = [v if d == 0 else hop(v, "own", NO, d) for d, v in enumerate(b_out)]
        with jax.named_scope("tiles"):
            parts = call(
                tile_kernel, (shape(PER, RK, SIDE),) * (2 * NO), [SMEM] * 2 + [VMEM] * 8,
                (at, lst, *a_in, *b_in), scratch=[pltpu.VMEM((SIDE, SIDE), f32)],
            )
        with jax.named_scope("dst_back"):
            g = [v if d == 0 else hop(v, "own", NO, -d) for d, v in enumerate(parts[NO:])]
            g_sum, hour_terms = call(
                dst_sum_kernel, (shape(NZ, RK, STORED * SIDE), shape(GROUPS, 8, SIDE)),
                [SMEM] * 2 + [VMEM] * (2 + NO), (at, lst, rows, b_all, *g),
            )
            grad_dst = lax.psum_scatter(g_sum, "z", scatter_dimension=0)
        with jax.named_scope("hours"):
            back = lax.all_to_all(hour_terms, SLAB, 0, 0)
            grad_hour = call(
                hour_kernel, shape(*hour_factor.shape), [SMEM] * 3 + [VMEM], (scal, tile_hour, where, back)
            )
        with jax.named_scope("src_back"):
            u = [v if d == 0 else hop(v, "own", NO, -d) for d, v in enumerate(parts[:NO])]
            keep, give = call(
                src_sum_kernel, (shape(NX, RK, STORED * SIDE),) * 2, [SMEM] * 2 + [VMEM] * NO + [ANY],
                (at, lst, *u, back),
            )
            s = keep + hop(give, "c", NC, 1)
            top = hop(s[2, :half], "x", NX, 1)
            bottom = hop(s[2, half:], "x", NX, -1)
            one = hop(jnp.concatenate([s[1, :half] + top, s[1, half:]]), "x", NX, 1)
            three = hop(jnp.concatenate([s[3, :half], s[3, half:] + bottom]), "x", NX, -1)
            grad_src = s[0] + one + three
        return (grad_src, grad_dst, grad_hour), hist

    zero = jnp.zeros((), i32)
    grads, hist = one_round(zero, zero)

    def busiest(pair_round):
        return jnp.max(jnp.sum(jnp.clip(hist - pair_round * SLOTS, 0, SLOTS), axis=0))

    def following(pair_round, base):
        more = base + ROUND < busiest(pair_round)
        return jnp.where(more, pair_round, pair_round + 1), jnp.where(more, base + ROUND, 0)

    def body(state):
        pair_round, base, sums = state
        terms, _ = one_round(pair_round, base)
        return following(pair_round, base) + (jax.tree.map(jnp.add, sums, terms),)

    last = lax.while_loop(lambda state: jnp.max(hist) > state[0] * SLOTS, body, following(zero, zero) + (grads,))
    return last[2]


def solution(mesh):
    fine = Mesh(mesh.devices.reshape(NZ, NX, NC, NO), SLAB + ("own",))
    return jax.shard_map(
        per_device,
        mesh=fine,
        in_specs=(
            P("own", SLAB), P("own", SLAB), P(SLAB, "own"), P(SLAB), P(SLAB), P(SLAB), P(SLAB), P(), P(),
            P(SLAB, None, None),
        ),
        out_specs=(P("own", SLAB), P("own", SLAB), P(SLAB, "own")),
        check_vma=False,
    )
```

profile of v0, /device:TPU:32, one launch (start us, length us, event | category | flops | bytes accessed | tf_op | source)
XLA Modules:
  0.0 208.9 jit_solution(2506378307299177774)
XLA Ops:
  7.9 1.6 collective-permute-start.18
  9.5 1.7 collective-permute-start.17
  11.9 3.5 %slots.2 = (f32[64,16,128]{2,1,0:T(8,128)}, s32[30]{0:T(128)S(1)}) custom-call(s32[4]{0:T(128)S(1)} %pad_add_fusion.3.scal, s32[30]{0:T(128)} %src_ids.1, s32[30]{0:T(128)} %dst_ids.1, s32[30]{0:T(128)} %hours.6, s32[1024]{0:T(1024)} %src_place.1, s32[1024]{0:T(1024)} %dst_place.1, s32[30,8,128]{2,1,0:T(8,128)} %bits.1, f32[8,64]{1,0:T(8,128)} %hour_rows.1), custom_call_target="tpu_custom_call" | custom-call | tf_op jit(solution)/shard_map/slots/pallas_call | solution.py:246
  15.4 10.3 %all-to-all-start.2 = ((f32[64,16,128]{2,1,0:T(8,128)}), f32[64,16,128]{2,1,0:T(8,128)S(1)}, u32[]{:S(2)}, u32[]{:S(2)}) async-start(f32[64,16,128]{2,1,0:T(8,128)} %get-tuple-element.197), calls=%async_computation.3 | async-start | bytes 1048576 | tf_op jit(solution)/shard_map/slots/all_to_all | solution.py:283
  26.1 1.6 collective-permute-start.19
  27.7 1.0 slice.77
  28.6 1.9 collective-permute-start.20
  31.0 7.2 %collective-permute-done.19.a2t0 = f32[32,2048]{1,0:T(8,128)} collective-permute-done((f32[32,2048]{1,0:T(8,128)S(1)}, f32[32,2048]{1,0:T(8,128)}, u32[]{:S(2)}, u32[]{:S(2)}) %collective-permute-start.19) | collective-permute-done | bytes 262176 | tf_op jit(solution)/shard_map/gather_src/ppermute | solution.py:253
  38.2 1.4 collective-permute-done.20.a2b0
  39.7 8.9 %all-to-all-done.2 = f32[64,16,128]{2,1,0:T(8,128)S(1)} async-done(((f32[64,16,128]{2,1,0:T(8,128)}), f32[64,16,128]{2,1,0:T(8,128)S(1)}, u32[]{:S(2)}, u32[]{:S(2)}) %all-to-all-start.2) | async-done | bytes 524320 | tf_op jit(solution)/shard_map/slots/all_to_all | solution.py:283
  49.4 6.1 %list.2.lst = s32[128]{0:T(128)S(1)} custom-call(s32[4]{0:T(128)S(1)} %pad_add_fusion.2.scal, s32[960]{0:T(1024)S(1)} %reshape.19.meta), custom_call_target="tpu_custom_call" | custom-call | tf_op jit(solution)/shard_map/list/pallas_call | solution.py:246
  55.6 3.5 %src_exchange.2 = (f32[10,64,128]{2,1,0:T(8,128)S(1)}, f32[10,64,128]{2,1,0:T(8,128)S(1)}, f32[10,64,128]{2,1,0:T(8,128)S(1)}, f32[10,64,128]{2,1,0:T(8,128)S(1)}) custom-call(s32[4]{0:T(128)S(1)} %pad_add_fusion.2.scal, s32[128]{0:T(128)S(1)} %list.2.lst, f32[64,2048]{1,0:T(8,128)} %a00.1, f32[64,2048]{1,0:T(8,128)} %collective-permute-done.17.a10, ...), custom_call_target="tpu_custom_call" | custom-call | tf_op jit(solution)/shard_map/src_exchange/pallas_call | solution.py:246
  59.1 1.7 collective-permute-start.26
  60.7 2.9 %collective-permute-start.27 = (f32[10,64,128]{2,1,0:T(8,128)S(1)}, f32[10,64,128]{2,1,0:T(8,128)S(1)}, u32[]{:S(2)}, u32[]{:S(2)}) collective-permute-start(f32[10,64,128]{2,1,0:T(8,128)S(1)} %get-tuple-element.200), channel_id=1, source_target_pairs={{0,2},{1,3},{2,0},{3,1},{4,6},{5,7},{6,4},{7,5},{8,10},{9,11},{10,... | collective-permute-start | bytes 983048 | tf_op jit(solution)/shard_map/src_exchange/ppermute | solution.py:253
  63.6 1.4 collective-permute-start.28
  65.0 5.0 %collective-permute-done.26.rest_1_.a1 = f32[10,64,128]{2,1,0:T(8,128)S(1)} collective-permute-done((f32[10,64,128]{2,1,0:T(8,128)S(1)}, f32[10,64,128]{2,1,0:T(8,128)S(1)}, u32[]{:S(2)}, u32[]{:S(2)}) %collective-permute-start.26) | collective-permute-done | bytes 327712 | tf_op jit(solution)/shard_map/src_exchange/ppermute | solution.py:253
  70.0 8.2 %collective-permute-done.27.rest_2_.a2 = f32[10,64,128]{2,1,0:T(8,128)S(1)} collective-permute-done((f32[10,64,128]{2,1,0:T(8,128)S(1)}, f32[10,64,128]{2,1,0:T(8,128)S(1)}, u32[]{:S(2)}, u32[]{:S(2)}) %collective-permute-start.27) | collective-permute-done | bytes 327712 | tf_op jit(solution)/shard_map/src_exchange/ppermute | solution.py:253
  78.2 4.7 %dst_exchange.2 = (f32[10,72,128]{2,1,0:T(8,128)S(1)}, f32[10,72,128]{2,1,0:T(8,128)S(1)}, f32[10,72,128]{2,1,0:T(8,128)S(1)}, f32[10,72,128]{2,1,0:T(8,128)S(1)}) custom-call(s32[4]{0:T(128)S(1)} %pad_add_fusion.2.scal, s32[128]{0:T(128)S(1)} %list.2.lst, f32[1024,128]{1,0:T(8,128)S(1)} %bitcast.87, f32[8,64,2048]{2,1,0:T(8,128)} %bitcast.89, ...), custom_call_target="tpu_custom_call" | custom-call | tf_op jit(solution)/shard_map/dst_exchange/pallas_call | solution.py:246
  82.9 1.3 collective-permute-start.29
  84.2 2.4 %collective-permute-start.30 = (f32[10,72,128]{2,1,0:T(8,128)S(1)}, f32[10,72,128]{2,1,0:T(8,128)S(1)}, u32[]{:S(2)}, u32[]{:S(2)}) collective-permute-start(f32[10,72,128]{2,1,0:T(8,128)S(1)} %get-tuple-element.204), channel_id=1, source_target_pairs={{0,2},{1,3},{2,0},{3,1},{4,6},{5,7},{6,4},{7,5},{8,10},{9,11},{10,... | collective-permute-start | bytes 1105928 | tf_op jit(solution)/shard_map/dst_exchange/ppermute | solution.py:253
  86.6 1.6 collective-permute-start.31
  88.2 5.5 %collective-permute-done.29.b1 = f32[10,72,128]{2,1,0:T(8,128)S(1)} collective-permute-done((f32[10,72,128]{2,1,0:T(8,128)S(1)}, f32[10,72,128]{2,1,0:T(8,128)S(1)}, u32[]{:S(2)}, u32[]{:S(2)}) %collective-permute-start.29) | collective-permute-done | bytes 368672 | tf_op jit(solution)/shard_map/dst_exchange/ppermute | solution.py:253
  93.7 9.0 %collective-permute-done.30.b2 = f32[10,72,128]{2,1,0:T(8,128)S(1)} collective-permute-done((f32[10,72,128]{2,1,0:T(8,128)S(1)}, f32[10,72,128]{2,1,0:T(8,128)S(1)}, u32[]{:S(2)}, u32[]{:S(2)}) %collective-permute-start.30) | collective-permute-done | bytes 368672 | tf_op jit(solution)/shard_map/dst_exchange/ppermute | solution.py:253
  102.7 4.6 %tiles.2 = (f32[10,64,128]{2,1,0:T(8,128)S(1)}, f32[10,64,128]{2,1,0:T(8,128)S(1)}, f32[10,64,128]{2,1,0:T(8,128)S(1)}, f32[10,64,128]{2,1,0:T(8,128)S(1)}, f32[...) custom-call(s32[4]{0:T(128)S(1)} %pad_add_fusion.2.scal, ...), custom_call_target="tpu_custom_call" | custom-call | tf_op jit(solution)/shard_map/tiles/pallas_call | solution.py:246
  107.3 1.7 collective-permute-start.35
  109.0 0.8 collective-permute-start.36
  110.0 12.7 %collective-permute-done.35.g1 = f32[10,64,128]{2,1,0:T(8,128)S(1)} collective-permute-done((f32[10,64,128]{2,1,0:T(8,128)S(1)}, f32[10,64,128]{2,1,0:T(8,128)S(1)}, u32[]{:S(2)}, u32[]{:S(2)}) %collective-permute-start.35) | collective-permute-done | bytes 327712 | tf_op jit(solution)/shard_map/dst_back/ppermute | solution.py:253
  122.6 3.7 %collective-permute-done.37.g3 = f32[10,64,128]{2,1,0:T(8,128)S(1)} collective-permute-done((f32[10,64,128]{2,1,0:T(8,128)S(1)}, f32[10,64,128]{2,1,0:T(8,128)S(1)}, u32[]{:S(2)}, u32[]{:S(2)}) %collective-permute-start.37) | collective-permute-done | bytes 327712 | tf_op jit(solution)/shard_map/dst_back/ppermute | solution.py:253
  126.3 7.2 %dst_back.2 = (f32[8,64,2048]{2,1,0:T(8,128)}, f32[64,8,128]{2,1,0:T(8,128)}) custom-call(s32[4]{0:T(128)S(1)} %pad_add_fusion.2.scal, s32[128]{0:T(128)S(1)} %list.2.lst, f32[1024,128]{1,0:T(8,128)S(1)} %bitcast.88, f32[8,64,2048]{2,1,0:T(8,128)S(1)} %bitcast.91, f32[10,64,128]{2,1,0:T(8,128)S(1)} %get-tuple-element.210.g0, ...), custom_call_target="tpu_custom_call" | custom-call | tf_op jit(solution)/shard_map/dst_back/pallas_call | solution.py:246
  133.5 11.1 %all-to-all-start.3 = ((f32[64,8,128]{2,1,0:T(8,128)}), f32[64,8,128]{2,1,0:T(8,128)S(1)}, u32[]{:S(2)}, u32[]{:S(2)}) async-start(f32[64,8,128]{2,1,0:T(8,128)} %get-tuple-element.214), calls=%async_computation.4 | async-start | bytes 524288 | tf_op jit(solution)/shard_map/hours/all_to_all | solution.py:314
  145.2 1.2 collective-permute-start.33
  146.4 0.8 collective-permute-start.34
  147.2 8.0 %collective-permute-done.32.u1 = f32[10,64,128]{2,1,0:T(8,128)S(1)} collective-permute-done((f32[10,64,128]{2,1,0:T(8,128)S(1)}, f32[10,64,128]{2,1,0:T(8,128)S(1)}, u32[]{:S(2)}, u32[]{:S(2)}) %collective-permute-start.32) | collective-permute-done | bytes 327712 | tf_op jit(solution)/shard_map/src_back/ppermute | solution.py:253
  155.2 2.2 %collective-permute-done.33.u2 = f32[10,64,128]{2,1,0:T(8,128)S(1)} collective-permute-done((f32[10,64,128]{2,1,0:T(8,128)S(1)}, f32[10,64,128]{2,1,0:T(8,128)S(1)}, u32[]{:S(2)}, u32[]{:S(2)}) %collective-permute-start.33) | collective-permute-done | bytes 327712 | tf_op jit(solution)/shard_map/src_back/ppermute | solution.py:253
  157.4 5.9 %collective-permute-done.34.u3 = f32[10,64,128]{2,1,0:T(8,128)S(1)} collective-permute-done((f32[10,64,128]{2,1,0:T(8,128)S(1)}, f32[10,64,128]{2,1,0:T(8,128)S(1)}, u32[]{:S(2)}, u32[]{:S(2)}) %collective-permute-start.34) | collective-permute-done | bytes 327712 | tf_op jit(solution)/shard_map/src_back/ppermute | solution.py:253
  163.3 1.5 src_back.2
  164.9 4.1 %collective-permute-done.38 = f32[4,64,2048]{2,1,0:T(8,128)S(1)} collective-permute-done((f32[4,64,2048]{2,1,0:T(8,128)S(1)}, f32[4,64,2048]{2,1,0:T(8,128)S(1)}, u32[]{:S(2)}, u32[]{:S(2)}) %collective-permute-start.38) | collective-permute-done | bytes 2097184 | tf_op jit(solution)/shard_map/src_back/ppermute | solution.py:253
  169.5 1.6 collective-permute-start.39
  171.1 1.7 collective-permute-start.41
  172.8 6.3 %collective-permute-done.39 = f32[32,2048]{1,0:T(8,128)S(1)} collective-permute-done((f32[32,2048]{1,0:T(8,128)S(1)}, f32[32,2048]{1,0:T(8,128)S(1)}, u32[]{:S(2)}, u32[]{:S(2)}) %collective-permute-start.39) | collective-permute-done | bytes 262176 | tf_op jit(solution)/shard_map/src_back/ppermute | solution.py:253
  179.3 3.0 %collective-permute-start.42 = (f32[64,2048]{1,0:T(8,128)S(1)}, f32[64,2048]{1,0:T(8,128)}, u32[]{:S(2)}, u32[]{:S(2)}) collective-permute-start(f32[64,2048]{1,0:T(8,128)S(1)} %pad_maximum_fusion.3), channel_id=1, source_target_pairs={{0,24},{8,0},{16,8},{24,16},{1,25},{9,1},{17,9},{25,17},{2,26},{10... | collective-permute-start | bytes 1572872 | tf_op jit(solution)/shard_map/src_back/ppermute | solution.py:253
  182.3 0.8 pad_maximum_fusion.2
  185.8 1.2 hours.5
  187.0 5.7 %collective-permute-done.42 = f32[64,2048]{1,0:T(8,128)} collective-permute-done((f32[64,2048]{1,0:T(8,128)S(1)}, f32[64,2048]{1,0:T(8,128)}, u32[]{:S(2)}, u32[]{:S(2)}) %collective-permute-start.42) | collective-permute-done | bytes 524320 | tf_op jit(solution)/shard_map/src_back/ppermute | solution.py:253
  192.7 4.4 %collective-permute-done.40 = f32[64,2048]{1,0:T(8,128)S(1)} collective-permute-done((f32[64,2048]{1,0:T(8,128)}, f32[64,2048]{1,0:T(8,128)S(1)}, u32[]{:S(2)}, u32[]{:S(2)}) %collective-permute-start.40) | collective-permute-done | bytes 524320 | tf_op jit(solution)/shard_map/src_back/ppermute | solution.py:253
  197.1 2.1 fusion.6
  199.3 2.2 %while.16 = (s32[]{:T(128)}, s32[]{:T(128)}, f32[64,2048]{1,0:T(8,128)}, f32[64,2048]{1,0:T(8,128)}, f32[8,64]{1,0:T(8,128)S(1)}, /*index=5*/s32[64,64]{1,0:T(8,...) while((s32[]{:T(128)}, s32[]{:T(128)}, ...), condition=%wide.region_7.9_spmd, body=%wide.region_3.7_spmd.sunk | while | flops 1459678 | bytes 80509168 | solution.py:347
  199.3 1.4 reduce_max.28
  (64 shorter events, 6.6 us)
Async XLA Ops:
  7.2 71.0 %all-gather.3.cloned.1.call-start = ((), (), s32[]{:S(2)}) async-start(), calls=%async_computation.7 | async-start | bytes 4718592 | tf_op jit(solution)/shard_map/gather_dst/all_gather | solution.py:265
  7.9 18.2 %collective-permute-start.18 = (f32[64,2048]{1,0:T(8,128)}, f32[64,2048]{1,0:T(8,128)S(1)}, u32[]{:S(2)}, u32[]{:S(2)}) collective-permute-start(f32[64,2048]{1,0:T(8,128)} %a00.1), channel_id=1, source_target_pairs={{0,8},{8,16},{16,24},{24,0},{1,9},{9,17},{17,25},{25,1},{2,10},{10... | collective-permute-start | bytes 1572872 | tf_op jit(solution)/shard_map/gather_src/ppermute | solution.py:253
  9.5 18.2 %collective-permute-start.17 = (f32[64,2048]{1,0:T(8,128)}, f32[64,2048]{1,0:T(8,128)}, u32[]{:S(2)}, u32[]{:S(2)}) collective-permute-start(f32[64,2048]{1,0:T(8,128)} %a00.1), channel_id=1, source_target_pairs={{0,24},{8,0},{16,8},{24,16},{1,25},{9,1},{17,9},{25,17},{2,26},{10... | collective-permute-start | bytes 1572872 | tf_op jit(solution)/shard_map/gather_src/ppermute | solution.py:253
  15.4 33.2 %all-to-all-start.2 = ((f32[64,16,128]{2,1,0:T(8,128)}), f32[64,16,128]{2,1,0:T(8,128)S(1)}, u32[]{:S(2)}, u32[]{:S(2)}) async-start(f32[64,16,128]{2,1,0:T(8,128)} %get-tuple-element.197), calls=%async_computation.3 | async-start | bytes 1048576 | tf_op jit(solution)/shard_map/slots/all_to_all | solution.py:283
  25.8 173.4 %reduce-scatter.3.cloned.1.call-start = ((), (), s32[]{:S(2)}) async-start(), calls=%async_computation.6 | async-start | bytes 4718592 | tf_op jit(solution)/shard_map/dst_back/reduce_scatter | solution.py:312
  25.8 29.7 %collective-permute-start.21 = (f32[64,2048]{1,0:T(8,128)}, f32[64,2048]{1,0:T(8,128)}, u32[]{:S(2)}, u32[]{:S(2)}) collective-permute-start(f32[64,2048]{1,0:T(8,128)} %a00.1), channel_id=1, source_target_pairs={{0,4},{4,0},{1,5},{5,1},{2,6},{6,2},{3,7},{7,3},{8,12},{12,8},{9,1... | collective-permute-start | bytes 1572872 | tf_op jit(solution)/shard_map/gather_src/ppermute | solution.py:253
  26.1 33.0 %copy-start.2 = (f32[64,2048]{1,0:T(8,128)}, f32[64,2048]{1,0:T(8,128)S(1)}, u32[]{:S(2)}) copy-start(f32[64,2048]{1,0:T(8,128)S(1)} %collective-permute-done.18.a30) | copy-start | bytes 1572868
  26.1 12.1 %collective-permute-start.19 = (f32[32,2048]{1,0:T(8,128)S(1)}, f32[32,2048]{1,0:T(8,128)}, u32[]{:S(2)}, u32[]{:S(2)}) collective-permute-start(f32[32,2048]{1,0:T(8,128)S(1)} %slice.76), channel_id=1, source_target_pairs={{0,8},{8,16},{16,24},{24,0},{1,9},{9,17},{17,25},{25,1},{2,10},{10... | collective-permute-start | bytes 786440 | tf_op jit(solution)/shard_map/gather_src/ppermute | solution.py:253
  28.6 11.0 %collective-permute-start.20 = (f32[32,2048]{1,0:T(8,128)S(1)}, f32[32,2048]{1,0:T(8,128)}, u32[]{:S(2)}, u32[]{:S(2)}) collective-permute-start(f32[32,2048]{1,0:T(8,128)S(1)} %slice.77), channel_id=1, source_target_pairs={{0,24},{8,0},{16,8},{24,16},{1,25},{9,1},{17,9},{25,17},{2,26},{10... | collective-permute-start | bytes 786440 | tf_op jit(solution)/shard_map/gather_src/ppermute | solution.py:253
  30.5 25.1 %collective-permute-start.23 = (f32[64,2048]{1,0:T(8,128)S(1)}, f32[64,2048]{1,0:T(8,128)}, u32[]{:S(2)}, u32[]{:S(2)}) collective-permute-start(f32[64,2048]{1,0:T(8,128)S(1)} %collective-permute-done.18.a30), channel_id=1, source_target_pairs={{0,4},{4,0},{1,5},{5,1},{2,6},{6,2},{3,7},{7,3},{8,12},{12,8},{9,1... | collective-permute-start | bytes 1572872 | tf_op jit(solution)/shard_map/gather_src/ppermute | solution.py:253
  30.5 25.1 %collective-permute-start.22 = (f32[64,2048]{1,0:T(8,128)}, f32[64,2048]{1,0:T(8,128)}, u32[]{:S(2)}, u32[]{:S(2)}) collective-permute-start(f32[64,2048]{1,0:T(8,128)} %collective-permute-done.17.a10), channel_id=1, source_target_pairs={{0,4},{4,0},{1,5},{5,1},{2,6},{6,2},{3,7},{7,3},{8,12},{12,8},{9,1... | collective-permute-start | bytes 1572872 | tf_op jit(solution)/shard_map/gather_src/ppermute | solution.py:253
  38.2 17.3 %collective-permute-start.24 = (f32[32,2048]{1,0:T(8,128)}, f32[32,2048]{1,0:T(8,128)}, u32[]{:S(2)}, u32[]{:S(2)}) collective-permute-start(f32[32,2048]{1,0:T(8,128)} %collective-permute-done.19.a2t0), channel_id=1, source_target_pairs={{0,4},{4,0},{1,5},{5,1},{2,6},{6,2},{3,7},{7,3},{8,12},{12,8},{9,1... | collective-permute-start | bytes 786440 | tf_op jit(solution)/shard_map/gather_src/ppermute | solution.py:253
  39.6 15.9 %collective-permute-start.25 = (f32[32,2048]{1,0:T(8,128)}, f32[32,2048]{1,0:T(8,128)}, u32[]{:S(2)}, u32[]{:S(2)}) collective-permute-start(f32[32,2048]{1,0:T(8,128)} %collective-permute-done.20.a2b0), channel_id=1, source_target_pairs={{0,4},{4,0},{1,5},{5,1},{2,6},{6,2},{3,7},{7,3},{8,12},{12,8},{9,1... | collective-permute-start | bytes 786440 | tf_op jit(solution)/shard_map/gather_src/ppermute | solution.py:253
  59.1 10.9 %collective-permute-start.26 = (f32[10,64,128]{2,1,0:T(8,128)S(1)}, f32[10,64,128]{2,1,0:T(8,128)S(1)}, u32[]{:S(2)}, u32[]{:S(2)}) collective-permute-start(f32[10,64,128]{2,1,0:T(8,128)S(1)} %get-tuple-element.199), channel_id=1, source_target_pairs={{0,1},{1,2},{2,3},{3,0},{4,5},{5,6},{6,7},{7,4},{8,9},{9,10},{10,1... | collective-permute-start | bytes 983048 | tf_op jit(solution)/shard_map/src_exchange/ppermute | solution.py:253
  60.7 17.4 %collective-permute-start.27 = (f32[10,64,128]{2,1,0:T(8,128)S(1)}, f32[10,64,128]{2,1,0:T(8,128)S(1)}, u32[]{:S(2)}, u32[]{:S(2)}) collective-permute-start(f32[10,64,128]{2,1,0:T(8,128)S(1)} %get-tuple-element.200), channel_id=1, source_target_pairs={{0,2},{1,3},{2,0},{3,1},{4,6},{5,7},{6,4},{7,5},{8,10},{9,11},{10,... | collective-permute-start | bytes 983048 | tf_op jit(solution)/shard_map/src_exchange/ppermute | solution.py:253
  63.6 14.5 %collective-permute-start.28 = (f32[10,64,128]{2,1,0:T(8,128)S(1)}, f32[10,64,128]{2,1,0:T(8,128)S(1)}, u32[]{:S(2)}, u32[]{:S(2)}) collective-permute-start(f32[10,64,128]{2,1,0:T(8,128)S(1)} %get-tuple-element.201), channel_id=1, source_target_pairs={{0,3},{1,0},{2,1},{3,2},{4,7},{5,4},{6,5},{7,6},{8,11},{9,8},{10,9... | collective-permute-start | bytes 983048 | tf_op jit(solution)/shard_map/src_exchange/ppermute | solution.py:253
  78.2 48.1 %copy-start = (f32[512,2048]{1,0:T(8,128)S(1)}, f32[512,2048]{1,0:T(8,128)}, u32[]{:S(2)}) copy-start(f32[512,2048]{1,0:T(8,128)} %all-gather.3.cloned.1.call-done) | copy-start | bytes 12582916
  82.9 10.8 %collective-permute-start.29 = (f32[10,72,128]{2,1,0:T(8,128)S(1)}, f32[10,72,128]{2,1,0:T(8,128)S(1)}, u32[]{:S(2)}, u32[]{:S(2)}) collective-permute-start(f32[10,72,128]{2,1,0:T(8,128)S(1)} %get-tuple-element.203), channel_id=1, source_target_pairs={{0,1},{1,2},{2,3},{3,0},{4,5},{5,6},{6,7},{7,4},{8,9},{9,10},{10,1... | collective-permute-start | bytes 1105928 | tf_op jit(solution)/shard_map/dst_exchange/ppermute | solution.py:253
  84.2 18.5 %collective-permute-start.30 = (f32[10,72,128]{2,1,0:T(8,128)S(1)}, f32[10,72,128]{2,1,0:T(8,128)S(1)}, u32[]{:S(2)}, u32[]{:S(2)}) collective-permute-start(f32[10,72,128]{2,1,0:T(8,128)S(1)} %get-tuple-element.204), channel_id=1, source_target_pairs={{0,2},{1,3},{2,0},{3,1},{4,6},{5,7},{6,4},{7,5},{8,10},{9,11},{10,... | collective-permute-start | bytes 1105928 | tf_op jit(solution)/shard_map/dst_exchange/ppermute | solution.py:253
  86.6 16.1 %collective-permute-start.31 = (f32[10,72,128]{2,1,0:T(8,128)S(1)}, f32[10,72,128]{2,1,0:T(8,128)S(1)}, u32[]{:S(2)}, u32[]{:S(2)}) collective-permute-start(f32[10,72,128]{2,1,0:T(8,128)S(1)} %get-tuple-element.205), channel_id=1, source_target_pairs={{0,3},{1,0},{2,1},{3,2},{4,7},{5,4},{6,5},{7,6},{8,11},{9,8},{10,9... | collective-permute-start | bytes 1105928 | tf_op jit(solution)/shard_map/dst_exchange/ppermute | solution.py:253
  107.3 15.3 %collective-permute-start.35 = (f32[10,64,128]{2,1,0:T(8,128)S(1)}, f32[10,64,128]{2,1,0:T(8,128)S(1)}, u32[]{:S(2)}, u32[]{:S(2)}) collective-permute-start(f32[10,64,128]{2,1,0:T(8,128)S(1)} %get-tuple-element.211), channel_id=1, source_target_pairs={{0,3},{1,0},{2,1},{3,2},{4,7},{5,4},{6,5},{7,6},{8,11},{9,8},{10,9... | collective-permute-start | bytes 983048 | tf_op jit(solution)/shard_map/dst_back/ppermute | solution.py:253
  109.0 13.6 %collective-permute-start.36 = (f32[10,64,128]{2,1,0:T(8,128)S(1)}, f32[10,64,128]{2,1,0:T(8,128)S(1)}, u32[]{:S(2)}, u32[]{:S(2)}) collective-permute-start(f32[10,64,128]{2,1,0:T(8,128)S(1)} %get-tuple-element.212), channel_id=1, source_target_pairs={{0,2},{1,3},{2,0},{3,1},{4,6},{5,7},{6,4},{7,5},{8,10},{9,11},{10,... | collective-permute-start | bytes 983048 | tf_op jit(solution)/shard_map/dst_back/ppermute | solution.py:253
  109.8 16.5 %collective-permute-start.37 = (f32[10,64,128]{2,1,0:T(8,128)S(1)}, f32[10,64,128]{2,1,0:T(8,128)S(1)}, u32[]{:S(2)}, u32[]{:S(2)}) collective-permute-start(f32[10,64,128]{2,1,0:T(8,128)S(1)} %get-tuple-element.213), channel_id=1, source_target_pairs={{0,1},{1,2},{2,3},{3,0},{4,5},{5,6},{6,7},{7,4},{8,9},{9,10},{10,1... | collective-permute-start | bytes 983048 | tf_op jit(solution)/shard_map/dst_back/ppermute | solution.py:253
  133.5 29.7 %all-to-all-start.3 = ((f32[64,8,128]{2,1,0:T(8,128)}), f32[64,8,128]{2,1,0:T(8,128)S(1)}, u32[]{:S(2)}, u32[]{:S(2)}) async-start(f32[64,8,128]{2,1,0:T(8,128)} %get-tuple-element.214), calls=%async_computation.4 | async-start | bytes 524288 | tf_op jit(solution)/shard_map/hours/all_to_all | solution.py:314
  144.6 10.6 %collective-permute-start.32 = (f32[10,64,128]{2,1,0:T(8,128)S(1)}, f32[10,64,128]{2,1,0:T(8,128)S(1)}, u32[]{:S(2)}, u32[]{:S(2)}) collective-permute-start(f32[10,64,128]{2,1,0:T(8,128)S(1)} %get-tuple-element.207), channel_id=1, source_target_pairs={{0,3},{1,0},{2,1},{3,2},{4,7},{5,4},{6,5},{7,6},{8,11},{9,8},{10,9... | collective-permute-start | bytes 983048 | tf_op jit(solution)/shard_map/src_back/ppermute | solution.py:253
  145.2 12.1 %collective-permute-start.33 = (f32[10,64,128]{2,1,0:T(8,128)S(1)}, f32[10,64,128]{2,1,0:T(8,128)S(1)}, u32[]{:S(2)}, u32[]{:S(2)}) collective-permute-start(f32[10,64,128]{2,1,0:T(8,128)S(1)} %get-tuple-element.208), channel_id=1, source_target_pairs={{0,2},{1,3},{2,0},{3,1},{4,6},{5,7},{6,4},{7,5},{8,10},{9,11},{10,... | collective-permute-start | bytes 983048 | tf_op jit(solution)/shard_map/src_back/ppermute | solution.py:253
  146.4 16.8 %collective-permute-start.34 = (f32[10,64,128]{2,1,0:T(8,128)S(1)}, f32[10,64,128]{2,1,0:T(8,128)S(1)}, u32[]{:S(2)}, u32[]{:S(2)}) collective-permute-start(f32[10,64,128]{2,1,0:T(8,128)S(1)} %get-tuple-element.209), channel_id=1, source_target_pairs={{0,1},{1,2},{2,3},{3,0},{4,5},{5,6},{6,7},{7,4},{8,9},{9,10},{10,1... | collective-permute-start | bytes 983048 | tf_op jit(solution)/shard_map/src_back/ppermute | solution.py:253
  164.8 4.2 %collective-permute-start.38 = (f32[4,64,2048]{2,1,0:T(8,128)S(1)}, f32[4,64,2048]{2,1,0:T(8,128)S(1)}, u32[]{:S(2)}, u32[]{:S(2)}) collective-permute-start(f32[4,64,2048]{2,1,0:T(8,128)S(1)} %get-tuple-element.216), channel_id=1, source_target_pairs={{0,4},{4,0},{1,5},{5,1},{2,6},{6,2},{3,7},{7,3},{8,12},{12,8},{9,1... | collective-permute-start | bytes 6291464 | tf_op jit(solution)/shard_map/src_back/ppermute | solution.py:253
  169.4 14.5 %copy-start.4 = (f32[4,64,2048]{2,1,0:T(8,128)}, f32[4,64,2048]{2,1,0:T(8,128)S(1)}, u32[]{:S(2)}) copy-start(f32[4,64,2048]{2,1,0:T(8,128)S(1)} %add.58) | copy-start | bytes 6291460
  169.5 16.3 %copy-start.10 = (s32[30]{0:T(128)S(1)}, s32[30]{0:T(128)}, u32[]{:S(2)}) copy-start(s32[30]{0:T(128)} %hours.6) | copy-start | bytes 364
  169.5 9.6 %collective-permute-start.39 = (f32[32,2048]{1,0:T(8,128)S(1)}, f32[32,2048]{1,0:T(8,128)S(1)}, u32[]{:S(2)}, u32[]{:S(2)}) collective-permute-start(f32[32,2048]{1,0:T(8,128)S(1)} %get-tuple-element.288), channel_id=1, source_target_pairs={{0,8},{8,16},{16,24},{24,0},{1,9},{9,17},{17,25},{25,1},{2,10},{10... | collective-permute-start | bytes 786440 | tf_op jit(solution)/shard_map/src_back/ppermute | solution.py:253
  171.1 8.1 %collective-permute-start.41 = (f32[32,2048]{1,0:T(8,128)S(1)}, f32[32,2048]{1,0:T(8,128)S(1)}, u32[]{:S(2)}, u32[]{:S(2)}) collective-permute-start(f32[32,2048]{1,0:T(8,128)S(1)} %get-tuple-element.289), channel_id=1, source_target_pairs={{0,24},{8,0},{16,8},{24,16},{1,25},{9,1},{17,9},{25,17},{2,26},{10... | collective-permute-start | bytes 786440 | tf_op jit(solution)/shard_map/src_back/ppermute | solution.py:253
  179.2 20.0 %copy-start.3 = (f32[64,2048]{1,0:T(8,128)S(1)}, f32[64,2048]{1,0:T(8,128)}, u32[]{:S(2)}) copy-start(f32[64,2048]{1,0:T(8,128)} %copy-done.2) | copy-start | bytes 1572868
  179.2 20.0 %copy-start.5 = (s32[30,8,128]{2,1,0:T(8,128)S(1)}, s32[30,8,128]{2,1,0:T(8,128)}, u32[]{:S(2)}) copy-start(s32[30,8,128]{2,1,0:T(8,128)} %bits.1) | copy-start | bytes 368644
  179.2 20.0 %copy-start.7 = (s32[1024]{0:T(1024)S(1)}, s32[1024]{0:T(1024)}, u32[]{:S(2)}) copy-start(s32[1024]{0:T(1024)} %src_place.1) | copy-start | bytes 12292
  179.2 20.0 %copy-start.8 = (s32[1024]{0:T(1024)S(1)}, s32[1024]{0:T(1024)}, u32[]{:S(2)}) copy-start(s32[1024]{0:T(1024)} %dst_place.1) | copy-start | bytes 12292
  179.3 20.0 %copy-start.9 = (f32[8,64]{1,0:T(8,128)S(1)}, f32[8,64]{1,0:T(8,128)}, u32[]{:S(2)}) copy-start(f32[8,64]{1,0:T(8,128)} %hour_rows.1) | copy-start | bytes 6148
  179.3 20.0 %copy-start.11 = (s32[30]{0:T(128)S(1)}, s32[30]{0:T(128)}, u32[]{:S(2)}) copy-start(s32[30]{0:T(128)} %src_ids.1) | copy-start | bytes 364
  179.3 20.0 %copy-start.12 = (s32[30]{0:T(128)S(1)}, s32[30]{0:T(128)}, u32[]{:S(2)}) copy-start(s32[30]{0:T(128)} %dst_ids.1) | copy-start | bytes 364
  179.3 13.3 %collective-permute-start.42 = (f32[64,2048]{1,0:T(8,128)S(1)}, f32[64,2048]{1,0:T(8,128)}, u32[]{:S(2)}, u32[]{:S(2)}) collective-permute-start(f32[64,2048]{1,0:T(8,128)S(1)} %pad_maximum_fusion.3), channel_id=1, source_target_pairs={{0,24},{8,0},{16,8},{24,16},{1,25},{9,1},{17,9},{25,17},{2,26},{10... | collective-permute-start | bytes 1572872 | tf_op jit(solution)/shard_map/src_back/ppermute | solution.py:253
  183.2 14.0 %collective-permute-start.40 = (f32[64,2048]{1,0:T(8,128)}, f32[64,2048]{1,0:T(8,128)S(1)}, u32[]{:S(2)}, u32[]{:S(2)}) collective-permute-start(f32[64,2048]{1,0:T(8,128)} %pad_maximum_fusion.2), channel_id=1, source_target_pairs={{0,8},{8,16},{16,24},{24,0},{1,9},{9,17},{17,25},{25,1},{2,10},{10... | collective-permute-start | bytes 1572872 | tf_op jit(solution)/shard_map/src_back/ppermute | solution.py:253
  201.4 0.6 copy-start.6
Sparse Core Ops, SparseCore 0:
  9.8 66.8 all-gather.2
  133.6 59.2 reduce-scatter.2
where the time goes:
time: 209 us
  waiting for transfers between devices  99 us (47%)
  starting transfers between devices  51.8 us (25%)
  Pallas kernels  32.2 us (15%)
  between operations  15.6 us (7%)
  other arithmetic  6.91 us (3%)
  local copies, waits for them, and re-layouts  2.5 us (1%)
    ppermute x26, waiting for transfers between devices, hop(): lax.ppermute(value, axis, [(i, (i + by) % size) for i in range(size)])  89.4 us
    pallas_call x8, Pallas kernels, call(): pl.pallas_call(kernel, out_shape=out_shape, in_specs=in_specs, out_specs=...  32.2 us
    ppermute x26, starting transfers between devices, hop(): lax.ppermute(value, axis, [(i, (i + by) % size) for i in range(size)])  30.4 us
    all_to_all x1, starting transfers between devices, one_round(): back = lax.all_to_all(hour_terms, SLAB, 0, 0)  11.1 us
    all_to_all x1, starting transfers between devices, one_round(): got = lax.all_to_all(sent, SLAB, 0, 0)  10.3 us
    all_to_all x1, waiting for transfers between devices, one_round(): got = lax.all_to_all(sent, SLAB, 0, 0)  8.92 us
  transfers between devices with their start and end apart: 30, of which 16 were waited for; matrix products, arithmetic and copies ran while one was open for 4% of the time, Pallas kernels for 8%

commit v1 on v0

v1 whole, which is shorter than its diff:
```python
import jax
import jax.numpy as jnp
from jax import lax
from jax.experimental import pallas as pl
from jax.experimental.pallas import tpu as pltpu
from jax.sharding import Mesh, PartitionSpec as P

NZ, NX, NC, NO = 8, 4, 2, 4
SLAB = ("z", "x", "c")
GROUPS = 64
TILE_CAP = 30
SIDE = 128
RK = 64
RANK = RK * NO
STORED = 16
PART = STORED // NO * SIDE
SLOTS = 5
ROWS = 3 * SLOTS + 1
PER = 16
LIST = NO * PER
XROWS = RK + 8
VMEM = pl.BlockSpec(memory_space=pltpu.VMEM)
SMEM = pl.BlockSpec(memory_space=pltpu.SMEM)
f32, bf16, i32 = jnp.float32, jnp.bfloat16, jnp.int32
PARAMS = pltpu.CompilerParams(vmem_limit_bytes=48 * 1024 * 1024)


def lane_block(within):
    return pl.ds(pl.multiple_of(within * SIDE, SIDE), SIDE)


def split(x):
    hi = x.astype(bf16)
    return hi, (x - hi.astype(f32)).astype(bf16)


def dot3(a, b, dims):
    dg = lambda p, q: lax.dot_general(p, q, (dims, ((), ())), preferred_element_type=f32)
    return dg(a[0], b[0]) + (dg(a[0], b[1]) + dg(a[1], b[0]))


def as_column(row):
    return jnp.broadcast_to(row, (SIDE, RK)).T


def send_kernel(scal, src_ids, dst_ids, hours, src_place, dst_place, bits, hour_rows, out, where, count):
    own, first_hour, live, pair_round = scal[0], scal[1], scal[2], scal[3]

    @pl.loop(0, GROUPS)
    def _(g):
        count[g] = 0

    out[...] = jnp.zeros_like(out)
    lane = lax.broadcasted_iota(i32, (1, SIDE), 1)

    def step(t, told):
        src_at = src_place[src_ids[t]]
        dst_at = dst_place[dst_ids[t]]
        to = jnp.right_shift(src_at, 7) * 8 + jnp.bitwise_and(jnp.right_shift(dst_at, 4), 7)
        rank = count[to]
        slot = rank - pair_round * SLOTS
        here = (t < live) & (slot >= 0) & (slot < SLOTS)
        where[t] = jnp.where(here, to * 8 + slot, -1)

        @pl.when(t < live)
        def _():
            count[to] = rank + 1

        @pl.when(here)
        def _():
            for i in range(2):
                out[to, pl.ds(3 * slot + i, 1), :] = bits[t, pl.ds(2 * own + i, 1), :].astype(f32)
            c = hour_rows[pl.ds(hours[t] - first_hour, 1), :]
            row = jnp.concatenate([c, jnp.zeros_like(c)], axis=1)
            row = jnp.where(lane == 64, 1.0, row)
            row = jnp.where(lane == 65, src_at.astype(f32), row)
            row = jnp.where(lane == 66, dst_at.astype(f32), row)
            out[to, pl.ds(3 * slot + 2, 1), :] = row

        alive = t < live
        told = jnp.where(lane == t, jnp.where(alive, src_at, -1).astype(f32), told)
        told = jnp.where(lane == t + 32, dst_at.astype(f32), told)
        return jnp.where(lane == t + 64, rank.astype(f32), told)

    told = lax.fori_loop(0, TILE_CAP, step, jnp.zeros((1, SIDE), f32))
    out[:, ROWS - 1 : ROWS, :] = jnp.broadcast_to(told[None], (GROUPS, 1, SIDE))


def list_kernel(scal, meta, lst, seen):
    base = scal[3]
    for o in range(NO):
        seen[o] = 0

    @pl.loop(0, GROUPS)
    def _(g):
        for s in range(SLOTS):
            i = g * SLOTS + s

            @pl.when(meta[3 * i] == 1)
            def _():
                dst_at = meta[3 * i + 2]
                to = jnp.bitwise_and(jnp.right_shift(dst_at, 2), NO - 1)
                pos = seen[to] - base
                seen[to] += 1

                @pl.when((pos >= 0) & (pos < PER))
                def _():
                    at = to * PER + pos
                    lst[at] = meta[3 * i + 1]
                    lst[LIST + at] = dst_at
                    lst[2 * LIST + at] = i

    for o in range(NO):
        lst[3 * LIST + o] = jnp.clip(seen[o] - base, 0, PER)


def each_tile(own, lst, d, work):
    to = jnp.bitwise_and(own + d, NO - 1)

    @pl.loop(0, lst[3 * LIST + to])
    def _(j):
        work(j, PER * to + j)


def slot_row(slot):
    return (slot // SLOTS) * ROWS + 3 * (slot % SLOTS)


def src_pack_kernel(scal, lst, recv, a00, a10, a30, a2t0, a2b0, a01, a11, a31, a2t1, a2b1, *outs):
    own, x_at, c_at = scal[0], scal[1], scal[2]
    sources = (
        ((a00,), (a01,)), ((a10,), (a11,)), ((a2t0, a2b0), (a2t1, a2b1)), ((a30,), (a31,)),
    )
    for d in range(NO):

        def work(j, k):
            src_at = lst[k]
            row = slot_row(lst[2 * LIST + k])
            cols = lane_block(jnp.bitwise_and(src_at, STORED - 1))
            dx = jnp.bitwise_and(jnp.right_shift(src_at, 5) - x_at, NX - 1)
            dc = jnp.bitwise_and(jnp.right_shift(src_at, 4) + c_at, NC - 1)
            for sx in range(NX):
                for sc in range(NC):

                    @pl.when((dx == sx) & (dc == sc))
                    def _():
                        refs = sources[sx][sc]
                        step = RK // len(refs)
                        for h, ref in enumerate(refs):
                            outs[d][j, h * step : (h + 1) * step, :] = ref[:, cols]

            for i in range(3):
                outs[d][j, RK + i : RK + i + 1, :] = recv[pl.ds(row + i, 1), :]

        each_tile(own, lst, d, work)


def tile_kernel(scal, lst, a0, a1, a2, a3, b_all, g_sum, u0, u1, u2, u3, res):
    own = scal[0]
    a_in, u_out = (a0, a1, a2, a3), (u0, u1, u2, u3)
    shift = jnp.bitwise_and(lax.broadcasted_iota(i32, (32, SIDE), 0), 15)
    ones = jnp.ones((8, SIDE), f32)
    g_sum[...] = jnp.zeros_like(g_sum)

    def work(j, k):
        dst_at = lst[LIST + k]
        z = jnp.right_shift(dst_at, 7)
        cols = lane_block(jnp.bitwise_and(dst_at, STORED // NO - 1))
        b_raw = b_all[z, :, cols]
        c = jnp.concatenate([as_column(r[j, RK + 2 : RK + 3, :RK]) for r in a_in], axis=0)
        a = split(jnp.concatenate([r[j, :RK] for r in a_in], axis=0))
        b = split(b_raw * c)
        res[...] = dot3(a, b, ((0,), (0,)))
        for d in range(NO):
            rows = pl.ds(pl.multiple_of(jnp.bitwise_and(own - d, NO - 1) * 32, 32), 32)
            words = jnp.concatenate(
                [jnp.broadcast_to(a_in[d][j, RK + i : RK + i + 1, :], (16, SIDE)) for i in range(2)], axis=0
            ).astype(i32)
            entries = jnp.bitwise_and(jnp.right_shift(words, shift), 1).astype(f32)
            res[rows, :] = jax.nn.sigmoid(res[rows, :]) - entries
        r = split(res[...])
        u = dot3(b, r, ((1,), (1,)))
        g = dot3(a, r, ((1,), (0,)))
        g_sum[z, :, cols] += g * c
        h = lax.dot_general(
            ones, b_raw * g, (((1,), (1,)), ((), ())),
            precision=lax.Precision.HIGHEST, preferred_element_type=f32,
        )
        for d in range(NO):
            u_out[d][j, :RK] = u[RK * d : RK * (d + 1)]
            u_out[d][j, RK : RK + 1, :RK] = h[:1, RK * d : RK * (d + 1)]

    each_tile(own, lst, 0, work)


def src_sum_kernel(scal, lst, u0, u1, u2, u3, keep, give, hour):
    own, x_at, c_at = scal[0], scal[1], scal[2]
    for ref in (keep, give, hour):
        ref[...] = jnp.zeros_like(ref)
    for d, u in enumerate((u0, u1, u2, u3)):

        def work(j, k):
            src_at = lst[k]
            slot = lst[2 * LIST + k]
            cols = lane_block(jnp.bitwise_and(src_at, STORED - 1))
            dx = jnp.bitwise_and(jnp.right_shift(src_at, 5) - x_at, NX - 1)
            dc = jnp.bitwise_and(jnp.right_shift(src_at, 4) + c_at, NC - 1)
            for sc, total in enumerate((keep, give)):

                @pl.when(dc == sc)
                def _():
                    total[dx, :, cols] += u[j, :RK]

            hour[slot // SLOTS, pl.ds(slot % SLOTS, 1), :RK] = u[j, RK : RK + 1, :RK]

        each_tile(own, lst, d, work)


def hour_kernel(scal, hours, where, back, out):
    first_hour = scal[1]
    out[...] = jnp.zeros_like(out)

    @pl.loop(0, TILE_CAP)
    def _(t):
        at = where[t]

        @pl.when(at >= 0)
        def _():
            h = hours[t] - first_hour
            out[pl.ds(h, 1), :] += back[jnp.right_shift(at, 3), pl.ds(jnp.bitwise_and(at, 7), 1), :RK]


def shape(*dims, dtype=f32):
    return jax.ShapeDtypeStruct(dims, dtype)


def call(kernel, out_shape, in_specs, args, out_specs=None, scratch=()):
    if out_specs is None:
        out_specs = jax.tree.map(lambda _: VMEM, out_shape)
    return pl.pallas_call(
        kernel, out_shape=out_shape, in_specs=in_specs, out_specs=out_specs,
        scratch_shapes=scratch, compiler_params=PARAMS,
    )(*args)


def hop(value, axis, size, by):
    if by == 0:
        return value
    return lax.ppermute(value, axis, [(i, (i + by) % size) for i in range(size)])


def per_device(
    src_factor, dst_factor, hour_factor, tile_src, tile_dst, tile_hour, tile_count, src_place, dst_place, tile_bits
):
    z_at, x_at, c_at, own = (lax.axis_index(n).astype(i32) for n in ("z", "x", "c", "own"))
    first_hour = ((z_at * NX + x_at) * NC + c_at) * hour_factor.shape[0]
    live = tile_count[0]
    half = RK // 2

    def part_of(d):
        return jnp.bitwise_and(own + d, NO - 1) * PART

    with jax.named_scope("gather_dst"):
        parts = [hop(lax.dynamic_slice(dst_factor, (0, part_of(d)), (RK, PART)), "own", NO, d) for d in range(NO)]
        b_all = lax.all_gather(jnp.concatenate(parts, axis=0), "z", axis=0)
    with jax.named_scope("gather_src"):
        up = hop(src_factor, "x", NX, 1)
        down = hop(src_factor, "x", NX, -1)
        far_top = hop(up[:half], "x", NX, 1)
        far_bottom = hop(down[half:], "x", NX, -1)
        mine = (src_factor, down, up, far_top, far_bottom)
        a_all = mine + tuple(hop(v, "c", NC, 1) for v in mine)

    def one_round(pair_round, base):
        with jax.named_scope("slots"):
            scal = jnp.stack([own, first_hour, live, pair_round])
            sent, where = call(
                send_kernel, (shape(GROUPS, ROWS, SIDE), shape(TILE_CAP, dtype=i32)),
                [SMEM] * 6 + [VMEM] * 2,
                (scal, tile_src, tile_dst, tile_hour, src_place, dst_place, tile_bits, hour_factor),
                out_specs=(VMEM, SMEM), scratch=[pltpu.SMEM((GROUPS,), i32)],
            )
            got = lax.all_to_all(sent, SLAB, 0, 0)
            meta = got[:, 2 : ROWS - 1 : 3, RK : RK + 3].astype(i32).reshape(-1)
            rows = got.reshape(GROUPS * ROWS, SIDE)
            told = got[:, ROWS - 1].astype(i32)
        at = jnp.stack([own, x_at, c_at, base])
        with jax.named_scope("list"):
            lst = call(
                list_kernel, shape(3 * LIST + 8, dtype=i32), [SMEM] * 2, (at, meta), out_specs=SMEM,
                scratch=[pltpu.SMEM((NO,), i32)],
            )
        with jax.named_scope("src_exchange"):
            a_out = call(
                src_pack_kernel, (shape(PER, XROWS, SIDE),) * NO, [SMEM] * 2 + [VMEM] * 11, (at, lst, rows) + a_all
            )
            a_in = [hop(v, "own", NO, d) for d, v in enumerate(a_out)]
        with jax.named_scope("tiles"):
            g_sum, *u_out = call(
                tile_kernel, (shape(NZ, RANK, PART),) + (shape(PER, XROWS, SIDE),) * NO, [SMEM] * 2 + [VMEM] * 5,
                (at, lst, *a_in, b_all), scratch=[pltpu.VMEM((SIDE, SIDE), f32)],
            )
        with jax.named_scope("dst_back"):
            g_part = lax.psum_scatter(g_sum, "z", scatter_dimension=0)
            grad_dst = jnp.zeros_like(dst_factor)
            for d in range(NO):
                piece = hop(g_part[RK * d : RK * (d + 1)], "own", NO, -d)
                grad_dst = lax.dynamic_update_slice(grad_dst, piece, (0, part_of(d)))
        with jax.named_scope("src_back"):
            u = [hop(v, "own", NO, -d) for d, v in enumerate(u_out)]
            keep, give, hour_terms = call(
                src_sum_kernel, (shape(NX, RK, STORED * SIDE),) * 2 + (shape(GROUPS, 8, SIDE),),
                [SMEM] * 2 + [VMEM] * NO, (at, lst, *u),
            )
            s = keep + hop(give, "c", NC, 1)
            top = hop(s[2, :half], "x", NX, 1)
            bottom = hop(s[2, half:], "x", NX, -1)
            one = hop(jnp.concatenate([s[1, :half] + top, s[1, half:]]), "x", NX, 1)
            three = hop(jnp.concatenate([s[3, :half], s[3, half:] + bottom]), "x", NX, -1)
            grad_src = s[0] + one + three
        with jax.named_scope("hours"):
            back = lax.all_to_all(hour_terms, SLAB, 0, 0)
            grad_hour = call(
                hour_kernel, shape(*hour_factor.shape), [SMEM] * 3 + [VMEM], (scal, tile_hour, where, back)
            )
        return (grad_src, grad_dst, grad_hour), told

    zero = jnp.zeros((), i32)
    grads, told = one_round(zero, zero)

    src_at, dst_at, rank = (told[:, 32 * i : 32 * i + TILE_CAP].reshape(-1) for i in range(3))
    worker = (src_at // 128) * 32 + (dst_at // STORED) % 8 * NO + dst_at % STORED // NO
    alive = src_at >= 0

    def busiest(pair_round):
        here = alive & (rank // SLOTS == pair_round)
        counts = jnp.sum((worker[None, :] == jnp.arange(GROUPS * NO, dtype=i32)[:, None]) & here[None, :], axis=1)
        return jnp.max(counts.astype(i32))

    def following(pair_round, base):
        more = base + PER < busiest(pair_round)
        return jnp.where(more, pair_round, pair_round + 1), jnp.where(more, base + PER, 0)

    def body(state):
        pair_round, base, sums = state
        terms, _ = one_round(pair_round, base)
        return following(pair_round, base) + (jax.tree.map(jnp.add, sums, terms),)

    top_rank = jnp.max(jnp.where(alive, rank, -1))
    last = lax.while_loop(lambda state: top_rank >= state[0] * SLOTS, body, following(zero, zero) + (grads,))
    return last[2]


def solution(mesh):
    fine = Mesh(mesh.devices.reshape(NZ, NX, NC, NO), SLAB + ("own",))
    return jax.shard_map(
        per_device,
        mesh=fine,
        in_specs=(
            P("own", SLAB), P("own", SLAB), P(SLAB, "own"), P(SLAB), P(SLAB), P(SLAB), P(SLAB), P(), P(),
            P(SLAB, None, None),
        ),
        out_specs=(P("own", SLAB), P("own", SLAB), P(SLAB, "own")),
        check_vma=False,
    )
```

time: 209 us -> 223 us (1.067); the launches traced: 209 us -> 221 us
  local copies, waits for them, and re-layouts: 2.5 us -> 16.8 us
  Pallas kernels: 32.2 us -> 28.1 us
  other arithmetic: 6.91 us -> 9.6 us
    ppermute x26, waiting for transfers between devices: 89.4 us -> 79 us  [hop(): lax.ppermute(value, axis, [(i, (i + by) % size) for i in range(size)])]
    all_to_all x1, waiting for transfers between devices: 0.01 us -> 9.17 us  [one_round(): back = lax.all_to_all(hour_terms, SLAB, 0, 0)]
    all_to_all x1, starting transfers between devices: 11.1 us -> 5.14 us  [one_round(): back = lax.all_to_all(hour_terms, SLAB, 0, 0)]
    ppermute x26, starting transfers between devices: 30.4 us -> 35.6 us  [hop(): lax.ppermute(value, axis, [(i, (i + by) % size) for i in range(size)])]
    unnamed x24 -> x52, local copies, waits for them, and re-layouts: 0.65 us -> 5.3 us
    pallas_call x8 -> x6, Pallas kernels: 32.2 us -> 28.1 us  [call(): pl.pallas_call(kernel, out_shape=out_shape, in_specs=in_specs, out_specs=...]
    dynamic_update_slice x0 -> x4, local copies, waits for them, and re-layouts: none -> 3.56 us  [one_round(): grad_dst = lax.dynamic_update_slice(grad_dst, piece, (0, part_of(d)))]
  transfers between devices with their start and end apart: 30 -> 30, of which waited for: 16 -> 17; matrix products, arithmetic and copies ran while one was open for 4% -> 8% of each run, Pallas kernels for 8% -> 8%
where the time goes in v1:
time: 223 us; the launch traced here: 221 us
  waiting for transfers between devices  98.1 us (44%)
  starting transfers between devices  51.3 us (23%)
  Pallas kernels  28.1 us (13%)
  local copies, waits for them, and re-layouts  16.8 us (8%)
  between operations  15.7 us (7%)
  other arithmetic  9.6 us (4%)
    ppermute x26, waiting for transfers between devices, hop(): lax.ppermute(value, axis, [(i, (i + by) % size) for i in range(size)])  79 us
    ppermute x26, starting transfers between devices, hop(): lax.ppermute(value, axis, [(i, (i + by) % size) for i in range(size)])  35.6 us
    pallas_call x6, Pallas kernels, call(): pl.pallas_call(kernel, out_shape=out_shape, in_specs=in_specs, out_specs=...  28.1 us
    all_to_all x1, starting transfers between devices, one_round(): got = lax.all_to_all(sent, SLAB, 0, 0)  10.5 us
    all_to_all x1, waiting for transfers between devices, one_round(): got = lax.all_to_all(sent, SLAB, 0, 0)  9.89 us
    all_to_all x1, waiting for transfers between devices, one_round(): back = lax.all_to_all(hour_terms, SLAB, 0, 0)  9.17 us
    unnamed x52, local copies, waits for them, and re-layouts  5.3 us
    all_to_all x1, starting transfers between devices, one_round(): back = lax.all_to_all(hour_terms, SLAB, 0, 0)  5.14 us
  transfers between devices with their start and end apart: 30, of which 17 were waited for; matrix products, arithmetic and copies ran while one was open for 8% of the time, Pallas kernels for 8%

profile of v1, /device:TPU:32, one launch (start us, length us, event | category | flops | bytes accessed | tf_op | source)
XLA Modules:
  0.0 220.6 jit_solution(13939592093391411956)
XLA Ops:
  7.3 1.2 constant_dynamic-slice_fusion.3
  8.5 1.7 collective-permute-start.26
  10.2 2.9 %collective-permute-start.27 = (f32[64,512]{1,0:T(8,128)S(1)}, f32[64,512]{1,0:T(8,128)S(1)}, u32[]{:S(2)}, u32[]{:S(2)}) collective-permute-start(f32[64,512]{1,0:T(8,128)S(1)} %get-tuple-element.568), channel_id=1, source_target_pairs={{0,2},{1,3},{2,0},{3,1},{4,6},{5,7},{6,4},{7,5},{8,10},{9,11},{10,... | collective-permute-start | bytes 393224 | tf_op jit(solution)/shard_map/gather_dst/ppermute | solution.py:249
  13.1 1.3 collective-permute-start.28
  15.1 4.0 %collective-permute-done.27 = f32[64,512]{1,0:T(8,128)S(1)} collective-permute-done((f32[64,512]{1,0:T(8,128)S(1)}, f32[64,512]{1,0:T(8,128)S(1)}, u32[]{:S(2)}, u32[]{:S(2)}) %collective-permute-start.27) | collective-permute-done | bytes 131104 | tf_op jit(solution)/shard_map/gather_dst/ppermute | solution.py:249
  20.0 1.6 collective-permute-start.15
  21.5 1.7 collective-permute-start.14
  24.0 3.0 %slots.5 = (f32[64,16,128]{2,1,0:T(8,128)}, s32[30]{0:T(128)S(1)}) custom-call(s32[4]{0:T(128)S(1)} %pad_add_fusion.3.scal, s32[30]{0:T(128)S(1)} %copy-done.29, s32[30]{0:T(128)S(1)} %copy-done.32, s32[30]{0:T(128)S(1)} %copy-done.25, s32[1024]{0:T(1024)} %src_place.1, s32[1024]{0:T(1024)} %dst_place.1, s32[30,8,128]{2,1,0:T(8,128)S(1)} %copy-done.20, ...), custom_call_target="tpu_custom_call" | custom-call | tf_op jit(solution)/shard_map/slots/pallas_call | solution.py:240
  27.0 10.5 %all-to-all-start.2 = ((f32[64,16,128]{2,1,0:T(8,128)}), f32[64,16,128]{2,1,0:T(8,128)S(1)}, u32[]{:S(2)}, u32[]{:S(2)}) async-start(f32[64,16,128]{2,1,0:T(8,128)} %get-tuple-element.454), calls=%async_computation.3 | async-start | bytes 1048576 | tf_op jit(solution)/shard_map/slots/all_to_all | solution.py:283
  37.8 1.6 collective-permute-start.16
  39.4 1.9 collective-permute-start.17
  41.8 8.1 %collective-permute-done.16.a2t0 = f32[32,2048]{1,0:T(8,128)S(1)} collective-permute-done((f32[32,2048]{1,0:T(8,128)S(1)}, f32[32,2048]{1,0:T(8,128)S(1)}, u32[]{:S(2)}, u32[]{:S(2)}) %collective-permute-start.16) | collective-permute-done | bytes 262176 | tf_op jit(solution)/shard_map/gather_src/ppermute | solution.py:249
  50.4 9.9 %all-to-all-done.2 = f32[64,16,128]{2,1,0:T(8,128)S(1)} async-done(((f32[64,16,128]{2,1,0:T(8,128)}), f32[64,16,128]{2,1,0:T(8,128)S(1)}, u32[]{:S(2)}, u32[]{:S(2)}) %all-to-all-start.2) | async-done | bytes 524320 | tf_op jit(solution)/shard_map/slots/all_to_all | solution.py:283
  60.3 1.5 slice.154
  61.8 1.7 convert_element_type.27
  63.5 1.1 reshape.216.meta
  64.7 5.5 %list.2.lst = s32[200]{0:T(256)S(1)} custom-call(s32[4]{0:T(128)S(1)} %pad_add_fusion.2.scal, s32[960]{0:T(1024)S(1)} %reshape.216.meta), custom_call_target="tpu_custom_call" | custom-call | tf_op jit(solution)/shard_map/list/pallas_call | solution.py:240
  71.9 3.6 %src_exchange.5 = (f32[16,72,128]{2,1,0:T(8,128)S(1)}, f32[16,72,128]{2,1,0:T(8,128)S(1)}, f32[16,72,128]{2,1,0:T(8,128)S(1)}, f32[16,72,128]{2,1,0:T(8,128)S(1)}) custom-call(s32[4]{0:T(128)S(1)} %pad_add_fusion.2.scal, s32[200]{0:T(256)S(1)} %list.2.lst, f32[1024,128]{1,0:T(8,128)S(1)} %bitcast.105, f32[64,2048]{1,0:T(8,128)S(1)} %copy-done.11, ...), custom_call_target="tpu_custom_call" | custom-call | tf_op jit(solution)/shard_map/src_exchange/pallas_call | solution.py:240
  75.5 1.3 collective-permute-start.23
  76.8 2.4 %collective-permute-start.24 = (f32[16,72,128]{2,1,0:T(8,128)S(1)}, f32[16,72,128]{2,1,0:T(8,128)S(1)}, u32[]{:S(2)}, u32[]{:S(2)}) collective-permute-start(f32[16,72,128]{2,1,0:T(8,128)S(1)} %get-tuple-element.457), channel_id=1, source_target_pairs={{0,2},{1,3},{2,0},{3,1},{4,6},{5,7},{6,4},{7,5},{8,10},{9,11},{10,... | collective-permute-start | bytes 1769480 | tf_op jit(solution)/shard_map/src_exchange/ppermute | solution.py:249
  79.2 1.6 collective-permute-start.25
  80.8 11.8 %collective-permute-done.23.a1 = f32[16,72,128]{2,1,0:T(8,128)S(1)} collective-permute-done((f32[16,72,128]{2,1,0:T(8,128)S(1)}, f32[16,72,128]{2,1,0:T(8,128)S(1)}, u32[]{:S(2)}, u32[]{:S(2)}) %collective-permute-start.23) | collective-permute-done | bytes 589856 | tf_op jit(solution)/shard_map/src_exchange/ppermute | solution.py:249
  92.6 12.5 %collective-permute-done.24.a2 = f32[16,72,128]{2,1,0:T(8,128)S(1)} collective-permute-done((f32[16,72,128]{2,1,0:T(8,128)S(1)}, f32[16,72,128]{2,1,0:T(8,128)S(1)}, u32[]{:S(2)}, u32[]{:S(2)}) %collective-permute-start.24) | collective-permute-done | bytes 589856 | tf_op jit(solution)/shard_map/src_exchange/ppermute | solution.py:249
  105.3 11.2 %tiles.5 = (f32[8,256,512]{2,1,0:T(8,128)}, f32[16,72,128]{2,1,0:T(8,128)S(1)}, f32[16,72,128]{2,1,0:T(8,128)S(1)}, f32[16,72,128]{2,1,0:T(8,128)S(1)}, f32[16,72,128]{2,1,0:T(8,128)S(1)}) custom-call(s32[4]{0:T(128)S(1)} %pad_add_fusion.2.scal, s32[200]{0:T(256)S(1)} %list.2.lst, f32[16,72,128]{2,1,0:T(8,128)S(1)} %get-tuple-element.455.a0, ...), custom_call_target="tpu_custom_call" | custom-call | tf_op jit(solution)/shard_map/tiles/pallas_call | solution.py:240
  119.0 1.0 copy-done.5
  120.1 4.8 %collective-permute-start.29 = (f32[16,72,128]{2,1,0:T(8,128)S(1)}, f32[16,72,128]{2,1,0:T(8,128)S(1)}, u32[]{:S(2)}, u32[]{:S(2)}) collective-permute-start(f32[16,72,128]{2,1,0:T(8,128)S(1)} %copy-done.5), channel_id=1, source_target_pairs={{0,3},{1,0},{2,1},{3,2},{4,7},{5,4},{6,5},{7,6},{8,11},{9,8},{10,9... | collective-permute-start | bytes 1769480 | tf_op jit(solution)/shard_map/src_back/ppermute | solution.py:249
  124.9 1.2 collective-permute-start.30
  126.1 1.2 collective-permute-start.31
  127.4 8.8 %collective-permute-done.29.u1 = f32[16,72,128]{2,1,0:T(8,128)S(1)} collective-permute-done((f32[16,72,128]{2,1,0:T(8,128)S(1)}, f32[16,72,128]{2,1,0:T(8,128)S(1)}, u32[]{:S(2)}, u32[]{:S(2)}) %collective-permute-start.29) | collective-permute-done | bytes 589856 | tf_op jit(solution)/shard_map/src_back/ppermute | solution.py:249
  136.1 6.5 %collective-permute-done.30.u2 = f32[16,72,128]{2,1,0:T(8,128)S(1)} collective-permute-done((f32[16,72,128]{2,1,0:T(8,128)S(1)}, f32[16,72,128]{2,1,0:T(8,128)S(1)}, u32[]{:S(2)}, u32[]{:S(2)}) %collective-permute-start.30) | collective-permute-done | bytes 589856 | tf_op jit(solution)/shard_map/src_back/ppermute | solution.py:249
  142.7 12.3 %collective-permute-done.31.u3 = f32[16,72,128]{2,1,0:T(8,128)S(1)} collective-permute-done((f32[16,72,128]{2,1,0:T(8,128)S(1)}, f32[16,72,128]{2,1,0:T(8,128)S(1)}, u32[]{:S(2)}, u32[]{:S(2)}) %collective-permute-start.31) | collective-permute-done | bytes 589856 | tf_op jit(solution)/shard_map/src_back/ppermute | solution.py:249
  155.0 3.3 %src_back.5 = (f32[4,64,2048]{2,1,0:T(8,128)S(1)}, f32[4,64,2048]{2,1,0:T(8,128)}, f32[64,8,128]{2,1,0:T(8,128)}) custom-call(s32[4]{0:T(128)S(1)} %pad_add_fusion.2.scal, s32[200]{0:T(256)S(1)} %list.2.lst, f32[16,72,128]{2,1,0:T(8,128)S(1)} %get-tuple-element.459.u0, f32[16,72,128]{2,1,0:T(8,128)S(1)} %collective-permute-done.29.u1, ...), custom_call_target="tpu_custom_call" | custom-call | tf_op jit(solution)/shard_map/src_back/pallas_call | solution.py:240
  158.4 4.3 %collective-permute-done.32 = f32[4,64,2048]{2,1,0:T(8,128)S(1)} collective-permute-done((f32[4,64,2048]{2,1,0:T(8,128)}, f32[4,64,2048]{2,1,0:T(8,128)S(1)}, u32[]{:S(2)}, u32[]{:S(2)}) %collective-permute-start.32) | collective-permute-done | bytes 2097184 | tf_op jit(solution)/shard_map/src_back/ppermute | solution.py:249
  162.9 1.0 slice_bitcast_fusion.16
  163.9 3.2 %collective-permute-start.35 = (f32[32,2048]{1,0:T(8,128)}, f32[32,2048]{1,0:T(8,128)}, u32[]{:S(2)}, u32[]{:S(2)}) collective-permute-start(f32[32,2048]{1,0:T(8,128)} %get-tuple-element.559), channel_id=1, source_target_pairs={{0,24},{8,0},{16,8},{24,16},{1,25},{9,1},{17,9},{25,17},{2,26},{10... | collective-permute-start | bytes 786440 | tf_op jit(solution)/shard_map/src_back/ppermute | solution.py:249
  168.4 5.3 %collective-permute-done.33 = f32[32,2048]{1,0:T(8,128)S(1)} collective-permute-done((f32[32,2048]{1,0:T(8,128)}, f32[32,2048]{1,0:T(8,128)S(1)}, u32[]{:S(2)}, u32[]{:S(2)}) %collective-permute-start.33) | collective-permute-done | bytes 262176 | tf_op jit(solution)/shard_map/src_back/ppermute | solution.py:249
  173.7 1.0 fusion.14
  175.6 3.3 %collective-permute-start.36 = (f32[64,2048]{1,0:T(8,128)S(1)}, f32[64,2048]{1,0:T(8,128)}, u32[]{:S(2)}, u32[]{:S(2)}) collective-permute-start(f32[64,2048]{1,0:T(8,128)S(1)} %pad_maximum_fusion.4), channel_id=1, source_target_pairs={{0,24},{8,0},{16,8},{24,16},{1,25},{9,1},{17,9},{25,17},{2,26},{10... | collective-permute-start | bytes 1572872 | tf_op jit(solution)/shard_map/src_back/ppermute | solution.py:249
  178.9 5.1 %all-to-all-start.3 = ((f32[64,8,128]{2,1,0:T(8,128)}), f32[64,8,128]{2,1,0:T(8,128)S(1)}, u32[]{:S(2)}, u32[]{:S(2)}) async-start(f32[64,8,128]{2,1,0:T(8,128)} %get-tuple-element.467), calls=%async_computation.5 | async-start | bytes 524288 | tf_op jit(solution)/shard_map/hours/all_to_all | solution.py:322
  187.0 9.2 %all-to-all-done.3.back = f32[64,8,128]{2,1,0:T(8,128)S(1)} async-done(((f32[64,8,128]{2,1,0:T(8,128)}), f32[64,8,128]{2,1,0:T(8,128)S(1)}, u32[]{:S(2)}, u32[]{:S(2)}) %all-to-all-start.3) | async-done | bytes 262176 | tf_op jit(solution)/shard_map/hours/all_to_all | solution.py:322
  196.2 1.6 hours.8
  197.9 2.4 %fusion.12 = f32[64,2048]{1,0:T(8,128)} fusion(f32[64,2048]{1,0:T(8,128)} %collective-permute-done.36, f32[64,2048]{1,0:T(8,128)} %collective-permute-done.34, f32[4,64,2048]{2,1,0:T(8,128)} %copy-done.19), kind=kLoop, calls=%fused_computation.38 | loop fusion | flops 262144 | bytes 2097152 | tf_op jit(solution)/shard_map/src_back/add | solution.py:320
  200.2 1.1 slice_bitcast_fusion.18
  202.1 1.5 collective-permute-start.38
  205.2 1.6 fusion.15
  206.7 0.9 collective-permute-done.37
  208.3 1.6 collective-permute-done.38
  210.6 1.5 collective-permute-done.39
  (104 shorter events, 17.7 us)
Async XLA Ops:
  7.2 12.8 %copy-start.11 = (f32[64,2048]{1,0:T(8,128)S(1)}, f32[64,2048]{1,0:T(8,128)}, u32[]{:S(2)}) copy-start(f32[64,2048]{1,0:T(8,128)} %a00.1) | copy-start | bytes 1572868
  7.2 16.9 %copy-start.29 = (s32[30]{0:T(128)S(1)}, s32[30]{0:T(128)}, u32[]{:S(2)}) copy-start(s32[30]{0:T(128)} %src_ids.1) | copy-start | bytes 364
  7.2 16.8 %copy-start.32 = (s32[30]{0:T(128)S(1)}, s32[30]{0:T(128)}, u32[]{:S(2)}) copy-start(s32[30]{0:T(128)} %dst_ids.1) | copy-start | bytes 364
  7.2 16.8 %copy-start.25 = (s32[30]{0:T(128)S(1)}, s32[30]{0:T(128)}, u32[]{:S(2)}) copy-start(s32[30]{0:T(128)} %hours.9) | copy-start | bytes 364
  7.2 16.8 %copy-start.20 = (s32[30,8,128]{2,1,0:T(8,128)S(1)}, s32[30,8,128]{2,1,0:T(8,128)}, u32[]{:S(2)}) copy-start(s32[30,8,128]{2,1,0:T(8,128)} %bits.1) | copy-start | bytes 368644
  7.2 98.1 %all-gather.3.cloned.1.call-start = ((), (), s32[]{:S(2)}) async-start(), calls=%async_computation.7 | async-start | bytes 4718592 | tf_op jit(solution)/shard_map/gather_dst/all_gather | solution.py:265
  8.5 6.6 %collective-permute-start.26 = (f32[64,512]{1,0:T(8,128)S(1)}, f32[64,512]{1,0:T(8,128)S(1)}, u32[]{:S(2)}, u32[]{:S(2)}) collective-permute-start(f32[64,512]{1,0:T(8,128)S(1)} %get-tuple-element.566), channel_id=1, source_target_pairs={{0,1},{1,2},{2,3},{3,0},{4,5},{5,6},{6,7},{7,4},{8,9},{9,10},{10,1... | collective-permute-start | bytes 393224 | tf_op jit(solution)/shard_map/gather_dst/ppermute | solution.py:249
  10.2 8.9 %collective-permute-start.27 = (f32[64,512]{1,0:T(8,128)S(1)}, f32[64,512]{1,0:T(8,128)S(1)}, u32[]{:S(2)}, u32[]{:S(2)}) collective-permute-start(f32[64,512]{1,0:T(8,128)S(1)} %get-tuple-element.568), channel_id=1, source_target_pairs={{0,2},{1,3},{2,0},{3,1},{4,6},{5,7},{6,4},{7,5},{8,10},{9,11},{10,... | collective-permute-start | bytes 393224 | tf_op jit(solution)/shard_map/gather_dst/ppermute | solution.py:249
  13.1 6.0 %collective-permute-start.28 = (f32[64,512]{1,0:T(8,128)S(1)}, f32[64,512]{1,0:T(8,128)S(1)}, u32[]{:S(2)}, u32[]{:S(2)}) collective-permute-start(f32[64,512]{1,0:T(8,128)S(1)} %get-tuple-element.567), channel_id=1, source_target_pairs={{0,3},{1,0},{2,1},{3,2},{4,7},{5,4},{6,5},{7,6},{8,11},{9,8},{10,9... | collective-permute-start | bytes 393224 | tf_op jit(solution)/shard_map/gather_dst/ppermute | solution.py:249
  20.0 17.8 %collective-permute-start.15 = (f32[64,2048]{1,0:T(8,128)S(1)}, f32[64,2048]{1,0:T(8,128)S(1)}, u32[]{:S(2)}, u32[]{:S(2)}) collective-permute-start(f32[64,2048]{1,0:T(8,128)S(1)} %copy-done.11), channel_id=1, source_target_pairs={{0,8},{8,16},{16,24},{24,0},{1,9},{9,17},{17,25},{25,1},{2,10},{10... | collective-permute-start | bytes 1572872 | tf_op jit(solution)/shard_map/gather_src/ppermute | solution.py:249
  21.5 17.8 %collective-permute-start.14 = (f32[64,2048]{1,0:T(8,128)S(1)}, f32[64,2048]{1,0:T(8,128)S(1)}, u32[]{:S(2)}, u32[]{:S(2)}) collective-permute-start(f32[64,2048]{1,0:T(8,128)S(1)} %copy-done.11), channel_id=1, source_target_pairs={{0,24},{8,0},{16,8},{24,16},{1,25},{9,1},{17,9},{25,17},{2,26},{10... | collective-permute-start | bytes 1572872 | tf_op jit(solution)/shard_map/gather_src/ppermute | solution.py:249
  27.0 33.3 %all-to-all-start.2 = ((f32[64,16,128]{2,1,0:T(8,128)}), f32[64,16,128]{2,1,0:T(8,128)S(1)}, u32[]{:S(2)}, u32[]{:S(2)}) async-start(f32[64,16,128]{2,1,0:T(8,128)} %get-tuple-element.454), calls=%async_computation.3 | async-start | bytes 1048576 | tf_op jit(solution)/shard_map/slots/all_to_all | solution.py:283
  37.5 162.7 %reduce-scatter.3.cloned.1.call-start = ((), (), s32[]{:S(2)}) async-start(), calls=%async_computation.6 | async-start | bytes 4718592 | tf_op jit(solution)/shard_map/dst_back/reduce_scatter | solution.py:304
  37.6 32.6 %collective-permute-start.18 = (f32[64,2048]{1,0:T(8,128)S(1)}, f32[64,2048]{1,0:T(8,128)}, u32[]{:S(2)}, u32[]{:S(2)}) collective-permute-start(f32[64,2048]{1,0:T(8,128)S(1)} %copy-done.11), channel_id=1, source_target_pairs={{0,4},{4,0},{1,5},{5,1},{2,6},{6,2},{3,7},{7,3},{8,12},{12,8},{9,1... | collective-permute-start | bytes 1572872 | tf_op jit(solution)/shard_map/gather_src/ppermute | solution.py:249
  37.8 37.7 %copy-start.7 = (f32[64,2048]{1,0:T(8,128)}, f32[64,2048]{1,0:T(8,128)S(1)}, u32[]{:S(2)}) copy-start(f32[64,2048]{1,0:T(8,128)S(1)} %collective-permute-done.15.a30) | copy-start | bytes 1572868
  37.8 12.0 %collective-permute-start.16 = (f32[32,2048]{1,0:T(8,128)S(1)}, f32[32,2048]{1,0:T(8,128)S(1)}, u32[]{:S(2)}, u32[]{:S(2)}) collective-permute-start(f32[32,2048]{1,0:T(8,128)S(1)} %slice.187), channel_id=1, source_target_pairs={{0,8},{8,16},{16,24},{24,0},{1,9},{9,17},{17,25},{25,1},{2,10},{10... | collective-permute-start | bytes 786440 | tf_op jit(solution)/shard_map/gather_src/ppermute | solution.py:249
  39.4 36.1 %copy-start.9 = (f32[64,2048]{1,0:T(8,128)}, f32[64,2048]{1,0:T(8,128)S(1)}, u32[]{:S(2)}) copy-start(f32[64,2048]{1,0:T(8,128)S(1)} %collective-permute-done.14.a10) | copy-start | bytes 1572868
  39.4 11.0 %collective-permute-start.17 = (f32[32,2048]{1,0:T(8,128)S(1)}, f32[32,2048]{1,0:T(8,128)}, u32[]{:S(2)}, u32[]{:S(2)}) collective-permute-start(f32[32,2048]{1,0:T(8,128)S(1)} %slice.188), channel_id=1, source_target_pairs={{0,24},{8,0},{16,8},{24,16},{1,25},{9,1},{17,9},{25,17},{2,26},{10... | collective-permute-start | bytes 786440 | tf_op jit(solution)/shard_map/gather_src/ppermute | solution.py:249
  41.3 28.9 %collective-permute-start.19 = (f32[64,2048]{1,0:T(8,128)S(1)}, f32[64,2048]{1,0:T(8,128)S(1)}, u32[]{:S(2)}, u32[]{:S(2)}) collective-permute-start(f32[64,2048]{1,0:T(8,128)S(1)} %collective-permute-done.14.a10), channel_id=1, source_target_pairs={{0,4},{4,0},{1,5},{5,1},{2,6},{6,2},{3,7},{7,3},{8,12},{12,8},{9,1... | collective-permute-start | bytes 1572872 | tf_op jit(solution)/shard_map/gather_src/ppermute | solution.py:249
  41.3 28.9 %collective-permute-start.20 = (f32[64,2048]{1,0:T(8,128)S(1)}, f32[64,2048]{1,0:T(8,128)S(1)}, u32[]{:S(2)}, u32[]{:S(2)}) collective-permute-start(f32[64,2048]{1,0:T(8,128)S(1)} %collective-permute-done.15.a30), channel_id=1, source_target_pairs={{0,4},{4,0},{1,5},{5,1},{2,6},{6,2},{3,7},{7,3},{8,12},{12,8},{9,1... | collective-permute-start | bytes 1572872 | tf_op jit(solution)/shard_map/gather_src/ppermute | solution.py:249
  49.8 25.6 %copy-start.18 = (f32[32,2048]{1,0:T(8,128)}, f32[32,2048]{1,0:T(8,128)S(1)}, u32[]{:S(2)}) copy-start(f32[32,2048]{1,0:T(8,128)S(1)} %collective-permute-done.16.a2t0) | copy-start | bytes 786436
  49.8 20.3 %collective-permute-start.21 = (f32[32,2048]{1,0:T(8,128)S(1)}, f32[32,2048]{1,0:T(8,128)}, u32[]{:S(2)}, u32[]{:S(2)}) collective-permute-start(f32[32,2048]{1,0:T(8,128)S(1)} %collective-permute-done.16.a2t0), channel_id=1, source_target_pairs={{0,4},{4,0},{1,5},{5,1},{2,6},{6,2},{3,7},{7,3},{8,12},{12,8},{9,1... | collective-permute-start | bytes 786440 | tf_op jit(solution)/shard_map/gather_src/ppermute | solution.py:249
  50.4 19.8 %collective-permute-start.22 = (f32[32,2048]{1,0:T(8,128)}, f32[32,2048]{1,0:T(8,128)}, u32[]{:S(2)}, u32[]{:S(2)}) collective-permute-start(f32[32,2048]{1,0:T(8,128)} %collective-permute-done.17.a2b0), channel_id=1, source_target_pairs={{0,4},{4,0},{1,5},{5,1},{2,6},{6,2},{3,7},{7,3},{8,12},{12,8},{9,1... | collective-permute-start | bytes 786440 | tf_op jit(solution)/shard_map/gather_src/ppermute | solution.py:249
  75.5 17.1 %collective-permute-start.23 = (f32[16,72,128]{2,1,0:T(8,128)S(1)}, f32[16,72,128]{2,1,0:T(8,128)S(1)}, u32[]{:S(2)}, u32[]{:S(2)}) collective-permute-start(f32[16,72,128]{2,1,0:T(8,128)S(1)} %get-tuple-element.456), channel_id=1, source_target_pairs={{0,1},{1,2},{2,3},{3,0},{4,5},{5,6},{6,7},{7,4},{8,9},{9,10},{10,1... | collective-permute-start | bytes 1769480 | tf_op jit(solution)/shard_map/src_exchange/ppermute | solution.py:249
  76.8 28.3 %collective-permute-start.24 = (f32[16,72,128]{2,1,0:T(8,128)S(1)}, f32[16,72,128]{2,1,0:T(8,128)S(1)}, u32[]{:S(2)}, u32[]{:S(2)}) collective-permute-start(f32[16,72,128]{2,1,0:T(8,128)S(1)} %get-tuple-element.457), channel_id=1, source_target_pairs={{0,2},{1,3},{2,0},{3,1},{4,6},{5,7},{6,4},{7,5},{8,10},{9,11},{10,... | collective-permute-start | bytes 1769480 | tf_op jit(solution)/shard_map/src_exchange/ppermute | solution.py:249
  79.2 26.1 %collective-permute-start.25 = (f32[16,72,128]{2,1,0:T(8,128)S(1)}, f32[16,72,128]{2,1,0:T(8,128)S(1)}, u32[]{:S(2)}, u32[]{:S(2)}) collective-permute-start(f32[16,72,128]{2,1,0:T(8,128)S(1)} %get-tuple-element.458), channel_id=1, source_target_pairs={{0,3},{1,0},{2,1},{3,2},{4,7},{5,4},{6,5},{7,6},{8,11},{9,8},{10,9... | collective-permute-start | bytes 1769480 | tf_op jit(solution)/shard_map/src_exchange/ppermute | solution.py:249
  120.1 16.1 %collective-permute-start.29 = (f32[16,72,128]{2,1,0:T(8,128)S(1)}, f32[16,72,128]{2,1,0:T(8,128)S(1)}, u32[]{:S(2)}, u32[]{:S(2)}) collective-permute-start(f32[16,72,128]{2,1,0:T(8,128)S(1)} %copy-done.5), channel_id=1, source_target_pairs={{0,3},{1,0},{2,1},{3,2},{4,7},{5,4},{6,5},{7,6},{8,11},{9,8},{10,9... | collective-permute-start | bytes 1769480 | tf_op jit(solution)/shard_map/src_back/ppermute | solution.py:249
  124.9 17.7 %collective-permute-start.30 = (f32[16,72,128]{2,1,0:T(8,128)S(1)}, f32[16,72,128]{2,1,0:T(8,128)S(1)}, u32[]{:S(2)}, u32[]{:S(2)}) collective-permute-start(f32[16,72,128]{2,1,0:T(8,128)S(1)} %copy-done.3), channel_id=1, source_target_pairs={{0,2},{1,3},{2,0},{3,1},{4,6},{5,7},{6,4},{7,5},{8,10},{9,11},{10,... | collective-permute-start | bytes 1769480 | tf_op jit(solution)/shard_map/src_back/ppermute | solution.py:249
  126.1 28.8 %collective-permute-start.31 = (f32[16,72,128]{2,1,0:T(8,128)S(1)}, f32[16,72,128]{2,1,0:T(8,128)S(1)}, u32[]{:S(2)}, u32[]{:S(2)}) collective-permute-start(f32[16,72,128]{2,1,0:T(8,128)S(1)} %copy-done.1), channel_id=1, source_target_pairs={{0,1},{1,2},{2,3},{3,0},{4,5},{5,6},{6,7},{7,4},{8,9},{9,10},{10,1... | collective-permute-start | bytes 1769480 | tf_op jit(solution)/shard_map/src_back/ppermute | solution.py:249
  158.3 4.4 %collective-permute-start.32 = (f32[4,64,2048]{2,1,0:T(8,128)}, f32[4,64,2048]{2,1,0:T(8,128)S(1)}, u32[]{:S(2)}, u32[]{:S(2)}) collective-permute-start(f32[4,64,2048]{2,1,0:T(8,128)} %get-tuple-element.464), channel_id=1, source_target_pairs={{0,4},{4,0},{1,5},{5,1},{2,6},{6,2},{3,7},{7,3},{8,12},{12,8},{9,1... | collective-permute-start | bytes 6291464 | tf_op jit(solution)/shard_map/src_back/ppermute | solution.py:249
  162.9 12.6 %copy-start.19 = (f32[4,64,2048]{2,1,0:T(8,128)}, f32[4,64,2048]{2,1,0:T(8,128)S(1)}, u32[]{:S(2)}) copy-start(f32[4,64,2048]{2,1,0:T(8,128)S(1)} %add.208) | copy-start | bytes 6291460
  163.9 9.8 %collective-permute-start.33 = (f32[32,2048]{1,0:T(8,128)}, f32[32,2048]{1,0:T(8,128)S(1)}, u32[]{:S(2)}, u32[]{:S(2)}) collective-permute-start(f32[32,2048]{1,0:T(8,128)} %get-tuple-element.558), channel_id=1, source_target_pairs={{0,8},{8,16},{16,24},{24,0},{1,9},{9,17},{17,25},{25,1},{2,10},{10... | collective-permute-start | bytes 786440 | tf_op jit(solution)/shard_map/src_back/ppermute | solution.py:249
  163.9 9.8 %collective-permute-start.35 = (f32[32,2048]{1,0:T(8,128)}, f32[32,2048]{1,0:T(8,128)}, u32[]{:S(2)}, u32[]{:S(2)}) collective-permute-start(f32[32,2048]{1,0:T(8,128)} %get-tuple-element.559), channel_id=1, source_target_pairs={{0,24},{8,0},{16,8},{24,16},{1,25},{9,1},{17,9},{25,17},{2,26},{10... | collective-permute-start | bytes 786440 | tf_op jit(solution)/shard_map/src_back/ppermute | solution.py:249
  168.4 27.8 %copy-start.26 = (s32[30]{0:T(128)S(1)}, s32[30]{0:T(128)}, u32[]{:S(2)}) copy-start(s32[30]{0:T(128)} %hours.9) | copy-start | bytes 364
  175.5 22.3 %collective-permute-start.34 = (f32[64,2048]{1,0:T(8,128)}, f32[64,2048]{1,0:T(8,128)}, u32[]{:S(2)}, u32[]{:S(2)}) collective-permute-start(f32[64,2048]{1,0:T(8,128)} %pad_maximum_fusion.3), channel_id=1, source_target_pairs={{0,8},{8,16},{16,24},{24,0},{1,9},{9,17},{17,25},{25,1},{2,10},{10... | collective-permute-start | bytes 1572872 | tf_op jit(solution)/shard_map/src_back/ppermute | solution.py:249
  175.6 22.3 %collective-permute-start.36 = (f32[64,2048]{1,0:T(8,128)S(1)}, f32[64,2048]{1,0:T(8,128)}, u32[]{:S(2)}, u32[]{:S(2)}) collective-permute-start(f32[64,2048]{1,0:T(8,128)S(1)} %pad_maximum_fusion.4), channel_id=1, source_target_pairs={{0,24},{8,0},{16,8},{24,16},{1,25},{9,1},{17,9},{25,17},{2,26},{10... | collective-permute-start | bytes 1572872 | tf_op jit(solution)/shard_map/src_back/ppermute | solution.py:249
  178.9 17.3 %all-to-all-start.3 = ((f32[64,8,128]{2,1,0:T(8,128)}), f32[64,8,128]{2,1,0:T(8,128)S(1)}, u32[]{:S(2)}, u32[]{:S(2)}) async-start(f32[64,8,128]{2,1,0:T(8,128)} %get-tuple-element.467), calls=%async_computation.5 | async-start | bytes 524288 | tf_op jit(solution)/shard_map/hours/all_to_all | solution.py:322
  197.8 15.0 %copy-start.8 = (f32[64,2048]{1,0:T(8,128)S(1)}, f32[64,2048]{1,0:T(8,128)}, u32[]{:S(2)}) copy-start(f32[64,2048]{1,0:T(8,128)} %copy-done.7) | copy-start | bytes 1572868
  197.8 15.0 %copy-start.10 = (f32[64,2048]{1,0:T(8,128)S(1)}, f32[64,2048]{1,0:T(8,128)}, u32[]{:S(2)}) copy-start(f32[64,2048]{1,0:T(8,128)} %copy-done.9) | copy-start | bytes 1572868
  197.8 15.0 %copy-start.12 = (f32[64,2048]{1,0:T(8,128)S(1)}, f32[64,2048]{1,0:T(8,128)}, u32[]{:S(2)}) copy-start(f32[64,2048]{1,0:T(8,128)} %a00.1) | copy-start | bytes 1572868
  197.8 15.0 %copy-start.15 = (f32[64,2048]{1,0:T(8,128)S(1)}, f32[64,2048]{1,0:T(8,128)}, u32[]{:S(2)}) copy-start(f32[64,2048]{1,0:T(8,128)} %copy-done.14) | copy-start | bytes 1572868
  197.8 15.0 %copy-start.21 = (s32[30,8,128]{2,1,0:T(8,128)S(1)}, s32[30,8,128]{2,1,0:T(8,128)}, u32[]{:S(2)}) copy-start(s32[30,8,128]{2,1,0:T(8,128)} %bits.1) | copy-start | bytes 368644
  197.8 15.0 %copy-start.27 = (s32[30]{0:T(128)S(1)}, s32[30]{0:T(128)}, u32[]{:S(2)}) copy-start(s32[30]{0:T(128)} %hours.9) | copy-start | bytes 364
  197.8 14.9 %copy-start.30 = (s32[30]{0:T(128)S(1)}, s32[30]{0:T(128)}, u32[]{:S(2)}) copy-start(s32[30]{0:T(128)} %src_ids.1) | copy-start | bytes 364
  197.8 14.9 %copy-start.33 = (s32[30]{0:T(128)S(1)}, s32[30]{0:T(128)}, u32[]{:S(2)}) copy-start(s32[30]{0:T(128)} %dst_ids.1) | copy-start | bytes 364
  201.3 6.4 %collective-permute-start.37 = (f32[64,512]{1,0:T(8,128)S(1)}, f32[64,512]{1,0:T(8,128)S(1)}, u32[]{:S(2)}, u32[]{:S(2)}) collective-permute-start(f32[64,512]{1,0:T(8,128)S(1)} %get-tuple-element.564), channel_id=1, source_target_pairs={{0,3},{1,0},{2,1},{3,2},{4,7},{5,4},{6,5},{7,6},{8,11},{9,8},{10,9... | collective-permute-start | bytes 393224 | tf_op jit(solution)/shard_map/dst_back/ppermute | solution.py:249
  202.1 7.8 %collective-permute-start.38 = (f32[64,512]{1,0:T(8,128)S(1)}, f32[64,512]{1,0:T(8,128)S(1)}, u32[]{:S(2)}, u32[]{:S(2)}) collective-permute-start(f32[64,512]{1,0:T(8,128)S(1)} %get-tuple-element.563), channel_id=1, source_target_pairs={{0,2},{1,3},{2,0},{3,1},{4,6},{5,7},{6,4},{7,5},{8,10},{9,11},{10,... | collective-permute-start | bytes 393224 | tf_op jit(solution)/shard_map/dst_back/ppermute | solution.py:249
  203.5 8.5 %collective-permute-start.39 = (f32[64,512]{1,0:T(8,128)S(1)}, f32[64,512]{1,0:T(8,128)S(1)}, u32[]{:S(2)}, u32[]{:S(2)}) collective-permute-start(f32[64,512]{1,0:T(8,128)S(1)} %get-tuple-element.562), channel_id=1, source_target_pairs={{0,1},{1,2},{2,3},{3,0},{4,5},{5,6},{6,7},{7,4},{8,9},{9,10},{10,1... | collective-permute-start | bytes 393224 | tf_op jit(solution)/shard_map/dst_back/ppermute | solution.py:249
  (8 other events, 18.3 us)
Sparse Core Ops, SparseCore 0:
  20.1 66.2 all-gather.2
  119.2 54.5 reduce-scatter.2

commit v2 on v1

v2 whole, which is shorter than its diff:
```python
import jax
import jax.numpy as jnp
from jax import lax
from jax.experimental import pallas as pl
from jax.experimental.pallas import tpu as pltpu
from jax.sharding import Mesh, PartitionSpec as P

NZ, NX, NC, NO = 8, 4, 2, 4
SLAB = ("z", "x", "c")
GROUPS = 64
TILE_CAP = 30
SIDE = 128
RK = 64
RANK = RK * NO
STORED = 16
PART = STORED // NO * SIDE
SLOTS = 5
ROWS = 3 * SLOTS + 1
PER = 16
LIST = NO * PER
XROWS = RK + 8
VMEM = pl.BlockSpec(memory_space=pltpu.VMEM)
SMEM = pl.BlockSpec(memory_space=pltpu.SMEM)
ANY = pl.BlockSpec(memory_space=pl.ANY)
f32, bf16, i32 = jnp.float32, jnp.bfloat16, jnp.int32
PARAMS = pltpu.CompilerParams(vmem_limit_bytes=24 * 1024 * 1024)


def lane_block(within):
    return pl.ds(pl.multiple_of(within * SIDE, SIDE), SIDE)


def split(x):
    hi = x.astype(bf16)
    return hi, (x - hi.astype(f32)).astype(bf16)


def dot3(a, b, dims):
    dg = lambda p, q: lax.dot_general(p, q, (dims, ((), ())), preferred_element_type=f32)
    return dg(a[0], b[0]) + (dg(a[0], b[1]) + dg(a[1], b[0]))


def as_column(row):
    return jnp.broadcast_to(row, (SIDE, RK)).T


def send_kernel(scal, src_ids, dst_ids, hours, src_place, dst_place, bits, hour_rows, out, where, count):
    own, first_hour, live, pair_round = scal[0], scal[1], scal[2], scal[3]

    @pl.loop(0, GROUPS)
    def _(g):
        count[g] = 0

    out[...] = jnp.zeros_like(out)
    lane = lax.broadcasted_iota(i32, (1, SIDE), 1)

    def step(t, told):
        src_at = src_place[src_ids[t]]
        dst_at = dst_place[dst_ids[t]]
        to = jnp.right_shift(src_at, 7) * 8 + jnp.bitwise_and(jnp.right_shift(dst_at, 4), 7)
        rank = count[to]
        slot = rank - pair_round * SLOTS
        here = (t < live) & (slot >= 0) & (slot < SLOTS)
        where[t] = jnp.where(here, to * 8 + slot, -1)

        @pl.when(t < live)
        def _():
            count[to] = rank + 1

        @pl.when(here)
        def _():
            for i in range(2):
                out[to, pl.ds(3 * slot + i, 1), :] = bits[t, pl.ds(2 * own + i, 1), :].astype(f32)
            out[to, pl.ds(3 * slot + 2, 1), :RK] = hour_rows[pl.ds(hours[t] - first_hour, 1), :]
            row = out[to, ROWS - 1 : ROWS, :]
            row = jnp.where(lane == slot, src_at.astype(f32), row)
            row = jnp.where(lane == 8 + slot, dst_at.astype(f32), row)
            out[to, ROWS - 1 : ROWS, :] = jnp.where(lane == 16, (slot + 1).astype(f32), row)

        alive = t < live
        told = jnp.where(lane == t + 32, jnp.where(alive, src_at, -1).astype(f32), told)
        told = jnp.where(lane == t + 64, dst_at.astype(f32), told)
        return jnp.where(lane == t + 96, rank.astype(f32), told)

    told = lax.fori_loop(0, TILE_CAP, step, jnp.zeros((1, SIDE), f32))
    out[:, ROWS - 1 : ROWS, :] += jnp.broadcast_to(told[None], (GROUPS, 1, SIDE))


def list_kernel(scal, got, lst, seen, staged, meta, sem):
    base = scal[3]
    for o in range(NO):
        seen[o] = 0
    staged[...] = got[:, ROWS - 1, :].astype(i32)
    copy = pltpu.make_async_copy(staged, meta, sem)
    copy.start()
    copy.wait()

    @pl.loop(0, GROUPS)
    def _(g):
        n = meta[g, 16]
        for s in range(SLOTS):

            @pl.when(s < n)
            def _():
                dst_at = meta[g, 8 + s]
                to = jnp.bitwise_and(jnp.right_shift(dst_at, 2), NO - 1)
                pos = seen[to] - base
                seen[to] += 1

                @pl.when((pos >= 0) & (pos < PER))
                def _():
                    at = to * PER + pos
                    lst[at] = meta[g, s]
                    lst[LIST + at] = dst_at
                    lst[2 * LIST + at] = g * 8 + s

    for o in range(NO):
        lst[3 * LIST + o] = jnp.clip(seen[o] - base, 0, PER)


def each_tile(own, lst, d, work):
    to = jnp.bitwise_and(own + d, NO - 1)

    @pl.loop(0, lst[3 * LIST + to])
    def _(j):
        work(j, PER * to + j)


def slot_row(slot):
    return jnp.right_shift(slot, 3) * ROWS + 3 * jnp.bitwise_and(slot, 7)


def src_pack_kernel(scal, lst, recv, a00, a10, a30, a2t0, a2b0, a01, a11, a31, a2t1, a2b1, *outs):
    own, x_at, c_at = scal[0], scal[1], scal[2]
    sources = (
        ((a00,), (a01,)), ((a10,), (a11,)), ((a2t0, a2b0), (a2t1, a2b1)), ((a30,), (a31,)),
    )
    for d in range(NO):

        def work(j, k):
            src_at = lst[k]
            row = slot_row(lst[2 * LIST + k])
            cols = lane_block(jnp.bitwise_and(src_at, STORED - 1))
            dx = jnp.bitwise_and(jnp.right_shift(src_at, 5) - x_at, NX - 1)
            dc = jnp.bitwise_and(jnp.right_shift(src_at, 4) + c_at, NC - 1)
            for sx in range(NX):
                for sc in range(NC):

                    @pl.when((dx == sx) & (dc == sc))
                    def _():
                        refs = sources[sx][sc]
                        step = RK // len(refs)
                        for h, ref in enumerate(refs):
                            outs[d][j, h * step : (h + 1) * step, :] = ref[:, cols]

            for i in range(3):
                outs[d][j, RK + i : RK + i + 1, :] = recv[pl.ds(row + i, 1), :]

        each_tile(own, lst, d, work)


def prepare_kernel(scal, lst, a0, a1, a2, a3, high, low, column, entries):
    own = scal[0]
    a_in = (a0, a1, a2, a3)
    shift = jnp.bitwise_and(lax.broadcasted_iota(i32, (32, SIDE), 0), 15)

    def work(j, k):
        high[j], low[j] = split(jnp.concatenate([r[j, :RK] for r in a_in], axis=0))
        column[j] = jnp.concatenate([as_column(r[j, RK + 2 : RK + 3, :RK]) for r in a_in], axis=0)
        for d in range(NO):
            rows = pl.ds(pl.multiple_of(jnp.bitwise_and(own - d, NO - 1) * 32, 32), 32)
            words = jnp.concatenate(
                [jnp.broadcast_to(a_in[d][j, RK + i : RK + i + 1, :], (16, SIDE)) for i in range(2)], axis=0
            ).astype(i32)
            entries[j, rows, :] = jnp.bitwise_and(jnp.right_shift(words, shift), 1).astype(f32)

    each_tile(own, lst, 0, work)


def tile_kernel(scal, lst, high, low, column, entries, b_all, g_sum, u0, u1, u2, u3, h0, h1, h2, h3):
    ones = jnp.ones((8, SIDE), bf16)
    g_sum[...] = jnp.zeros_like(g_sum)

    def work(j, k):
        dst_at = lst[LIST + k]
        z = jnp.right_shift(dst_at, 7)
        cols = lane_block(jnp.bitwise_and(dst_at, STORED // NO - 1))
        b_raw = b_all[z, :, cols]
        c = column[j]
        a = high[j], low[j]
        b = split(b_raw * c)
        r = split(jax.nn.sigmoid(dot3(a, b, ((0,), (0,)))) - entries[j])
        u = dot3(b, r, ((1,), (1,)))
        g = dot3(a, r, ((1,), (0,)))
        g_sum[z, :, cols] += g * c
        along = lambda x: lax.dot_general(ones, x, (((1,), (1,)), ((), ())), preferred_element_type=f32)
        h_high, h_low = split(b_raw * g)
        h = along(h_high) + along(h_low)
        for d, (u_out, h_out) in enumerate(zip((u0, u1, u2, u3), (h0, h1, h2, h3))):
            u_out[j] = u[RK * d : RK * (d + 1)]
            h_out[pl.ds(j, 1), :RK] = h[:1, RK * d : RK * (d + 1)]

    each_tile(scal[0], lst, 0, work)


def hour_pack_kernel(scal, lst, h0, h1, h2, h3, hour):
    hour[...] = jnp.zeros_like(hour)
    for d, h in enumerate((h0, h1, h2, h3)):

        def work(j, k):
            slot = lst[2 * LIST + k]
            hour[jnp.right_shift(slot, 3), pl.ds(jnp.bitwise_and(slot, 7), 1), :RK] = h[pl.ds(j, 1), :RK]

        each_tile(scal[0], lst, d, work)


def src_sum_kernel(scal, lst, u0, u1, u2, u3, back, keep, give):
    own, x_at, c_at = scal[0], scal[1], scal[2]
    keep[...] = jnp.zeros_like(keep)
    give[...] = jnp.zeros_like(give)
    for d, u in enumerate((u0, u1, u2, u3)):

        def work(j, k):
            src_at = lst[k]
            cols = lane_block(jnp.bitwise_and(src_at, STORED - 1))
            dx = jnp.bitwise_and(jnp.right_shift(src_at, 5) - x_at, NX - 1)
            dc = jnp.bitwise_and(jnp.right_shift(src_at, 4) + c_at, NC - 1)
            for sc, total in enumerate((keep, give)):

                @pl.when(dc == sc)
                def _():
                    total[dx, :, cols] += u[j]

        each_tile(own, lst, d, work)


def stack_kernel(p0, p1, p2, p3, out):
    for d, p in enumerate((p0, p1, p2, p3)):
        out[RK * d : RK * (d + 1), :] = p[...]


def join_kernel(scal, p0, p1, p2, p3, out):
    for d, p in enumerate((p0, p1, p2, p3)):
        to = jnp.bitwise_and(scal[0] + d, NO - 1)
        out[:, pl.ds(pl.multiple_of(to * PART, PART), PART)] = p[...]


def hour_kernel(scal, hours, where, back, out):
    first_hour = scal[1]
    out[...] = jnp.zeros_like(out)

    @pl.loop(0, TILE_CAP)
    def _(t):
        at = where[t]

        @pl.when(at >= 0)
        def _():
            h = hours[t] - first_hour
            out[pl.ds(h, 1), :] += back[jnp.right_shift(at, 3), pl.ds(jnp.bitwise_and(at, 7), 1), :RK]


def shape(*dims, dtype=f32):
    return jax.ShapeDtypeStruct(dims, dtype)


def call(kernel, out_shape, in_specs, args, out_specs=None, scratch=()):
    if out_specs is None:
        out_specs = jax.tree.map(lambda _: VMEM, out_shape)
    return pl.pallas_call(
        kernel, out_shape=out_shape, in_specs=in_specs, out_specs=out_specs,
        scratch_shapes=scratch, compiler_params=PARAMS,
    )(*args)


def hop(value, axis, size, by):
    if by == 0:
        return value
    return lax.ppermute(value, axis, [(i, (i + by) % size) for i in range(size)])


def per_device(
    src_factor, dst_factor, hour_factor, tile_src, tile_dst, tile_hour, tile_count, src_place, dst_place, tile_bits
):
    z_at, x_at, c_at, own = (lax.axis_index(n).astype(i32) for n in ("z", "x", "c", "own"))
    first_hour = ((z_at * NX + x_at) * NC + c_at) * hour_factor.shape[0]
    live = tile_count[0]
    half = RK // 2

    def part_of(d):
        return jnp.bitwise_and(own + d, NO - 1) * PART

    def one_round(pair_round, base, src_factor, dst_factor):
        src_factor, dst_factor, pair_round = lax.optimization_barrier((src_factor, dst_factor, pair_round))
        with jax.named_scope("slots"):
            scal = jnp.stack([own, first_hour, live, pair_round])
            sent, where = call(
                send_kernel, (shape(GROUPS, ROWS, SIDE), shape(TILE_CAP, dtype=i32)),
                [SMEM] * 6 + [VMEM] * 2,
                (scal, tile_src, tile_dst, tile_hour, src_place, dst_place, tile_bits, hour_factor),
                out_specs=(VMEM, SMEM), scratch=[pltpu.SMEM((GROUPS,), i32)],
            )
        with jax.named_scope("gather_dst"):
            parts = [
                hop(lax.dynamic_slice(dst_factor, (0, part_of(d)), (RK, PART)), "own", NO, d) for d in range(NO)
            ]
            parts, sent = lax.optimization_barrier((parts, sent))
            b_mine = call(stack_kernel, shape(RANK, PART), [VMEM] * NO, parts)
            b_all = lax.all_gather(b_mine, "z", axis=0)
        with jax.named_scope("slots"):
            got = lax.all_to_all(sent, SLAB, 0, 0)
            rows = got.reshape(GROUPS * ROWS, SIDE)
            told = got[:, ROWS - 1].astype(i32)
        with jax.named_scope("gather_src"):
            stored, _ = lax.optimization_barrier((src_factor, b_mine))
            up = hop(stored, "x", NX, 1)
            down = hop(stored, "x", NX, -1)
            far_top = hop(up[:half], "x", NX, 1)
            far_bottom = hop(down[half:], "x", NX, -1)
            mine = (stored, down, up, far_top, far_bottom)
            a_all = mine + tuple(hop(v, "c", NC, 1) for v in mine)
        at = jnp.stack([own, x_at, c_at, base])
        with jax.named_scope("list"):
            lst = call(
                list_kernel, shape(3 * LIST + 8, dtype=i32), [SMEM, VMEM], (at, got), out_specs=SMEM,
                scratch=[
                    pltpu.SMEM((NO,), i32), pltpu.VMEM((GROUPS, SIDE), i32), pltpu.SMEM((GROUPS, SIDE), i32),
                    pltpu.SemaphoreType.DMA,
                ],
            )
        with jax.named_scope("src_exchange"):
            a_out = call(
                src_pack_kernel, (shape(PER, XROWS, SIDE),) * NO, [SMEM] * 2 + [VMEM] * 11, (at, lst, rows) + a_all
            )
            a_in = [hop(v, "own", NO, d) for d, v in enumerate(a_out)]
            ready = call(
                prepare_kernel,
                (shape(PER, RANK, SIDE, dtype=bf16),) * 2 + (shape(PER, RANK, SIDE), shape(PER, SIDE, SIDE)),
                [SMEM] * 2 + [VMEM] * NO, (at, lst, *a_in),
            )
        with jax.named_scope("tiles"):
            g_sum, *out = call(
                tile_kernel,
                (shape(NZ, RANK, PART),) + (shape(PER, RK, SIDE),) * NO + (shape(PER, SIDE),) * NO,
                [SMEM] * 2 + [VMEM] * 5, (at, lst, *ready, b_all),
            )
        with jax.named_scope("hours"):
            h = [hop(v, "own", NO, -d) for d, v in enumerate(out[NO:])]
            hour_terms = call(hour_pack_kernel, shape(GROUPS, 8, SIDE), [SMEM] * 2 + [VMEM] * NO, (at, lst, *h))
            back = lax.all_to_all(hour_terms, SLAB, 0, 0)
            grad_hour = call(
                hour_kernel, shape(*hour_factor.shape), [SMEM] * 3 + [VMEM], (scal, tile_hour, where, back)
            )
        with jax.named_scope("src_back"):
            u = [hop(v, "own", NO, -d) for d, v in enumerate(out[:NO])]
            keep, give = call(
                src_sum_kernel, (shape(NX, RK, STORED * SIDE),) * 2, [SMEM] * 2 + [VMEM] * NO + [ANY],
                (at, lst, *u, back),
            )
            s = keep + hop(give, "c", NC, 1)
            top = hop(s[2, :half], "x", NX, 1)
            bottom = hop(s[2, half:], "x", NX, -1)
            one = hop(jnp.concatenate([s[1, :half] + top, s[1, half:]]), "x", NX, 1)
            three = hop(jnp.concatenate([s[3, :half], s[3, half:] + bottom]), "x", NX, -1)
            grad_src = s[0] + one + three
        with jax.named_scope("dst_back"):
            g_part = lax.psum_scatter(g_sum, "z", scatter_dimension=0)
            pieces = [hop(g_part[RK * d : RK * (d + 1)], "own", NO, -d) for d in range(NO)]
            grad_dst = call(join_kernel, shape(*dst_factor.shape), [SMEM] + [VMEM] * NO, (at, *pieces))
        return (grad_src, grad_dst, grad_hour), told

    zero = jnp.zeros((), i32)
    grads, told = one_round(zero, zero, src_factor, dst_factor)

    src_at, dst_at, rank = (told[:, 32 * i : 32 * i + TILE_CAP].reshape(-1) for i in range(1, 4))
    worker = (src_at // 128) * 32 + (dst_at // STORED) % 8 * NO + dst_at % STORED // NO
    alive = src_at >= 0

    def busiest(pair_round):
        here = alive & (rank // SLOTS == pair_round)
        counts = jnp.sum((worker[None, :] == jnp.arange(GROUPS * NO, dtype=i32)[:, None]) & here[None, :], axis=1)
        return jnp.max(counts.astype(i32))

    def following(pair_round, base):
        more = base + PER < busiest(pair_round)
        return jnp.where(more, pair_round, pair_round + 1), jnp.where(more, base + PER, 0)

    def body(state):
        pair_round, base, sums = state
        terms, _ = one_round(pair_round, base, src_factor, dst_factor)
        return following(pair_round, base) + (jax.tree.map(jnp.add, sums, terms),)

    top_rank = jnp.max(jnp.where(alive, rank, -1))
    last = lax.while_loop(lambda state: top_rank >= state[0] * SLOTS, body, following(zero, zero) + (grads,))
    return last[2]


def solution(mesh):
    fine = Mesh(mesh.devices.reshape(NZ, NX, NC, NO), SLAB + ("own",))
    return jax.shard_map(
        per_device,
        mesh=fine,
        in_specs=(
            P("own", SLAB), P("own", SLAB), P(SLAB, "own"), P(SLAB), P(SLAB), P(SLAB), P(SLAB), P(), P(),
            P(SLAB, None, None),
        ),
        out_specs=(P("own", SLAB), P("own", SLAB), P(SLAB, "own")),
        check_vma=False,
    )
```

time: 223 us -> 203 us (0.910)
  waiting for transfers between devices: 98.1 us -> 63.1 us
  blocking collectives: 0 us -> 25.4 us
  starting transfers between devices: 51.3 us -> 42.8 us
    all_to_all x0 -> x1, blocking collectives: none -> 25.4 us  [one_round(): back = lax.all_to_all(hour_terms, SLAB, 0, 0)]
    ppermute x26 -> x29, waiting for transfers between devices: 79 us -> 54 us  [hop(): lax.ppermute(value, axis, [(i, (i + by) % size) for i in range(size)])]
    all_to_all x1 -> x0, waiting for transfers between devices: 9.17 us -> none  [one_round(): back = lax.all_to_all(hour_terms, SLAB, 0, 0)]
    unnamed x52 -> x40, local copies, waits for them, and re-layouts: 5.3 us -> 14 us
    all_to_all x1 -> x0, starting transfers between devices: 5.14 us -> none  [one_round(): back = lax.all_to_all(hour_terms, SLAB, 0, 0)]
    dynamic_update_slice x4 -> x0, local copies, waits for them, and re-layouts: 3.56 us -> none  [one_round(): grad_dst = lax.dynamic_update_slice(grad_dst, piece, (0, part_of(d)))]
    ppermute x26 -> x29, starting transfers between devices: 35.6 us -> 32.3 us  [hop(): lax.ppermute(value, axis, [(i, (i + by) % size) for i in range(size)])]
    pallas_call x6 -> x10, Pallas kernels: 28.1 us -> 27.8 us  [call(): pl.pallas_call(kernel, out_shape=out_shape, in_specs=in_specs, out_specs=...]
  transfers between devices with their start and end apart: 30 -> 32, of which waited for: 17 -> 13; matrix products, arithmetic and copies ran while one was open for 8% -> 5% of each run, Pallas kernels for 8% -> 9%
where the time goes in v2:
time: 203 us; the launch traced here: 201 us
  waiting for transfers between devices  63.1 us (31%)
  starting transfers between devices  42.8 us (21%)
  Pallas kernels  27.8 us (14%)
  blocking collectives  25.4 us (13%)
  local copies, waits for them, and re-layouts  18.4 us (9%)
  between operations  15.6 us (8%)
  other arithmetic  7.48 us (4%)
    ppermute x29, waiting for transfers between devices, hop(): lax.ppermute(value, axis, [(i, (i + by) % size) for i in range(size)])  54 us
    ppermute x29, starting transfers between devices, hop(): lax.ppermute(value, axis, [(i, (i + by) % size) for i in range(size)])  32.3 us
    pallas_call x10, Pallas kernels, call(): pl.pallas_call(kernel, out_shape=out_shape, in_specs=in_specs, out_specs=...  27.8 us
    all_to_all x1, blocking collectives, one_round(): back = lax.all_to_all(hour_terms, SLAB, 0, 0)  25.4 us
    unnamed x40, local copies, waits for them, and re-layouts  14 us
    all_to_all x1, starting transfers between devices, one_round(): got = lax.all_to_all(sent, SLAB, 0, 0)  10.4 us
    all_to_all x1, waiting for transfers between devices, one_round(): got = lax.all_to_all(sent, SLAB, 0, 0)  9.03 us
  transfers between devices with their start and end apart: 32, of which 13 were waited for; matrix products, arithmetic and copies ran while one was open for 5% of the time, Pallas kernels for 9%

profile of v2, /device:TPU:32, one launch (start us, length us, event | category | flops | bytes accessed | tf_op | source)
XLA Modules:
  0.0 201.4 jit_solution(2518397288943571887)
XLA Ops:
  7.2 1.1 constant_dynamic-slice_fusion.4
  8.4 3.1 %collective-permute-start.31 = (f32[64,512]{1,0:T(8,128)S(1)}, f32[64,512]{1,0:T(8,128)S(1)}, u32[]{:S(2)}, u32[]{:S(2)}) collective-permute-start(f32[64,512]{1,0:T(8,128)S(1)} %get-tuple-element.504), channel_id=1, source_target_pairs={{0,3},{1,0},{2,1},{3,2},{4,7},{5,4},{6,5},{7,6},{8,11},{9,8},{10,9... | collective-permute-start | bytes 393224 | tf_op jit(solution)/shard_map/gather_dst/ppermute | solution.py:278
  12.1 1.0 collective-permute-start.29
  13.8 3.1 %slots.5 = (f32[64,16,128]{2,1,0:T(8,128)}, s32[30]{0:T(128)S(1)}) custom-call(s32[4]{0:T(128)S(1)} %pad_add_fusion.2.scal, s32[30]{0:T(128)} %src_ids.1, s32[30]{0:T(128)} %dst_ids.1, s32[30]{0:T(128)} %hours.15, s32[1024]{0:T(1024)} %src_place.1, s32[1024]{0:T(1024)} %dst_place.1, s32[30,8,128]{2,1,0:T(8,128)} %bits.1, f32[8,64]{1,0:T(8,128)} %hour_rows.1), custom_call_target="tpu_custom_call" | custom-call | tf_op jit(solution)/shard_map/slots/pallas_call | solution.py:269
  17.0 2.3 %collective-permute-done.30.p2 = f32[64,512]{1,0:T(8,128)S(1)} collective-permute-done((f32[64,512]{1,0:T(8,128)S(1)}, f32[64,512]{1,0:T(8,128)S(1)}, u32[]{:S(2)}, u32[]{:S(2)}) %collective-permute-start.30) | collective-permute-done | bytes 131104 | tf_op jit(solution)/shard_map/gather_dst/ppermute | solution.py:278
  19.3 1.4 collective-permute-done.29.p1
  21.6 1.6 collective-permute-start.33
  23.2 1.7 collective-permute-start.32
  24.9 10.4 %all-to-all-start.2 = ((f32[64,16,128]{2,1,0:T(8,128)}), f32[64,16,128]{2,1,0:T(8,128)S(1)}, u32[]{:S(2)}, u32[]{:S(2)}) async-start(f32[64,16,128]{2,1,0:T(8,128)} %get-tuple-element.392), calls=%async_computation.3 | async-start | bytes 1048576 | tf_op jit(solution)/shard_map/slots/all_to_all | solution.py:310
  35.6 1.2 collective-permute-done.33.a30
  37.8 3.0 %collective-permute-start.35 = (f32[32,2048]{1,0:T(8,128)S(1)}, f32[32,2048]{1,0:T(8,128)}, u32[]{:S(2)}, u32[]{:S(2)}) collective-permute-start(f32[32,2048]{1,0:T(8,128)S(1)} %slice.192), channel_id=1, source_target_pairs={{0,24},{8,0},{16,8},{24,16},{1,25},{9,1},{17,9},{25,17},{2,26},{10... | collective-permute-start | bytes 786440 | tf_op jit(solution)/shard_map/gather_src/ppermute | solution.py:278
  40.8 6.8 %collective-permute-done.34.a2t0 = f32[32,2048]{1,0:T(8,128)S(1)} collective-permute-done((f32[32,2048]{1,0:T(8,128)S(1)}, f32[32,2048]{1,0:T(8,128)S(1)}, u32[]{:S(2)}, u32[]{:S(2)}) %collective-permute-start.34) | collective-permute-done | bytes 262176 | tf_op jit(solution)/shard_map/gather_src/ppermute | solution.py:278
  47.6 1.4 collective-permute-done.35.a2b0
  49.1 9.0 %all-to-all-done.2.got = f32[64,16,128]{2,1,0:T(8,128)S(1)} async-done(((f32[64,16,128]{2,1,0:T(8,128)}), f32[64,16,128]{2,1,0:T(8,128)S(1)}, u32[]{:S(2)}, u32[]{:S(2)}) %all-to-all-start.2) | async-done | bytes 524320 | tf_op jit(solution)/shard_map/slots/all_to_all | solution.py:310
  58.1 5.9 %list.2.lst = s32[200]{0:T(256)S(1)} custom-call(s32[4]{0:T(128)S(1)} %pad_add_fusion.3.scal, f32[64,16,128]{2,1,0:T(8,128)S(1)} %all-to-all-done.2.got), custom_call_target="tpu_custom_call" | custom-call | tf_op jit(solution)/shard_map/list/pallas_call | solution.py:269
  64.1 3.1 %src_exchange.10 = (f32[16,72,128]{2,1,0:T(8,128)S(1)}, f32[16,72,128]{2,1,0:T(8,128)S(1)}, f32[16,72,128]{2,1,0:T(8,128)S(1)}, f32[16,72,128]{2,1,0:T(8,128)S(1)}) custom-call(s32[4]{0:T(128)S(1)} %pad_add_fusion.3.scal, s32[200]{0:T(256)S(1)} %list.2.lst, f32[1024,128]{1,0:T(8,128)S(1)} %bitcast.104, f32[64,2048]{1,0:T(8,128)} %a00, ...), custom_call_target="tpu_custom_call" | custom-call | tf_op jit(solution)/shard_map/src_exchange/pallas_call | solution.py:269
  67.3 2.0 %collective-permute-start.42 = (f32[16,72,128]{2,1,0:T(8,128)S(1)}, f32[16,72,128]{2,1,0:T(8,128)S(1)}, u32[]{:S(2)}, u32[]{:S(2)}) collective-permute-start(f32[16,72,128]{2,1,0:T(8,128)S(1)} %get-tuple-element.401), channel_id=1, source_target_pairs={{0,2},{1,3},{2,0},{3,1},{4,6},{5,7},{6,4},{7,5},{8,10},{9,11},{10,... | collective-permute-start | bytes 1769480 | tf_op jit(solution)/shard_map/src_exchange/ppermute | solution.py:278
  69.3 1.3 collective-permute-start.43
  70.6 25.9 %collective-permute-done.41.a1 = f32[16,72,128]{2,1,0:T(8,128)S(1)} collective-permute-done((f32[16,72,128]{2,1,0:T(8,128)S(1)}, f32[16,72,128]{2,1,0:T(8,128)S(1)}, u32[]{:S(2)}, u32[]{:S(2)}) %collective-permute-start.41) | collective-permute-done | bytes 589856 | tf_op jit(solution)/shard_map/src_exchange/ppermute | solution.py:278
  97.2 1.9 src_exchange.11
  99.1 1.0 copy-done.10
  100.1 1.0 copy-done.12
  101.1 1.1 copy-done.14
  102.1 2.2 %copy-done.8 = f32[2048,512]{1,0:T(8,128)S(1)} copy-done((f32[2048,512]{1,0:T(8,128)S(1)}, f32[2048,512]{1,0:T(8,128)}, u32[]{:S(2)}) %copy-start.8) | copy-done | bytes 4194328
  104.3 1.2 copy-done.11
  105.6 1.2 copy-done.13
  106.8 1.2 copy-done.15
  108.0 7.4 %tiles.5 = (f32[8,256,512]{2,1,0:T(8,128)S(1)}, f32[16,64,128]{2,1,0:T(8,128)S(1)}, f32[16,64,128]{2,1,0:T(8,128)S(1)}, f32[16,64,128]{2,1,0:T(8,128)S(1)}, f32[...) custom-call(s32[4]{0:T(128)S(1)} %pad_add_fusion.3.scal, ...), custom_call_target="tpu_custom_call" | custom-call | tf_op jit(solution)/shard_map/tiles/pallas_call | solution.py:269
  115.4 2.0 %copy-done.9 = f32[8,256,512]{2,1,0:T(8,128)} copy-done((f32[8,256,512]{2,1,0:T(8,128)}, f32[8,256,512]{2,1,0:T(8,128)S(1)}, u32[]{:S(2)}) %copy-start.9) | copy-done | bytes 4194328
  119.9 1.6 collective-permute-start.47
  121.4 1.0 collective-permute-start.49
  122.4 2.3 %collective-permute-start.44 = (f32[16,64,128]{2,1,0:T(8,128)S(1)}, f32[16,64,128]{2,1,0:T(8,128)S(1)}, u32[]{:S(2)}, u32[]{:S(2)}) collective-permute-start(f32[16,64,128]{2,1,0:T(8,128)S(1)} %copy-done.25), channel_id=1, source_target_pairs={{0,3},{1,0},{2,1},{3,2},{4,7},{5,4},{6,5},{7,6},{8,11},{9,8},{10,9... | collective-permute-start | bytes 1572872 | tf_op jit(solution)/shard_map/src_back/ppermute | solution.py:278
  124.7 2.3 %collective-permute-start.45 = (f32[16,64,128]{2,1,0:T(8,128)S(1)}, f32[16,64,128]{2,1,0:T(8,128)S(1)}, u32[]{:S(2)}, u32[]{:S(2)}) collective-permute-start(f32[16,64,128]{2,1,0:T(8,128)S(1)} %copy-done.21), channel_id=1, source_target_pairs={{0,2},{1,3},{2,0},{3,1},{4,6},{5,7},{6,4},{7,5},{8,10},{9,11},{10,... | collective-permute-start | bytes 1572872 | tf_op jit(solution)/shard_map/src_back/ppermute | solution.py:278
  128.4 25.4 %all_to_all.22.back = f32[64,8,128]{2,1,0:T(8,128)S(1)} all-to-all(f32[64,8,128]{2,1,0:T(8,128)S(1)} %hours.13), channel_id=1, replica_groups=mesh['z'=8,'x'=4,'c'=2,'own'=4] {'z','x','c'}, dimensions={0} | all-to-all | bytes 524288 | tf_op jit(solution)/shard_map/hours/all_to_all | solution.py:349
  153.8 1.6 src_back.5
  155.7 4.0 %collective-permute-done.50 = f32[4,64,2048]{2,1,0:T(8,128)S(1)} collective-permute-done((f32[4,64,2048]{2,1,0:T(8,128)S(1)}, f32[4,64,2048]{2,1,0:T(8,128)S(1)}, u32[]{:S(2)}, u32[]{:S(2)}) %collective-permute-start.50) | collective-permute-done | bytes 2097184 | tf_op jit(solution)/shard_map/src_back/ppermute | solution.py:278
  160.9 1.1 collective-permute-start.51
  161.9 2.2 %collective-permute-start.53 = (f32[32,2048]{1,0:T(8,128)}, f32[32,2048]{1,0:T(8,128)}, u32[]{:S(2)}, u32[]{:S(2)}) collective-permute-start(f32[32,2048]{1,0:T(8,128)} %get-tuple-element.497), channel_id=1, source_target_pairs={{0,24},{8,0},{16,8},{24,16},{1,25},{9,1},{17,9},{25,17},{2,26},{10... | collective-permute-start | bytes 786440 | tf_op jit(solution)/shard_map/src_back/ppermute | solution.py:278
  165.3 5.3 %collective-permute-done.51 = f32[32,2048]{1,0:T(8,128)S(1)} collective-permute-done((f32[32,2048]{1,0:T(8,128)}, f32[32,2048]{1,0:T(8,128)S(1)}, u32[]{:S(2)}, u32[]{:S(2)}) %collective-permute-start.51) | collective-permute-done | bytes 262176 | tf_op jit(solution)/shard_map/src_back/ppermute | solution.py:278
  171.3 1.1 fusion.13
  173.3 2.4 %collective-permute-start.54 = (f32[64,2048]{1,0:T(8,128)}, f32[64,2048]{1,0:T(8,128)}, u32[]{:S(2)}, u32[]{:S(2)}) collective-permute-start(f32[64,2048]{1,0:T(8,128)} %pad_maximum_fusion.3), channel_id=1, source_target_pairs={{0,24},{8,0},{16,8},{24,16},{1,25},{9,1},{17,9},{25,17},{2,26},{10... | collective-permute-start | bytes 1572872 | tf_op jit(solution)/shard_map/src_back/ppermute | solution.py:278
  179.4 1.6 hours.14
  181.1 1.2 slice_bitcast_fusion.18
  183.1 2.4 %collective-permute-start.55 = (f32[64,512]{1,0:T(8,128)S(1)}, f32[64,512]{1,0:T(8,128)S(1)}, u32[]{:S(2)}, u32[]{:S(2)}) collective-permute-start(f32[64,512]{1,0:T(8,128)S(1)} %get-tuple-element.502), channel_id=1, source_target_pairs={{0,3},{1,0},{2,1},{3,2},{4,7},{5,4},{6,5},{7,6},{8,11},{9,8},{10,9... | collective-permute-start | bytes 393224 | tf_op jit(solution)/shard_map/dst_back/ppermute | solution.py:278
  185.6 1.1 collective-permute-done.54
  186.7 3.7 %collective-permute-done.52 = f32[64,2048]{1,0:T(8,128)S(1)} collective-permute-done((f32[64,2048]{1,0:T(8,128)}, f32[64,2048]{1,0:T(8,128)S(1)}, u32[]{:S(2)}, u32[]{:S(2)}) %collective-permute-start.52) | collective-permute-done | bytes 524320 | tf_op jit(solution)/shard_map/src_back/ppermute | solution.py:278
  190.4 1.9 fusion.11
  192.3 1.4 dst_back.5
  (92 shorter events, 16.6 us)
Async XLA Ops:
  7.2 95.0 %all-gather.7.cloned.1.call-start = ((), (), s32[]{:S(2)}) async-start(), calls=%async_computation.7 | async-start | bytes 4718592 | tf_op jit(solution)/shard_map/gather_dst/all_gather | solution.py:308
  8.4 8.7 %collective-permute-start.31 = (f32[64,512]{1,0:T(8,128)S(1)}, f32[64,512]{1,0:T(8,128)S(1)}, u32[]{:S(2)}, u32[]{:S(2)}) collective-permute-start(f32[64,512]{1,0:T(8,128)S(1)} %get-tuple-element.504), channel_id=1, source_target_pairs={{0,3},{1,0},{2,1},{3,2},{4,7},{5,4},{6,5},{7,6},{8,11},{9,8},{10,9... | collective-permute-start | bytes 393224 | tf_op jit(solution)/shard_map/gather_dst/ppermute | solution.py:278
  11.5 7.9 %collective-permute-start.30 = (f32[64,512]{1,0:T(8,128)S(1)}, f32[64,512]{1,0:T(8,128)S(1)}, u32[]{:S(2)}, u32[]{:S(2)}) collective-permute-start(f32[64,512]{1,0:T(8,128)S(1)} %get-tuple-element.505), channel_id=1, source_target_pairs={{0,2},{1,3},{2,0},{3,1},{4,6},{5,7},{6,4},{7,5},{8,10},{9,11},{10,... | collective-permute-start | bytes 393224 | tf_op jit(solution)/shard_map/gather_dst/ppermute | solution.py:278
  12.1 8.6 %collective-permute-start.29 = (f32[64,512]{1,0:T(8,128)S(1)}, f32[64,512]{1,0:T(8,128)S(1)}, u32[]{:S(2)}, u32[]{:S(2)}) collective-permute-start(f32[64,512]{1,0:T(8,128)S(1)} %get-tuple-element.506), channel_id=1, source_target_pairs={{0,1},{1,2},{2,3},{3,0},{4,5},{5,6},{6,7},{7,4},{8,9},{9,10},{10,1... | collective-permute-start | bytes 393224 | tf_op jit(solution)/shard_map/gather_dst/ppermute | solution.py:278
  21.6 15.2 %collective-permute-start.33 = (f32[64,2048]{1,0:T(8,128)}, f32[64,2048]{1,0:T(8,128)S(1)}, u32[]{:S(2)}, u32[]{:S(2)}) collective-permute-start(f32[64,2048]{1,0:T(8,128)} %a00), channel_id=1, source_target_pairs={{0,8},{8,16},{16,24},{24,0},{1,9},{9,17},{17,25},{25,1},{2,10},{10... | collective-permute-start | bytes 1572872 | tf_op jit(solution)/shard_map/gather_src/ppermute | solution.py:278
  23.2 14.1 %collective-permute-start.32 = (f32[64,2048]{1,0:T(8,128)}, f32[64,2048]{1,0:T(8,128)S(1)}, u32[]{:S(2)}, u32[]{:S(2)}) collective-permute-start(f32[64,2048]{1,0:T(8,128)} %a00), channel_id=1, source_target_pairs={{0,24},{8,0},{16,8},{24,16},{1,25},{9,1},{17,9},{25,17},{2,26},{10... | collective-permute-start | bytes 1572872 | tf_op jit(solution)/shard_map/gather_src/ppermute | solution.py:278
  24.9 33.2 %all-to-all-start.2 = ((f32[64,16,128]{2,1,0:T(8,128)}), f32[64,16,128]{2,1,0:T(8,128)S(1)}, u32[]{:S(2)}, u32[]{:S(2)}) async-start(f32[64,16,128]{2,1,0:T(8,128)} %get-tuple-element.392), calls=%async_computation.3 | async-start | bytes 1048576 | tf_op jit(solution)/shard_map/slots/all_to_all | solution.py:310
  35.3 145.8 %reduce-scatter.3.cloned.1.call-start = ((), (), s32[]{:S(2)}) async-start(), calls=%async_computation.6 | async-start | bytes 4718592 | tf_op jit(solution)/shard_map/dst_back/reduce_scatter | solution.py:366
  35.3 28.7 %collective-permute-start.36 = (f32[64,2048]{1,0:T(8,128)}, f32[64,2048]{1,0:T(8,128)S(1)}, u32[]{:S(2)}, u32[]{:S(2)}) collective-permute-start(f32[64,2048]{1,0:T(8,128)} %a00), channel_id=1, source_target_pairs={{0,4},{4,0},{1,5},{5,1},{2,6},{6,2},{3,7},{7,3},{8,12},{12,8},{9,1... | collective-permute-start | bytes 1572872 | tf_op jit(solution)/shard_map/gather_src/ppermute | solution.py:278
  36.8 10.8 %collective-permute-start.34 = (f32[32,2048]{1,0:T(8,128)S(1)}, f32[32,2048]{1,0:T(8,128)S(1)}, u32[]{:S(2)}, u32[]{:S(2)}) collective-permute-start(f32[32,2048]{1,0:T(8,128)S(1)} %slice.191), channel_id=1, source_target_pairs={{0,8},{8,16},{16,24},{24,0},{1,9},{9,17},{17,25},{25,1},{2,10},{10... | collective-permute-start | bytes 786440 | tf_op jit(solution)/shard_map/gather_src/ppermute | solution.py:278
  37.2 26.9 %collective-permute-start.38 = (f32[64,2048]{1,0:T(8,128)S(1)}, f32[64,2048]{1,0:T(8,128)S(1)}, u32[]{:S(2)}, u32[]{:S(2)}) collective-permute-start(f32[64,2048]{1,0:T(8,128)S(1)} %collective-permute-done.33.a30), channel_id=1, source_target_pairs={{0,4},{4,0},{1,5},{5,1},{2,6},{6,2},{3,7},{7,3},{8,12},{12,8},{9,1... | collective-permute-start | bytes 1572872 | tf_op jit(solution)/shard_map/gather_src/ppermute | solution.py:278
  37.2 26.8 %collective-permute-start.37 = (f32[64,2048]{1,0:T(8,128)S(1)}, f32[64,2048]{1,0:T(8,128)S(1)}, u32[]{:S(2)}, u32[]{:S(2)}) collective-permute-start(f32[64,2048]{1,0:T(8,128)S(1)} %collective-permute-done.32.a10), channel_id=1, source_target_pairs={{0,4},{4,0},{1,5},{5,1},{2,6},{6,2},{3,7},{7,3},{8,12},{12,8},{9,1... | collective-permute-start | bytes 1572872 | tf_op jit(solution)/shard_map/gather_src/ppermute | solution.py:278
  37.8 11.2 %collective-permute-start.35 = (f32[32,2048]{1,0:T(8,128)S(1)}, f32[32,2048]{1,0:T(8,128)}, u32[]{:S(2)}, u32[]{:S(2)}) collective-permute-start(f32[32,2048]{1,0:T(8,128)S(1)} %slice.192), channel_id=1, source_target_pairs={{0,24},{8,0},{16,8},{24,16},{1,25},{9,1},{17,9},{25,17},{2,26},{10... | collective-permute-start | bytes 786440 | tf_op jit(solution)/shard_map/gather_src/ppermute | solution.py:278
  47.6 16.5 %collective-permute-start.39 = (f32[32,2048]{1,0:T(8,128)S(1)}, f32[32,2048]{1,0:T(8,128)}, u32[]{:S(2)}, u32[]{:S(2)}) collective-permute-start(f32[32,2048]{1,0:T(8,128)S(1)} %collective-permute-done.34.a2t0), channel_id=1, source_target_pairs={{0,4},{4,0},{1,5},{5,1},{2,6},{6,2},{3,7},{7,3},{8,12},{12,8},{9,1... | collective-permute-start | bytes 786440 | tf_op jit(solution)/shard_map/gather_src/ppermute | solution.py:278
  49.0 15.1 %collective-permute-start.40 = (f32[32,2048]{1,0:T(8,128)}, f32[32,2048]{1,0:T(8,128)}, u32[]{:S(2)}, u32[]{:S(2)}) collective-permute-start(f32[32,2048]{1,0:T(8,128)} %collective-permute-done.35.a2b0), channel_id=1, source_target_pairs={{0,4},{4,0},{1,5},{5,1},{2,6},{6,2},{3,7},{7,3},{8,12},{12,8},{9,1... | collective-permute-start | bytes 786440 | tf_op jit(solution)/shard_map/gather_src/ppermute | solution.py:278
  67.2 29.3 %collective-permute-start.41 = (f32[16,72,128]{2,1,0:T(8,128)S(1)}, f32[16,72,128]{2,1,0:T(8,128)S(1)}, u32[]{:S(2)}, u32[]{:S(2)}) collective-permute-start(f32[16,72,128]{2,1,0:T(8,128)S(1)} %get-tuple-element.400), channel_id=1, source_target_pairs={{0,1},{1,2},{2,3},{3,0},{4,5},{5,6},{6,7},{7,4},{8,9},{9,10},{10,1... | collective-permute-start | bytes 1769480 | tf_op jit(solution)/shard_map/src_exchange/ppermute | solution.py:278
  67.3 29.2 %collective-permute-start.42 = (f32[16,72,128]{2,1,0:T(8,128)S(1)}, f32[16,72,128]{2,1,0:T(8,128)S(1)}, u32[]{:S(2)}, u32[]{:S(2)}) collective-permute-start(f32[16,72,128]{2,1,0:T(8,128)S(1)} %get-tuple-element.401), channel_id=1, source_target_pairs={{0,2},{1,3},{2,0},{3,1},{4,6},{5,7},{6,4},{7,5},{8,10},{9,11},{10,... | collective-permute-start | bytes 1769480 | tf_op jit(solution)/shard_map/src_exchange/ppermute | solution.py:278
  69.3 27.8 %collective-permute-start.43 = (f32[16,72,128]{2,1,0:T(8,128)S(1)}, f32[16,72,128]{2,1,0:T(8,128)S(1)}, u32[]{:S(2)}, u32[]{:S(2)}) collective-permute-start(f32[16,72,128]{2,1,0:T(8,128)S(1)} %get-tuple-element.402), channel_id=1, source_target_pairs={{0,3},{1,0},{2,1},{3,2},{4,7},{5,4},{6,5},{7,6},{8,11},{9,8},{10,9... | collective-permute-start | bytes 1769480 | tf_op jit(solution)/shard_map/src_exchange/ppermute | solution.py:278
  99.1 1.0 copy-start.10
  100.1 1.0 copy-start.12
  101.1 1.1 copy-start.14
  102.1 2.2 %copy-start.8 = (f32[2048,512]{1,0:T(8,128)S(1)}, f32[2048,512]{1,0:T(8,128)}, u32[]{:S(2)}) copy-start(f32[2048,512]{1,0:T(8,128)} %all-gather.7.cloned.1.call-done) | copy-start | bytes 12582916
  104.3 1.2 copy-start.11
  105.5 1.2 copy-start.13
  106.8 1.2 copy-start.15
  115.4 2.0 %copy-start.9 = (f32[8,256,512]{2,1,0:T(8,128)}, f32[8,256,512]{2,1,0:T(8,128)S(1)}, u32[]{:S(2)}) copy-start(f32[8,256,512]{2,1,0:T(8,128)S(1)} %get-tuple-element.417) | copy-start | bytes 12582916
  119.8 2.6 %copy-start.25 = (f32[16,64,128]{2,1,0:T(8,128)S(1)}, f32[16,64,128]{2,1,0:T(8,128)}, u32[]{:S(2)}) copy-start(f32[16,64,128]{2,1,0:T(8,128)} %copy-done.24) | copy-start | bytes 1572868
  119.8 4.8 %copy-start.21 = (f32[16,64,128]{2,1,0:T(8,128)S(1)}, f32[16,64,128]{2,1,0:T(8,128)}, u32[]{:S(2)}) copy-start(f32[16,64,128]{2,1,0:T(8,128)} %copy-done.20) | copy-start | bytes 1572868
  119.8 7.2 %copy-start.17 = (f32[16,64,128]{2,1,0:T(8,128)S(1)}, f32[16,64,128]{2,1,0:T(8,128)}, u32[]{:S(2)}) copy-start(f32[16,64,128]{2,1,0:T(8,128)} %copy-done.16) | copy-start | bytes 1572868
  119.9 7.1 %collective-permute-start.47 = (f32[16,128]{1,0:T(8,128)S(1)}, f32[16,128]{1,0:T(8,128)S(1)}, u32[]{:S(2)}, u32[]{:S(2)}) collective-permute-start(f32[16,128]{1,0:T(8,128)S(1)} %get-tuple-element.412), channel_id=1, source_target_pairs={{0,3},{1,0},{2,1},{3,2},{4,7},{5,4},{6,5},{7,6},{8,11},{9,8},{10,9... | collective-permute-start | bytes 24584 | tf_op jit(solution)/shard_map/hours/ppermute | solution.py:278
  121.4 6.1 %collective-permute-start.48 = (f32[16,128]{1,0:T(8,128)S(1)}, f32[16,128]{1,0:T(8,128)S(1)}, u32[]{:S(2)}, u32[]{:S(2)}) collective-permute-start(f32[16,128]{1,0:T(8,128)S(1)} %get-tuple-element.413), channel_id=1, source_target_pairs={{0,2},{1,3},{2,0},{3,1},{4,6},{5,7},{6,4},{7,5},{8,10},{9,11},{10,... | collective-permute-start | bytes 24584 | tf_op jit(solution)/shard_map/hours/ppermute | solution.py:278
  121.4 6.1 %collective-permute-start.49 = (f32[16,128]{1,0:T(8,128)S(1)}, f32[16,128]{1,0:T(8,128)S(1)}, u32[]{:S(2)}, u32[]{:S(2)}) collective-permute-start(f32[16,128]{1,0:T(8,128)S(1)} %get-tuple-element.414), channel_id=1, source_target_pairs={{0,1},{1,2},{2,3},{3,0},{4,5},{5,6},{6,7},{7,4},{8,9},{9,10},{10,1... | collective-permute-start | bytes 24584 | tf_op jit(solution)/shard_map/hours/ppermute | solution.py:278
  122.4 31.4 %collective-permute-start.44 = (f32[16,64,128]{2,1,0:T(8,128)S(1)}, f32[16,64,128]{2,1,0:T(8,128)S(1)}, u32[]{:S(2)}, u32[]{:S(2)}) collective-permute-start(f32[16,64,128]{2,1,0:T(8,128)S(1)} %copy-done.25), channel_id=1, source_target_pairs={{0,3},{1,0},{2,1},{3,2},{4,7},{5,4},{6,5},{7,6},{8,11},{9,8},{10,9... | collective-permute-start | bytes 1572872 | tf_op jit(solution)/shard_map/src_back/ppermute | solution.py:278
  124.7 29.1 %collective-permute-start.45 = (f32[16,64,128]{2,1,0:T(8,128)S(1)}, f32[16,64,128]{2,1,0:T(8,128)S(1)}, u32[]{:S(2)}, u32[]{:S(2)}) collective-permute-start(f32[16,64,128]{2,1,0:T(8,128)S(1)} %copy-done.21), channel_id=1, source_target_pairs={{0,2},{1,3},{2,0},{3,1},{4,6},{5,7},{6,4},{7,5},{8,10},{9,11},{10,... | collective-permute-start | bytes 1572872 | tf_op jit(solution)/shard_map/src_back/ppermute | solution.py:278
  127.0 26.8 %collective-permute-start.46 = (f32[16,64,128]{2,1,0:T(8,128)S(1)}, f32[16,64,128]{2,1,0:T(8,128)S(1)}, u32[]{:S(2)}, u32[]{:S(2)}) collective-permute-start(f32[16,64,128]{2,1,0:T(8,128)S(1)} %copy-done.17), channel_id=1, source_target_pairs={{0,1},{1,2},{2,3},{3,0},{4,5},{5,6},{6,7},{7,4},{8,9},{9,10},{10,1... | collective-permute-start | bytes 1572872 | tf_op jit(solution)/shard_map/src_back/ppermute | solution.py:278
  155.4 4.2 %collective-permute-start.50 = (f32[4,64,2048]{2,1,0:T(8,128)S(1)}, f32[4,64,2048]{2,1,0:T(8,128)S(1)}, u32[]{:S(2)}, u32[]{:S(2)}) collective-permute-start(f32[4,64,2048]{2,1,0:T(8,128)S(1)} %get-tuple-element.416), channel_id=1, source_target_pairs={{0,4},{4,0},{1,5},{5,1},{2,6},{6,2},{3,7},{7,3},{8,12},{12,8},{9,1... | collective-permute-start | bytes 6291464 | tf_op jit(solution)/shard_map/src_back/ppermute | solution.py:278
  160.9 18.6 %copy-start.36 = (s32[30]{0:T(128)S(1)}, s32[30]{0:T(128)}, u32[]{:S(2)}) copy-start(s32[30]{0:T(128)} %hours.15) | copy-start | bytes 364
  160.9 9.8 %collective-permute-start.51 = (f32[32,2048]{1,0:T(8,128)}, f32[32,2048]{1,0:T(8,128)S(1)}, u32[]{:S(2)}, u32[]{:S(2)}) collective-permute-start(f32[32,2048]{1,0:T(8,128)} %get-tuple-element.496), channel_id=1, source_target_pairs={{0,8},{8,16},{16,24},{24,0},{1,9},{9,17},{17,25},{25,1},{2,10},{10... | collective-permute-start | bytes 786440 | tf_op jit(solution)/shard_map/src_back/ppermute | solution.py:278
  161.9 9.4 %collective-permute-start.53 = (f32[32,2048]{1,0:T(8,128)}, f32[32,2048]{1,0:T(8,128)}, u32[]{:S(2)}, u32[]{:S(2)}) collective-permute-start(f32[32,2048]{1,0:T(8,128)} %get-tuple-element.497), channel_id=1, source_target_pairs={{0,24},{8,0},{16,8},{24,16},{1,25},{9,1},{17,9},{25,17},{2,26},{10... | collective-permute-start | bytes 786440 | tf_op jit(solution)/shard_map/src_back/ppermute | solution.py:278
  165.3 14.2 %copy-start.32 = (s32[1920]{0:T(1024)}, s32[1920]{0:T(1024)S(1)}, u32[]{:S(2)}) copy-start(s32[1920]{0:T(1024)S(1)} %fusion.17) | copy-start | bytes 23044
  173.3 13.5 %collective-permute-start.54 = (f32[64,2048]{1,0:T(8,128)}, f32[64,2048]{1,0:T(8,128)}, u32[]{:S(2)}, u32[]{:S(2)}) collective-permute-start(f32[64,2048]{1,0:T(8,128)} %pad_maximum_fusion.3), channel_id=1, source_target_pairs={{0,24},{8,0},{16,8},{24,16},{1,25},{9,1},{17,9},{25,17},{2,26},{10... | collective-permute-start | bytes 1572872 | tf_op jit(solution)/shard_map/src_back/ppermute | solution.py:278
  176.4 14.0 %collective-permute-start.52 = (f32[64,2048]{1,0:T(8,128)}, f32[64,2048]{1,0:T(8,128)S(1)}, u32[]{:S(2)}, u32[]{:S(2)}) collective-permute-start(f32[64,2048]{1,0:T(8,128)} %pad_maximum_fusion.2), channel_id=1, source_target_pairs={{0,8},{8,16},{16,24},{24,0},{1,9},{9,17},{17,25},{25,1},{2,10},{10... | collective-permute-start | bytes 1572872 | tf_op jit(solution)/shard_map/src_back/ppermute | solution.py:278
  181.0 12.7 %copy-start.28 = (f32[64,2048]{1,0:T(8,128)S(1)}, f32[64,2048]{1,0:T(8,128)}, u32[]{:S(2)}) copy-start(f32[64,2048]{1,0:T(8,128)} %param.13) | copy-start | bytes 1572868
  181.0 12.7 %copy-start.31 = (s32[30,8,128]{2,1,0:T(8,128)S(1)}, s32[30,8,128]{2,1,0:T(8,128)}, u32[]{:S(2)}) copy-start(s32[30,8,128]{2,1,0:T(8,128)} %bits.1) | copy-start | bytes 368644
  181.0 12.7 %copy-start.34 = (s32[1024]{0:T(1024)S(1)}, s32[1024]{0:T(1024)}, u32[]{:S(2)}) copy-start(s32[1024]{0:T(1024)} %src_place.1) | copy-start | bytes 12292
  182.3 10.1 %collective-permute-start.57 = (f32[64,512]{1,0:T(8,128)S(1)}, f32[64,512]{1,0:T(8,128)S(1)}, u32[]{:S(2)}, u32[]{:S(2)}) collective-permute-start(f32[64,512]{1,0:T(8,128)S(1)} %get-tuple-element.500), channel_id=1, source_target_pairs={{0,1},{1,2},{2,3},{3,0},{4,5},{5,6},{6,7},{7,4},{8,9},{9,10},{10,1... | collective-permute-start | bytes 393224 | tf_op jit(solution)/shard_map/dst_back/ppermute | solution.py:278
  182.4 10.0 %collective-permute-start.56 = (f32[64,512]{1,0:T(8,128)S(1)}, f32[64,512]{1,0:T(8,128)S(1)}, u32[]{:S(2)}, u32[]{:S(2)}) collective-permute-start(f32[64,512]{1,0:T(8,128)S(1)} %get-tuple-element.501), channel_id=1, source_target_pairs={{0,2},{1,3},{2,0},{3,1},{4,6},{5,7},{6,4},{7,5},{8,10},{9,11},{10,... | collective-permute-start | bytes 393224 | tf_op jit(solution)/shard_map/dst_back/ppermute | solution.py:278
  183.1 9.2 %collective-permute-start.55 = (f32[64,512]{1,0:T(8,128)S(1)}, f32[64,512]{1,0:T(8,128)S(1)}, u32[]{:S(2)}, u32[]{:S(2)}) collective-permute-start(f32[64,512]{1,0:T(8,128)S(1)} %get-tuple-element.502), channel_id=1, source_target_pairs={{0,3},{1,0},{2,1},{3,2},{4,7},{5,4},{6,5},{7,6},{8,11},{9,8},{10,9... | collective-permute-start | bytes 393224 | tf_op jit(solution)/shard_map/dst_back/ppermute | solution.py:278
  (4 other events, 3.1 us)
Sparse Core Ops, SparseCore 0:
  21.7 64.2 all-gather.6
  120.0 57.4 reduce-scatter.2

commit v3 on v2

--- a/solution.py
+++ b/solution.py
@@ -22,8 +22,9 @@
 VMEM = pl.BlockSpec(memory_space=pltpu.VMEM)
 SMEM = pl.BlockSpec(memory_space=pltpu.SMEM)
 ANY = pl.BlockSpec(memory_space=pl.ANY)
+HBM = pl.BlockSpec(memory_space=pltpu.HBM)
 f32, bf16, i32 = jnp.float32, jnp.bfloat16, jnp.int32
-PARAMS = pltpu.CompilerParams(vmem_limit_bytes=24 * 1024 * 1024)
+MIB = 1024 * 1024
 
 
 def lane_block(within):
@@ -97,22 +98,19 @@
 
     @pl.loop(0, GROUPS)
     def _(g):
-        n = meta[g, 16]
-        for s in range(SLOTS):
-
-            @pl.when(s < n)
+        @pl.loop(0, meta[g, 16])
+        def _(i):
+            dst_at = meta[g, 8 + i]
+            to = jnp.bitwise_and(jnp.right_shift(dst_at, 2), NO - 1)
+            pos = seen[to] - base
+            seen[to] += 1
+
+            @pl.when((pos >= 0) & (pos < PER))
             def _():
-                dst_at = meta[g, 8 + s]
-                to = jnp.bitwise_and(jnp.right_shift(dst_at, 2), NO - 1)
-                pos = seen[to] - base
-                seen[to] += 1
-
-                @pl.when((pos >= 0) & (pos < PER))
-                def _():
-                    at = to * PER + pos
-                    lst[at] = meta[g, s]
-                    lst[LIST + at] = dst_at
-                    lst[2 * LIST + at] = g * 8 + s
+                at = to * PER + pos
+                lst[at] = meta[g, i]
+                lst[LIST + at] = dst_at
+                lst[2 * LIST + at] = g * 8 + i
 
     for o in range(NO):
         lst[3 * LIST + o] = jnp.clip(seen[o] - base, 0, PER)
@@ -159,62 +157,80 @@
         each_tile(own, lst, d, work)
 
 
-def prepare_kernel(scal, lst, a0, a1, a2, a3, high, low, column, entries):
+def tile_kernel(
+    scal, lst, a0, a1, a2, a3, b_all, g_out, u0, u1, u2, u3, h0, h1, h2, h3,
+    blocks, g_sum, u_sum, entries, in_sems, out_sems,
+):
     own = scal[0]
-    a_in = (a0, a1, a2, a3)
+    a_in, u_out, h_out = (a0, a1, a2, a3), (u0, u1, u2, u3), (h0, h1, h2, h3)
+    n = lst[3 * LIST + own]
     shift = jnp.bitwise_and(lax.broadcasted_iota(i32, (32, SIDE), 0), 15)
-
-    def work(j, k):
-        high[j], low[j] = split(jnp.concatenate([r[j, :RK] for r in a_in], axis=0))
-        column[j] = jnp.concatenate([as_column(r[j, RK + 2 : RK + 3, :RK]) for r in a_in], axis=0)
+    ones = jnp.ones((8, SIDE), bf16)
+
+    def place(j):
+        dst_at = lst[LIST + PER * own + j]
+        return jnp.right_shift(dst_at, 7), lane_block(jnp.bitwise_and(dst_at, STORED // NO - 1))
+
+    def fetch(j):
+        z, cols = place(j)
+        return pltpu.make_async_copy(b_all.at[z, :, cols], blocks.at[j], in_sems.at[j])
+
+    @pl.loop(0, n)
+    def _(j):
+        fetch(j).start()
+
+    g_sum[...] = jnp.zeros_like(g_sum)
+
+    @pl.loop(0, n)
+    def _(j):
+        a = split(jnp.concatenate([r[j, :RK] for r in a_in], axis=0))
+        c = jnp.concatenate([as_column(r[j, RK + 2 : RK + 3, :RK]) for r in a_in], axis=0)
         for d in range(NO):
             rows = pl.ds(pl.multiple_of(jnp.bitwise_and(own - d, NO - 1) * 32, 32), 32)
             words = jnp.concatenate(
                 [jnp.broadcast_to(a_in[d][j, RK + i : RK + i + 1, :], (16, SIDE)) for i in range(2)], axis=0
             ).astype(i32)
-            entries[j, rows, :] = jnp.bitwise_and(jnp.right_shift(words, shift), 1).astype(f32)
-
-    each_tile(own, lst, 0, work)
-
-
-def tile_kernel(scal, lst, high, low, column, entries, b_all, g_sum, u0, u1, u2, u3, h0, h1, h2, h3):
-    ones = jnp.ones((8, SIDE), bf16)
-    g_sum[...] = jnp.zeros_like(g_sum)
-
-    def work(j, k):
-        dst_at = lst[LIST + k]
-        z = jnp.right_shift(dst_at, 7)
-        cols = lane_block(jnp.bitwise_and(dst_at, STORED // NO - 1))
-        b_raw = b_all[z, :, cols]
-        c = column[j]
-        a = high[j], low[j]
+            entries[rows, :] = jnp.bitwise_and(jnp.right_shift(words, shift), 1).astype(f32)
+        fetch(j).wait()
+        z, cols = place(j)
+        b_raw = blocks[j]
         b = split(b_raw * c)
-        r = split(jax.nn.sigmoid(dot3(a, b, ((0,), (0,)))) - entries[j])
+        r = split(jax.nn.sigmoid(dot3(a, b, ((0,), (0,)))) - entries[...])
         u = dot3(b, r, ((1,), (1,)))
         g = dot3(a, r, ((1,), (0,)))
         g_sum[z, :, cols] += g * c
         along = lambda x: lax.dot_general(ones, x, (((1,), (1,)), ((), ())), preferred_element_type=f32)
         h_high, h_low = split(b_raw * g)
         h = along(h_high) + along(h_low)
-        for d, (u_out, h_out) in enumerate(zip((u0, u1, u2, u3), (h0, h1, h2, h3))):
-            u_out[j] = u[RK * d : RK * (d + 1)]
-            h_out[pl.ds(j, 1), :RK] = h[:1, RK * d : RK * (d + 1)]
-
-    each_tile(scal[0], lst, 0, work)
+        for d in range(NO):
+            u_sum[d, j] = u[RK * d : RK * (d + 1)]
+            h_out[d][pl.ds(j, 1), :RK] = h[:1, RK * d : RK * (d + 1)]
+
+    copies = [pltpu.make_async_copy(g_sum.at[z], g_out.at[z], out_sems.at[z]) for z in range(NZ)]
+    copies += [pltpu.make_async_copy(u_sum.at[d], u_out[d], out_sems.at[NZ + d]) for d in range(NO)]
+    for copy in copies:
+        copy.start()
+    for copy in copies:
+        copy.wait()
 
 
 def hour_pack_kernel(scal, lst, h0, h1, h2, h3, hour):
     hour[...] = jnp.zeros_like(hour)
+    upper = jnp.right_shift(lax.broadcasted_iota(i32, (1, SIDE), 1), 6)
     for d, h in enumerate((h0, h1, h2, h3)):
 
         def work(j, k):
             slot = lst[2 * LIST + k]
-            hour[jnp.right_shift(slot, 3), pl.ds(jnp.bitwise_and(slot, 7), 1), :RK] = h[pl.ds(j, 1), :RK]
+            g, i = jnp.right_shift(slot, 3), jnp.bitwise_and(slot, 7)
+            cols = lane_block(jnp.right_shift(i, 1))
+            row = h[pl.ds(j, 1), :RK]
+            both = jnp.concatenate([row, row], axis=1)
+            hour[g, :, cols] = jnp.where(upper == jnp.bitwise_and(i, 1), both, hour[g, :, cols])
 
         each_tile(scal[0], lst, d, work)
 
 
-def src_sum_kernel(scal, lst, u0, u1, u2, u3, back, keep, give):
+def src_sum_kernel(scal, lst, u0, u1, u2, u3, hour_terms, keep, give):
     own, x_at, c_at = scal[0], scal[1], scal[2]
     keep[...] = jnp.zeros_like(keep)
     give[...] = jnp.zeros_like(give)
@@ -256,19 +272,22 @@
         @pl.when(at >= 0)
         def _():
             h = hours[t] - first_hour
-            out[pl.ds(h, 1), :] += back[jnp.right_shift(at, 3), pl.ds(jnp.bitwise_and(at, 7), 1), :RK]
+            slot = jnp.bitwise_and(at, 7)
+            both = back[jnp.right_shift(at, 3), :, lane_block(jnp.right_shift(slot, 1))]
+            odd = jnp.broadcast_to(jnp.bitwise_and(slot, 1), (1, RK)) == 1
+            out[pl.ds(h, 1), :] += jnp.where(odd, both[:, RK:], both[:, :RK])
 
 
 def shape(*dims, dtype=f32):
     return jax.ShapeDtypeStruct(dims, dtype)
 
 
-def call(kernel, out_shape, in_specs, args, out_specs=None, scratch=()):
+def call(kernel, out_shape, in_specs, args, out_specs=None, scratch=(), vmem=24):
     if out_specs is None:
         out_specs = jax.tree.map(lambda _: VMEM, out_shape)
     return pl.pallas_call(
         kernel, out_shape=out_shape, in_specs=in_specs, out_specs=out_specs,
-        scratch_shapes=scratch, compiler_params=PARAMS,
+        scratch_shapes=scratch, compiler_params=pltpu.CompilerParams(vmem_limit_bytes=vmem * MIB),
     )(*args)
 
 
@@ -332,20 +351,21 @@
                 src_pack_kernel, (shape(PER, XROWS, SIDE),) * NO, [SMEM] * 2 + [VMEM] * 11, (at, lst, rows) + a_all
             )
             a_in = [hop(v, "own", NO, d) for d, v in enumerate(a_out)]
-            ready = call(
-                prepare_kernel,
-                (shape(PER, RANK, SIDE, dtype=bf16),) * 2 + (shape(PER, RANK, SIDE), shape(PER, SIDE, SIDE)),
-                [SMEM] * 2 + [VMEM] * NO, (at, lst, *a_in),
-            )
         with jax.named_scope("tiles"):
             g_sum, *out = call(
                 tile_kernel,
                 (shape(NZ, RANK, PART),) + (shape(PER, RK, SIDE),) * NO + (shape(PER, SIDE),) * NO,
-                [SMEM] * 2 + [VMEM] * 5, (at, lst, *ready, b_all),
+                [SMEM] * 2 + [VMEM] * NO + [HBM], (at, lst, *a_in, b_all), out_specs=(HBM,) * (1 + NO) + (VMEM,) * NO,
+                scratch=[
+                    pltpu.VMEM((PER, RANK, SIDE), f32), pltpu.VMEM((NZ, RANK, PART), f32),
+                    pltpu.VMEM((NO, PER, RK, SIDE), f32), pltpu.VMEM((SIDE, SIDE), f32),
+                    pltpu.SemaphoreType.DMA((PER,)), pltpu.SemaphoreType.DMA((NZ + NO,)),
+                ],
+                vmem=60,
             )
         with jax.named_scope("hours"):
             h = [hop(v, "own", NO, -d) for d, v in enumerate(out[NO:])]
-            hour_terms = call(hour_pack_kernel, shape(GROUPS, 8, SIDE), [SMEM] * 2 + [VMEM] * NO, (at, lst, *h))
+            hour_terms = call(hour_pack_kernel, shape(GROUPS, 1, 3 * SIDE), [SMEM] * 2 + [VMEM] * NO, (at, lst, *h))
             back = lax.all_to_all(hour_terms, SLAB, 0, 0)
             grad_hour = call(
                 hour_kernel, shape(*hour_factor.shape), [SMEM] * 3 + [VMEM], (scal, tile_hour, where, back)
@@ -354,9 +374,9 @@
             u = [hop(v, "own", NO, -d) for d, v in enumerate(out[:NO])]
             keep, give = call(
                 src_sum_kernel, (shape(NX, RK, STORED * SIDE),) * 2, [SMEM] * 2 + [VMEM] * NO + [ANY],
-                (at, lst, *u, back),
-            )
-            s = keep + hop(give, "c", NC, 1)
+                (at, lst, *u, hour_terms),
+            )
+            s, _ = lax.optimization_barrier((keep + hop(give, "c", NC, 1), back))
             top = hop(s[2, :half], "x", NX, 1)
             bottom = hop(s[2, half:], "x", NX, -1)
             one = hop(jnp.concatenate([s[1, :half] + top, s[1, half:]]), "x", NX, 1)

time: 203 us -> 209 us (1.030)
  blocking collectives: 25.4 us -> 0 us
  waiting for transfers between devices: 63.1 us -> 87 us
  local copies, waits for them, and re-layouts: 18.4 us -> 9.18 us
  Pallas kernels: 27.8 us -> 33.8 us
  starting transfers between devices: 42.8 us -> 48.7 us
  other arithmetic: 7.48 us -> 10.6 us
    all_to_all x1 -> x0, blocking collectives: 25.4 us -> none  [one_round(): back = lax.all_to_all(hour_terms, SLAB, 0, 0)]
    ppermute x29, waiting for transfers between devices: 54 us -> 70.7 us  [hop(): lax.ppermute(value, axis, [(i, (i + by) % size) for i in range(size)])]
    unnamed x40 -> x52, local copies, waits for them, and re-layouts: 14 us -> 3.54 us
    all_to_all x0 -> x1, starting transfers between devices: none -> 7.24 us  [one_round(): back = lax.all_to_all(hour_terms, SLAB, 0, 0)]
    all_to_all x0 -> x1, waiting for transfers between devices: none -> 7.23 us  [one_round(): back = lax.all_to_all(hour_terms, SLAB, 0, 0)]
    pallas_call x10 -> x9, Pallas kernels: 27.8 us -> 33.8 us  [call(): pl.pallas_call(kernel, out_shape=out_shape, in_specs=in_specs, out_specs=...]
    add x1, other arithmetic: 0.3 us -> 3.31 us  [one_round(): s, _ = lax.optimization_barrier((keep + hop(give, 'c', NC, 1), back))]
  transfers between devices with their start and end apart: 32 -> 33, of which waited for: 13 -> 17; matrix products, arithmetic and copies ran while one was open for 5% -> 7% of each run, Pallas kernels for 9% -> 9%
where the time goes in v3:
time: 209 us; the launch traced here: 206 us
  waiting for transfers between devices  87 us (42%)
  starting transfers between devices  48.7 us (23%)
  Pallas kernels  33.8 us (16%)
  between operations  15.8 us (8%)
  other arithmetic  10.6 us (5%)
  local copies, waits for them, and re-layouts  9.18 us (4%)
    ppermute x29, waiting for transfers between devices, hop(): lax.ppermute(value, axis, [(i, (i + by) % size) for i in range(size)])  70.7 us
    pallas_call x9, Pallas kernels, call(): pl.pallas_call(kernel, out_shape=out_shape, in_specs=in_specs, out_specs=...  33.8 us
    ppermute x29, starting transfers between devices, hop(): lax.ppermute(value, axis, [(i, (i + by) % size) for i in range(size)])  31 us
    all_to_all x1, starting transfers between devices, one_round(): got = lax.all_to_all(sent, SLAB, 0, 0)  10.4 us
    all_to_all x1, waiting for transfers between devices, one_round(): got = lax.all_to_all(sent, SLAB, 0, 0)  9.03 us
    all_to_all x1, starting transfers between devices, one_round(): back = lax.all_to_all(hour_terms, SLAB, 0, 0)  7.24 us
    all_to_all x1, waiting for transfers between devices, one_round(): back = lax.all_to_all(hour_terms, SLAB, 0, 0)  7.23 us
  transfers between devices with their start and end apart: 33, of which 17 were waited for; matrix products, arithmetic and copies ran while one was open for 7% of the time, Pallas kernels for 9%

profile of v3, /device:TPU:32, one launch (start us, length us, event | category | flops | bytes accessed | tf_op | source)
XLA Modules:
  0.0 205.8 jit_solution(10033439570119190546)
XLA Ops:
  7.2 1.1 constant_dynamic-slice_fusion.4
  8.4 3.1 %collective-permute-start.31 = (f32[64,512]{1,0:T(8,128)S(1)}, f32[64,512]{1,0:T(8,128)S(1)}, u32[]{:S(2)}, u32[]{:S(2)}) collective-permute-start(f32[64,512]{1,0:T(8,128)S(1)} %get-tuple-element.495), channel_id=1, source_target_pairs={{0,3},{1,0},{2,1},{3,2},{4,7},{5,4},{6,5},{7,6},{8,11},{9,8},{10,9... | collective-permute-start | bytes 393224 | tf_op jit(solution)/shard_map/gather_dst/ppermute | solution.py:297
  12.1 1.0 collective-permute-start.29
  13.8 3.1 %slots.5 = (f32[64,16,128]{2,1,0:T(8,128)}, s32[30]{0:T(128)S(1)}) custom-call(s32[4]{0:T(128)S(1)} %pad_add_fusion.2.scal, s32[30]{0:T(128)} %src_ids.1, s32[30]{0:T(128)} %dst_ids.1, s32[30]{0:T(128)} %hours.12, s32[1024]{0:T(1024)} %src_place.1, s32[1024]{0:T(1024)} %dst_place.1, s32[30,8,128]{2,1,0:T(8,128)} %bits.1, f32[8,64]{1,0:T(8,128)} %hour_rows.1), custom_call_target="tpu_custom_call" | custom-call | tf_op jit(solution)/shard_map/slots/pallas_call | solution.py:288
  17.0 2.3 %collective-permute-done.30.p2 = f32[64,512]{1,0:T(8,128)S(1)} collective-permute-done((f32[64,512]{1,0:T(8,128)S(1)}, f32[64,512]{1,0:T(8,128)S(1)}, u32[]{:S(2)}, u32[]{:S(2)}) %collective-permute-start.30) | collective-permute-done | bytes 131104 | tf_op jit(solution)/shard_map/gather_dst/ppermute | solution.py:297
  19.3 1.4 collective-permute-done.29.p1
  21.6 1.6 collective-permute-start.33
  23.2 1.7 collective-permute-start.32
  24.9 10.4 %all-to-all-start.2 = ((f32[64,16,128]{2,1,0:T(8,128)}), f32[64,16,128]{2,1,0:T(8,128)S(1)}, u32[]{:S(2)}, u32[]{:S(2)}) async-start(f32[64,16,128]{2,1,0:T(8,128)} %get-tuple-element.386), calls=%async_computation.3 | async-start | bytes 1048576 | tf_op jit(solution)/shard_map/slots/all_to_all | solution.py:329
  35.6 1.2 collective-permute-done.33.a30
  37.8 3.0 %collective-permute-start.35 = (f32[32,2048]{1,0:T(8,128)S(1)}, f32[32,2048]{1,0:T(8,128)}, u32[]{:S(2)}, u32[]{:S(2)}) collective-permute-start(f32[32,2048]{1,0:T(8,128)S(1)} %slice.185), channel_id=1, source_target_pairs={{0,24},{8,0},{16,8},{24,16},{1,25},{9,1},{17,9},{25,17},{2,26},{10... | collective-permute-start | bytes 786440 | tf_op jit(solution)/shard_map/gather_src/ppermute | solution.py:297
  40.8 6.8 %collective-permute-done.34.a2t0 = f32[32,2048]{1,0:T(8,128)S(1)} collective-permute-done((f32[32,2048]{1,0:T(8,128)S(1)}, f32[32,2048]{1,0:T(8,128)S(1)}, u32[]{:S(2)}, u32[]{:S(2)}) %collective-permute-start.34) | collective-permute-done | bytes 262176 | tf_op jit(solution)/shard_map/gather_src/ppermute | solution.py:297
  47.6 1.4 collective-permute-done.35.a2b0
  49.1 9.0 %all-to-all-done.2.got = f32[64,16,128]{2,1,0:T(8,128)S(1)} async-done(((f32[64,16,128]{2,1,0:T(8,128)}), f32[64,16,128]{2,1,0:T(8,128)S(1)}, u32[]{:S(2)}, u32[]{:S(2)}) %all-to-all-start.2) | async-done | bytes 524320 | tf_op jit(solution)/shard_map/slots/all_to_all | solution.py:329
  58.1 3.7 %list.2.lst = s32[200]{0:T(256)S(1)} custom-call(s32[4]{0:T(128)S(1)} %pad_add_fusion.3.scal, f32[64,16,128]{2,1,0:T(8,128)S(1)} %all-to-all-done.2.got), custom_call_target="tpu_custom_call" | custom-call | tf_op jit(solution)/shard_map/list/pallas_call | solution.py:288
  61.8 2.9 %src_exchange.5 = (f32[16,72,128]{2,1,0:T(8,128)S(1)}, f32[16,72,128]{2,1,0:T(8,128)S(1)}, f32[16,72,128]{2,1,0:T(8,128)S(1)}, f32[16,72,128]{2,1,0:T(8,128)S(1)}) custom-call(s32[4]{0:T(128)S(1)} %pad_add_fusion.3.scal, s32[200]{0:T(256)S(1)} %list.2.lst, f32[1024,128]{1,0:T(8,128)S(1)} %bitcast.91, f32[64,2048]{1,0:T(8,128)} %a00, ...), custom_call_target="tpu_custom_call" | custom-call | tf_op jit(solution)/shard_map/src_exchange/pallas_call | solution.py:288
  64.8 0.8 copy-done.6
  65.6 2.0 collective-permute-start.42
  67.7 1.3 collective-permute-start.43
  69.0 25.5 %collective-permute-done.41.a1 = f32[16,72,128]{2,1,0:T(8,128)S(1)} collective-permute-done((f32[16,72,128]{2,1,0:T(8,128)S(1)}, f32[16,72,128]{2,1,0:T(8,128)S(1)}, u32[]{:S(2)}, u32[]{:S(2)}) %collective-permute-start.41) | collective-permute-done | bytes 589856 | tf_op jit(solution)/shard_map/src_exchange/ppermute | solution.py:297
  95.9 12.8 %tiles.5 = (f32[8,256,512]{2,1,0:T(8,128)}, f32[16,64,128]{2,1,0:T(8,128)}, f32[16,64,128]{2,1,0:T(8,128)}, f32[16,64,128]{2,1,0:T(8,128)}, f32[16,64,128]{2,1,0...) custom-call(s32[4]{0:T(128)} %copy-done.11, s32[200]{0:T(256)} %copy-done.9, ...), custom_call_target="tpu_custom_call" | custom-call | tf_op jit(solution)/shard_map/tiles/pallas_call | solution.py:288
  108.8 0.9 copy-done.41
  109.9 2.6 %collective-permute-start.45 = (f32[16,64,128]{2,1,0:T(8,128)S(1)}, f32[16,64,128]{2,1,0:T(8,128)S(1)}, u32[]{:S(2)}, u32[]{:S(2)}) collective-permute-start(f32[16,64,128]{2,1,0:T(8,128)S(1)} %copy-done.39), channel_id=1, source_target_pairs={{0,2},{1,3},{2,0},{3,1},{4,6},{5,7},{6,4},{7,5},{8,10},{9,11},{10,... | collective-permute-start | bytes 1572872 | tf_op jit(solution)/shard_map/src_back/ppermute | solution.py:297
  112.5 1.3 collective-permute-start.46
  113.7 2.0 collective-permute-start.47
  116.0 17.0 %collective-permute-done.47.h1 = f32[16,128]{1,0:T(8,128)S(1)} collective-permute-done((f32[16,128]{1,0:T(8,128)S(1)}, f32[16,128]{1,0:T(8,128)S(1)}, u32[]{:S(2)}, u32[]{:S(2)}) %collective-permute-start.47) | collective-permute-done | bytes 8224 | tf_op jit(solution)/shard_map/hours/ppermute | solution.py:297
  132.9 3.6 %collective-permute-done.48.h2 = f32[16,128]{1,0:T(8,128)S(1)} collective-permute-done((f32[16,128]{1,0:T(8,128)S(1)}, f32[16,128]{1,0:T(8,128)S(1)}, u32[]{:S(2)}, u32[]{:S(2)}) %collective-permute-start.48) | collective-permute-done | bytes 8224 | tf_op jit(solution)/shard_map/hours/ppermute | solution.py:297
  136.5 1.7 collective-permute-done.49.h3
  138.3 3.0 %hours.10.hour_terms = f32[64,1,384]{2,1,0:T(1,128)} custom-call(s32[4]{0:T(128)S(1)} %copy-done.12, s32[200]{0:T(256)S(1)} %copy-done.10, f32[16,128]{1,0:T(8,128)S(1)} %copy-done.13, f32[16,128]{1,0:T(8,128)S(1)} %collective-permute-done.47.h1, f32[16,128]{1,0:T(8,128)S(1)} %collective-permute-done.48.h2, f32[16,128]{1,0:T(8,128)S(1)} %collective-permute-done.49.h3), custom_call_target="tpu_custom_call" | custom-call | tf_op jit(solution)/shard_map/hours/pallas_call | solution.py:288
  141.3 2.9 %src_back.5 = (f32[4,64,2048]{2,1,0:T(8,128)S(1)}, f32[4,64,2048]{2,1,0:T(8,128)}) custom-call(s32[4]{0:T(128)S(1)} %copy-done.12, s32[200]{0:T(256)S(1)} %copy-done.10, f32[16,64,128]{2,1,0:T(8,128)S(1)} %copy-done.7, f32[16,64,128]{2,1,0:T(8,128)S(1)} %collective-permute-done.44.u1, f32[16,64,128]{2,1,0:T(8,128)S(1)} %collective-permute-done.45.u2, ...), custom_call_target="tpu_custom_call" | custom-call | tf_op jit(solution)/shard_map/src_back/pallas_call | solution.py:288
  144.2 7.2 %all-to-all-start.3 = ((f32[64,1,384]{2,1,0:T(1,128)}), f32[64,1,384]{2,1,0:T(1,128)S(1)}, u32[]{:S(2)}, u32[]{:S(2)}) async-start(f32[64,1,384]{2,1,0:T(1,128)} %hours.10.hour_terms), calls=%async_computation.4 | async-start | bytes 196608 | tf_op jit(solution)/shard_map/hours/all_to_all | solution.py:369
  151.5 3.3 %add.201 = f32[4,64,2048]{2,1,0:T(8,128)} add(f32[4,64,2048]{2,1,0:T(8,128)S(1)} %get-tuple-element.405, f32[4,64,2048]{2,1,0:T(8,128)} %collective-permute-done.50) | non-fusion elementwise | flops 524288 | bytes 6291456 | tf_op jit(solution)/shard_map/src_back/add | solution.py:379
  154.8 7.2 %all-to-all-done.3.back = f32[64,1,384]{2,1,0:T(1,128)S(1)} async-done(((f32[64,1,384]{2,1,0:T(1,128)}), f32[64,1,384]{2,1,0:T(1,128)S(1)}, u32[]{:S(2)}, u32[]{:S(2)}) %all-to-all-start.3) | async-done | bytes 98336 | tf_op jit(solution)/shard_map/hours/all_to_all | solution.py:369
  162.1 2.0 slice_bitcast_fusion.11
  164.7 2.6 %collective-permute-start.53 = (f32[32,2048]{1,0:T(8,128)S(1)}, f32[32,2048]{1,0:T(8,128)}, u32[]{:S(2)}, u32[]{:S(2)}) collective-permute-start(f32[32,2048]{1,0:T(8,128)S(1)} %get-tuple-element.488), channel_id=1, source_target_pairs={{0,24},{8,0},{16,8},{24,16},{1,25},{9,1},{17,9},{25,17},{2,26},{10... | collective-permute-start | bytes 786440 | tf_op jit(solution)/shard_map/src_back/ppermute | solution.py:297
  167.3 1.4 slice_sign_fusion
  169.1 4.7 %collective-permute-done.51 = f32[32,2048]{1,0:T(8,128)S(1)} collective-permute-done((f32[32,2048]{1,0:T(8,128)}, f32[32,2048]{1,0:T(8,128)S(1)}, u32[]{:S(2)}, u32[]{:S(2)}) %collective-permute-start.51) | collective-permute-done | bytes 262176 | tf_op jit(solution)/shard_map/src_back/ppermute | solution.py:297
  174.5 1.1 bitcast_add_fusion.5
  176.4 2.1 %collective-permute-start.54 = (f32[64,2048]{1,0:T(8,128)}, f32[64,2048]{1,0:T(8,128)}, u32[]{:S(2)}, u32[]{:S(2)}) collective-permute-start(f32[64,2048]{1,0:T(8,128)} %pad_maximum_fusion.3), channel_id=1, source_target_pairs={{0,24},{8,0},{16,8},{24,16},{1,25},{9,1},{17,9},{25,17},{2,26},{10... | collective-permute-start | bytes 1572872 | tf_op jit(solution)/shard_map/src_back/ppermute | solution.py:297
  180.9 0.9 sign.59
  181.9 3.2 %hours.11 = f32[8,64]{1,0:T(8,128)} custom-call(s32[4]{0:T(128)S(1)} %pad_add_fusion.2.scal, s32[30]{0:T(128)S(1)} %copy-done.30, s32[30]{0:T(128)S(1)} %get-tuple-element.409.where, f32[64,1,384]{2,1,0:T(1,128)S(1)} %all-to-all-done.3.back), custom_call_target="tpu_custom_call" | custom-call | tf_op jit(solution)/shard_map/hours/pallas_call | solution.py:288
  185.2 1.2 slice_bitcast_fusion.12
  186.5 3.2 %collective-permute-start.56 = (f32[64,512]{1,0:T(8,128)S(1)}, f32[64,512]{1,0:T(8,128)S(1)}, u32[]{:S(2)}, u32[]{:S(2)}) collective-permute-start(f32[64,512]{1,0:T(8,128)S(1)} %get-tuple-element.492), channel_id=1, source_target_pairs={{0,2},{1,3},{2,0},{3,1},{4,6},{5,7},{6,4},{7,5},{8,10},{9,11},{10,... | collective-permute-start | bytes 393224 | tf_op jit(solution)/shard_map/dst_back/ppermute | solution.py:297
  190.3 2.2 %collective-permute-done.52 = f32[64,2048]{1,0:T(8,128)} collective-permute-done((f32[64,2048]{1,0:T(8,128)S(1)}, f32[64,2048]{1,0:T(8,128)}, u32[]{:S(2)}, u32[]{:S(2)}) %collective-permute-start.52) | collective-permute-done | bytes 524320 | tf_op jit(solution)/shard_map/src_back/ppermute | solution.py:297
  192.5 2.1 %fusion.7 = f32[64,2048]{1,0:T(8,128)} fusion(f32[64,2048]{1,0:T(8,128)} %collective-permute-done.54, f32[64,2048]{1,0:T(8,128)} %collective-permute-done.52, f32[4,64,2048]{2,1,0:T(8,128)S(1)} %copy-done.22), kind=kLoop, calls=%fused_computation.36 | loop fusion | flops 262144 | bytes 2097152 | tf_op jit(solution)/shard_map/src_back/add | solution.py:384
  194.6 1.5 collective-permute-done.56.p2
  196.6 1.4 dst_back.5
  198.1 0.9 while.18
  (104 shorter events, 10.7 us)
Async XLA Ops:
  7.2 87.9 %all-gather.7.cloned.1.call-start = ((), (), s32[]{:S(2)}) async-start(), calls=%async_computation.7 | async-start | bytes 4718592 | tf_op jit(solution)/shard_map/gather_dst/all_gather | solution.py:327
  8.4 8.7 %collective-permute-start.31 = (f32[64,512]{1,0:T(8,128)S(1)}, f32[64,512]{1,0:T(8,128)S(1)}, u32[]{:S(2)}, u32[]{:S(2)}) collective-permute-start(f32[64,512]{1,0:T(8,128)S(1)} %get-tuple-element.495), channel_id=1, source_target_pairs={{0,3},{1,0},{2,1},{3,2},{4,7},{5,4},{6,5},{7,6},{8,11},{9,8},{10,9... | collective-permute-start | bytes 393224 | tf_op jit(solution)/shard_map/gather_dst/ppermute | solution.py:297
  11.5 7.9 %collective-permute-start.30 = (f32[64,512]{1,0:T(8,128)S(1)}, f32[64,512]{1,0:T(8,128)S(1)}, u32[]{:S(2)}, u32[]{:S(2)}) collective-permute-start(f32[64,512]{1,0:T(8,128)S(1)} %get-tuple-element.496), channel_id=1, source_target_pairs={{0,2},{1,3},{2,0},{3,1},{4,6},{5,7},{6,4},{7,5},{8,10},{9,11},{10,... | collective-permute-start | bytes 393224 | tf_op jit(solution)/shard_map/gather_dst/ppermute | solution.py:297
  12.1 8.6 %collective-permute-start.29 = (f32[64,512]{1,0:T(8,128)S(1)}, f32[64,512]{1,0:T(8,128)S(1)}, u32[]{:S(2)}, u32[]{:S(2)}) collective-permute-start(f32[64,512]{1,0:T(8,128)S(1)} %get-tuple-element.497), channel_id=1, source_target_pairs={{0,1},{1,2},{2,3},{3,0},{4,5},{5,6},{6,7},{7,4},{8,9},{9,10},{10,1... | collective-permute-start | bytes 393224 | tf_op jit(solution)/shard_map/gather_dst/ppermute | solution.py:297
  21.6 15.2 %collective-permute-start.33 = (f32[64,2048]{1,0:T(8,128)}, f32[64,2048]{1,0:T(8,128)S(1)}, u32[]{:S(2)}, u32[]{:S(2)}) collective-permute-start(f32[64,2048]{1,0:T(8,128)} %a00), channel_id=1, source_target_pairs={{0,8},{8,16},{16,24},{24,0},{1,9},{9,17},{17,25},{25,1},{2,10},{10... | collective-permute-start | bytes 1572872 | tf_op jit(solution)/shard_map/gather_src/ppermute | solution.py:297
  23.2 14.1 %collective-permute-start.32 = (f32[64,2048]{1,0:T(8,128)}, f32[64,2048]{1,0:T(8,128)S(1)}, u32[]{:S(2)}, u32[]{:S(2)}) collective-permute-start(f32[64,2048]{1,0:T(8,128)} %a00), channel_id=1, source_target_pairs={{0,24},{8,0},{16,8},{24,16},{1,25},{9,1},{17,9},{25,17},{2,26},{10... | collective-permute-start | bytes 1572872 | tf_op jit(solution)/shard_map/gather_src/ppermute | solution.py:297
  24.9 33.2 %all-to-all-start.2 = ((f32[64,16,128]{2,1,0:T(8,128)}), f32[64,16,128]{2,1,0:T(8,128)S(1)}, u32[]{:S(2)}, u32[]{:S(2)}) async-start(f32[64,16,128]{2,1,0:T(8,128)} %get-tuple-element.386), calls=%async_computation.3 | async-start | bytes 1048576 | tf_op jit(solution)/shard_map/slots/all_to_all | solution.py:329
  35.3 149.9 %reduce-scatter.3.cloned.1.call-start = ((), (), s32[]{:S(2)}) async-start(), calls=%async_computation.6 | async-start | bytes 4718592 | tf_op jit(solution)/shard_map/dst_back/reduce_scatter | solution.py:386
  35.3 26.4 %collective-permute-start.36 = (f32[64,2048]{1,0:T(8,128)}, f32[64,2048]{1,0:T(8,128)S(1)}, u32[]{:S(2)}, u32[]{:S(2)}) collective-permute-start(f32[64,2048]{1,0:T(8,128)} %a00), channel_id=1, source_target_pairs={{0,4},{4,0},{1,5},{5,1},{2,6},{6,2},{3,7},{7,3},{8,12},{12,8},{9,1... | collective-permute-start | bytes 1572872 | tf_op jit(solution)/shard_map/gather_src/ppermute | solution.py:297
  36.8 10.8 %collective-permute-start.34 = (f32[32,2048]{1,0:T(8,128)S(1)}, f32[32,2048]{1,0:T(8,128)S(1)}, u32[]{:S(2)}, u32[]{:S(2)}) collective-permute-start(f32[32,2048]{1,0:T(8,128)S(1)} %slice.184), channel_id=1, source_target_pairs={{0,8},{8,16},{16,24},{24,0},{1,9},{9,17},{17,25},{25,1},{2,10},{10... | collective-permute-start | bytes 786440 | tf_op jit(solution)/shard_map/gather_src/ppermute | solution.py:297
  37.2 24.6 %collective-permute-start.38 = (f32[64,2048]{1,0:T(8,128)S(1)}, f32[64,2048]{1,0:T(8,128)S(1)}, u32[]{:S(2)}, u32[]{:S(2)}) collective-permute-start(f32[64,2048]{1,0:T(8,128)S(1)} %collective-permute-done.33.a30), channel_id=1, source_target_pairs={{0,4},{4,0},{1,5},{5,1},{2,6},{6,2},{3,7},{7,3},{8,12},{12,8},{9,1... | collective-permute-start | bytes 1572872 | tf_op jit(solution)/shard_map/gather_src/ppermute | solution.py:297
  37.2 24.6 %collective-permute-start.37 = (f32[64,2048]{1,0:T(8,128)S(1)}, f32[64,2048]{1,0:T(8,128)S(1)}, u32[]{:S(2)}, u32[]{:S(2)}) collective-permute-start(f32[64,2048]{1,0:T(8,128)S(1)} %collective-permute-done.32.a10), channel_id=1, source_target_pairs={{0,4},{4,0},{1,5},{5,1},{2,6},{6,2},{3,7},{7,3},{8,12},{12,8},{9,1... | collective-permute-start | bytes 1572872 | tf_op jit(solution)/shard_map/gather_src/ppermute | solution.py:297
  37.8 11.2 %collective-permute-start.35 = (f32[32,2048]{1,0:T(8,128)S(1)}, f32[32,2048]{1,0:T(8,128)}, u32[]{:S(2)}, u32[]{:S(2)}) collective-permute-start(f32[32,2048]{1,0:T(8,128)S(1)} %slice.185), channel_id=1, source_target_pairs={{0,24},{8,0},{16,8},{24,16},{1,25},{9,1},{17,9},{25,17},{2,26},{10... | collective-permute-start | bytes 786440 | tf_op jit(solution)/shard_map/gather_src/ppermute | solution.py:297
  47.6 14.2 %collective-permute-start.39 = (f32[32,2048]{1,0:T(8,128)S(1)}, f32[32,2048]{1,0:T(8,128)}, u32[]{:S(2)}, u32[]{:S(2)}) collective-permute-start(f32[32,2048]{1,0:T(8,128)S(1)} %collective-permute-done.34.a2t0), channel_id=1, source_target_pairs={{0,4},{4,0},{1,5},{5,1},{2,6},{6,2},{3,7},{7,3},{8,12},{12,8},{9,1... | collective-permute-start | bytes 786440 | tf_op jit(solution)/shard_map/gather_src/ppermute | solution.py:297
  49.0 12.8 %collective-permute-start.40 = (f32[32,2048]{1,0:T(8,128)}, f32[32,2048]{1,0:T(8,128)}, u32[]{:S(2)}, u32[]{:S(2)}) collective-permute-start(f32[32,2048]{1,0:T(8,128)} %collective-permute-done.35.a2b0), channel_id=1, source_target_pairs={{0,4},{4,0},{1,5},{5,1},{2,6},{6,2},{3,7},{7,3},{8,12},{12,8},{9,1... | collective-permute-start | bytes 786440 | tf_op jit(solution)/shard_map/gather_src/ppermute | solution.py:297
  49.1 15.7 %copy-start.11 = (s32[4]{0:T(128)}, s32[4]{0:T(128)S(1)}, u32[]{:S(2)}) copy-start(s32[4]{0:T(128)S(1)} %pad_add_fusion.3.scal) | copy-start | bytes 52
  65.6 28.8 %collective-permute-start.41 = (f32[16,72,128]{2,1,0:T(8,128)S(1)}, f32[16,72,128]{2,1,0:T(8,128)S(1)}, u32[]{:S(2)}, u32[]{:S(2)}) collective-permute-start(f32[16,72,128]{2,1,0:T(8,128)S(1)} %get-tuple-element.394), channel_id=1, source_target_pairs={{0,1},{1,2},{2,3},{3,0},{4,5},{5,6},{6,7},{7,4},{8,9},{9,10},{10,1... | collective-permute-start | bytes 1769480 | tf_op jit(solution)/shard_map/src_exchange/ppermute | solution.py:297
  65.6 28.8 %collective-permute-start.42 = (f32[16,72,128]{2,1,0:T(8,128)S(1)}, f32[16,72,128]{2,1,0:T(8,128)S(1)}, u32[]{:S(2)}, u32[]{:S(2)}) collective-permute-start(f32[16,72,128]{2,1,0:T(8,128)S(1)} %get-tuple-element.395), channel_id=1, source_target_pairs={{0,2},{1,3},{2,0},{3,1},{4,6},{5,7},{6,4},{7,5},{8,10},{9,11},{10,... | collective-permute-start | bytes 1769480 | tf_op jit(solution)/shard_map/src_exchange/ppermute | solution.py:297
  67.7 27.4 %collective-permute-start.43 = (f32[16,72,128]{2,1,0:T(8,128)S(1)}, f32[16,72,128]{2,1,0:T(8,128)S(1)}, u32[]{:S(2)}, u32[]{:S(2)}) collective-permute-start(f32[16,72,128]{2,1,0:T(8,128)S(1)} %get-tuple-element.396), channel_id=1, source_target_pairs={{0,3},{1,0},{2,1},{3,2},{4,7},{5,4},{6,5},{7,6},{8,11},{9,8},{10,9... | collective-permute-start | bytes 1769480 | tf_op jit(solution)/shard_map/src_exchange/ppermute | solution.py:297
  108.7 24.2 %copy-start.43 = (f32[16,128]{1,0:T(8,128)S(1)}, f32[16,128]{1,0:T(8,128)}, u32[]{:S(2)}) copy-start(f32[16,128]{1,0:T(8,128)} %get-tuple-element.404) | copy-start | bytes 24580
  108.7 29.5 %copy-start.10 = (s32[200]{0:T(256)S(1)}, s32[200]{0:T(256)}, u32[]{:S(2)}) copy-start(s32[200]{0:T(256)} %copy-done.9) | copy-start | bytes 2404
  108.7 29.5 %copy-start.12 = (s32[4]{0:T(128)S(1)}, s32[4]{0:T(128)}, u32[]{:S(2)}) copy-start(s32[4]{0:T(128)} %copy-done.11) | copy-start | bytes 52
  108.7 29.5 %copy-start.13 = (f32[16,128]{1,0:T(8,128)S(1)}, f32[16,128]{1,0:T(8,128)}, u32[]{:S(2)}) copy-start(f32[16,128]{1,0:T(8,128)} %get-tuple-element.401.h0) | copy-start | bytes 24580
  108.8 32.6 %copy-start.7 = (f32[16,64,128]{2,1,0:T(8,128)S(1)}, f32[16,64,128]{2,1,0:T(8,128)}, u32[]{:S(2)}) copy-start(f32[16,64,128]{2,1,0:T(8,128)} %get-tuple-element.397.u0) | copy-start | bytes 1572868
  109.7 31.6 %collective-permute-start.44 = (f32[16,64,128]{2,1,0:T(8,128)S(1)}, f32[16,64,128]{2,1,0:T(8,128)S(1)}, u32[]{:S(2)}, u32[]{:S(2)}) collective-permute-start(f32[16,64,128]{2,1,0:T(8,128)S(1)} %copy-done.41), channel_id=1, source_target_pairs={{0,3},{1,0},{2,1},{3,2},{4,7},{5,4},{6,5},{7,6},{8,11},{9,8},{10,9... | collective-permute-start | bytes 1572872 | tf_op jit(solution)/shard_map/src_back/ppermute | solution.py:297
  109.9 31.4 %collective-permute-start.45 = (f32[16,64,128]{2,1,0:T(8,128)S(1)}, f32[16,64,128]{2,1,0:T(8,128)S(1)}, u32[]{:S(2)}, u32[]{:S(2)}) collective-permute-start(f32[16,64,128]{2,1,0:T(8,128)S(1)} %copy-done.39), channel_id=1, source_target_pairs={{0,2},{1,3},{2,0},{3,1},{4,6},{5,7},{6,4},{7,5},{8,10},{9,11},{10,... | collective-permute-start | bytes 1572872 | tf_op jit(solution)/shard_map/src_back/ppermute | solution.py:297
  112.5 28.9 %collective-permute-start.46 = (f32[16,64,128]{2,1,0:T(8,128)S(1)}, f32[16,64,128]{2,1,0:T(8,128)S(1)}, u32[]{:S(2)}, u32[]{:S(2)}) collective-permute-start(f32[16,64,128]{2,1,0:T(8,128)S(1)} %copy-done.37), channel_id=1, source_target_pairs={{0,1},{1,2},{2,3},{3,0},{4,5},{5,6},{6,7},{7,4},{8,9},{9,10},{10,1... | collective-permute-start | bytes 1572872 | tf_op jit(solution)/shard_map/src_back/ppermute | solution.py:297
  113.7 19.2 %collective-permute-start.47 = (f32[16,128]{1,0:T(8,128)S(1)}, f32[16,128]{1,0:T(8,128)S(1)}, u32[]{:S(2)}, u32[]{:S(2)}) collective-permute-start(f32[16,128]{1,0:T(8,128)S(1)} %copy-done.47), channel_id=1, source_target_pairs={{0,3},{1,0},{2,1},{3,2},{4,7},{5,4},{6,5},{7,6},{8,11},{9,8},{10,9... | collective-permute-start | bytes 24584 | tf_op jit(solution)/shard_map/hours/ppermute | solution.py:297
  115.7 20.8 %collective-permute-start.48 = (f32[16,128]{1,0:T(8,128)S(1)}, f32[16,128]{1,0:T(8,128)S(1)}, u32[]{:S(2)}, u32[]{:S(2)}) collective-permute-start(f32[16,128]{1,0:T(8,128)S(1)} %copy-done.45), channel_id=1, source_target_pairs={{0,2},{1,3},{2,0},{3,1},{4,6},{5,7},{6,4},{7,5},{8,10},{9,11},{10,... | collective-permute-start | bytes 24584 | tf_op jit(solution)/shard_map/hours/ppermute | solution.py:297
  132.9 5.3 %collective-permute-start.49 = (f32[16,128]{1,0:T(8,128)S(1)}, f32[16,128]{1,0:T(8,128)S(1)}, u32[]{:S(2)}, u32[]{:S(2)}) collective-permute-start(f32[16,128]{1,0:T(8,128)S(1)} %copy-done.43), channel_id=1, source_target_pairs={{0,1},{1,2},{2,3},{3,0},{4,5},{5,6},{6,7},{7,4},{8,9},{9,10},{10,1... | collective-permute-start | bytes 24584 | tf_op jit(solution)/shard_map/hours/ppermute | solution.py:297
  144.2 7.3 %collective-permute-start.50 = (f32[4,64,2048]{2,1,0:T(8,128)}, f32[4,64,2048]{2,1,0:T(8,128)}, u32[]{:S(2)}, u32[]{:S(2)}) collective-permute-start(f32[4,64,2048]{2,1,0:T(8,128)} %get-tuple-element.406), channel_id=1, source_target_pairs={{0,4},{4,0},{1,5},{5,1},{2,6},{6,2},{3,7},{7,3},{8,12},{12,8},{9,1... | collective-permute-start | bytes 6291464 | tf_op jit(solution)/shard_map/src_back/ppermute | solution.py:297
  144.2 17.8 %all-to-all-start.3 = ((f32[64,1,384]{2,1,0:T(1,128)}), f32[64,1,384]{2,1,0:T(1,128)S(1)}, u32[]{:S(2)}, u32[]{:S(2)}) async-start(f32[64,1,384]{2,1,0:T(1,128)} %hours.10.hour_terms), calls=%async_computation.4 | async-start | bytes 196608 | tf_op jit(solution)/shard_map/hours/all_to_all | solution.py:369
  154.8 19.7 %copy-start.22 = (f32[4,64,2048]{2,1,0:T(8,128)S(1)}, f32[4,64,2048]{2,1,0:T(8,128)}, u32[]{:S(2)}) copy-start(f32[4,64,2048]{2,1,0:T(8,128)} %add.201) | copy-start | bytes 6291460
  164.0 17.8 %copy-start.30 = (s32[30]{0:T(128)S(1)}, s32[30]{0:T(128)}, u32[]{:S(2)}) copy-start(s32[30]{0:T(128)} %hours.12) | copy-start | bytes 364
  164.0 9.7 %collective-permute-start.51 = (f32[32,2048]{1,0:T(8,128)}, f32[32,2048]{1,0:T(8,128)S(1)}, u32[]{:S(2)}, u32[]{:S(2)}) collective-permute-start(f32[32,2048]{1,0:T(8,128)} %get-tuple-element.487), channel_id=1, source_target_pairs={{0,8},{8,16},{16,24},{24,0},{1,9},{9,17},{17,25},{25,1},{2,10},{10... | collective-permute-start | bytes 786440 | tf_op jit(solution)/shard_map/src_back/ppermute | solution.py:297
  164.7 9.8 %collective-permute-start.53 = (f32[32,2048]{1,0:T(8,128)S(1)}, f32[32,2048]{1,0:T(8,128)}, u32[]{:S(2)}, u32[]{:S(2)}) collective-permute-start(f32[32,2048]{1,0:T(8,128)S(1)} %get-tuple-element.488), channel_id=1, source_target_pairs={{0,24},{8,0},{16,8},{24,16},{1,25},{9,1},{17,9},{25,17},{2,26},{10... | collective-permute-start | bytes 786440 | tf_op jit(solution)/shard_map/src_back/ppermute | solution.py:297
  176.4 13.8 %collective-permute-start.54 = (f32[64,2048]{1,0:T(8,128)}, f32[64,2048]{1,0:T(8,128)}, u32[]{:S(2)}, u32[]{:S(2)}) collective-permute-start(f32[64,2048]{1,0:T(8,128)} %pad_maximum_fusion.3), channel_id=1, source_target_pairs={{0,24},{8,0},{16,8},{24,16},{1,25},{9,1},{17,9},{25,17},{2,26},{10... | collective-permute-start | bytes 1572872 | tf_op jit(solution)/shard_map/src_back/ppermute | solution.py:297
  178.6 13.9 %collective-permute-start.52 = (f32[64,2048]{1,0:T(8,128)S(1)}, f32[64,2048]{1,0:T(8,128)}, u32[]{:S(2)}, u32[]{:S(2)}) collective-permute-start(f32[64,2048]{1,0:T(8,128)S(1)} %pad_maximum_fusion.2), channel_id=1, source_target_pairs={{0,8},{8,16},{16,24},{24,0},{1,9},{9,17},{17,25},{25,1},{2,10},{10... | collective-permute-start | bytes 1572872 | tf_op jit(solution)/shard_map/src_back/ppermute | solution.py:297
  185.1 12.9 %copy-start.17 = (f32[64,2048]{1,0:T(8,128)S(1)}, f32[64,2048]{1,0:T(8,128)}, u32[]{:S(2)}) copy-start(f32[64,2048]{1,0:T(8,128)} %param.13) | copy-start | bytes 1572868
  185.1 12.9 %copy-start.27 = (s32[1024]{0:T(1024)S(1)}, s32[1024]{0:T(1024)}, u32[]{:S(2)}) copy-start(s32[1024]{0:T(1024)} %src_place.1) | copy-start | bytes 12292
  185.1 12.9 %copy-start.28 = (s32[1024]{0:T(1024)S(1)}, s32[1024]{0:T(1024)}, u32[]{:S(2)}) copy-start(s32[1024]{0:T(1024)} %dst_place.1) | copy-start | bytes 12292
  185.1 12.9 %copy-start.29 = (f32[8,64]{1,0:T(8,128)S(1)}, f32[8,64]{1,0:T(8,128)}, u32[]{:S(2)}) copy-start(f32[8,64]{1,0:T(8,128)} %hour_rows.1) | copy-start | bytes 6148
  185.1 12.9 %copy-start.31 = (s32[30]{0:T(128)S(1)}, s32[30]{0:T(128)}, u32[]{:S(2)}) copy-start(s32[30]{0:T(128)} %hours.12) | copy-start | bytes 364
  185.1 12.9 %copy-start.33 = (s32[30]{0:T(128)S(1)}, s32[30]{0:T(128)}, u32[]{:S(2)}) copy-start(s32[30]{0:T(128)} %src_ids.1) | copy-start | bytes 364
  185.1 12.9 %copy-start.35 = (s32[30]{0:T(128)S(1)}, s32[30]{0:T(128)}, u32[]{:S(2)}) copy-start(s32[30]{0:T(128)} %dst_ids.1) | copy-start | bytes 364
  186.4 8.2 %collective-permute-start.57 = (f32[64,512]{1,0:T(8,128)S(1)}, f32[64,512]{1,0:T(8,128)S(1)}, u32[]{:S(2)}, u32[]{:S(2)}) collective-permute-start(f32[64,512]{1,0:T(8,128)S(1)} %get-tuple-element.491), channel_id=1, source_target_pairs={{0,1},{1,2},{2,3},{3,0},{4,5},{5,6},{6,7},{7,4},{8,9},{9,10},{10,1... | collective-permute-start | bytes 393224 | tf_op jit(solution)/shard_map/dst_back/ppermute | solution.py:297
  186.5 9.6 %collective-permute-start.56 = (f32[64,512]{1,0:T(8,128)S(1)}, f32[64,512]{1,0:T(8,128)S(1)}, u32[]{:S(2)}, u32[]{:S(2)}) collective-permute-start(f32[64,512]{1,0:T(8,128)S(1)} %get-tuple-element.492), channel_id=1, source_target_pairs={{0,2},{1,3},{2,0},{3,1},{4,6},{5,7},{6,4},{7,5},{8,10},{9,11},{10,... | collective-permute-start | bytes 393224 | tf_op jit(solution)/shard_map/dst_back/ppermute | solution.py:297
  189.7 6.9 %collective-permute-start.55 = (f32[64,512]{1,0:T(8,128)S(1)}, f32[64,512]{1,0:T(8,128)S(1)}, u32[]{:S(2)}, u32[]{:S(2)}) collective-permute-start(f32[64,512]{1,0:T(8,128)S(1)} %get-tuple-element.493), channel_id=1, source_target_pairs={{0,3},{1,0},{2,1},{3,2},{4,7},{5,4},{6,5},{7,6},{8,11},{9,8},{10,9... | collective-permute-start | bytes 393224 | tf_op jit(solution)/shard_map/dst_back/ppermute | solution.py:297
  (11 other events, 25.3 us)
Sparse Core Ops, SparseCore 0:
  21.7 64.2 all-gather.6
  108.9 53.6 reduce-scatter.2

commit v4 on v3

--- a/solution.py
+++ b/solution.py
@@ -159,13 +159,15 @@
 
 def tile_kernel(
     scal, lst, a0, a1, a2, a3, b_all, g_out, u0, u1, u2, u3, h0, h1, h2, h3,
-    blocks, g_sum, u_sum, entries, in_sems, out_sems,
+    a_in, blocks, g_sum, u_sum, entries, a_sems, in_sems, out_sems,
 ):
     own = scal[0]
-    a_in, u_out, h_out = (a0, a1, a2, a3), (u0, u1, u2, u3), (h0, h1, h2, h3)
+    u_out, h_out = (u0, u1, u2, u3), (h0, h1, h2, h3)
     n = lst[3 * LIST + own]
     shift = jnp.bitwise_and(lax.broadcasted_iota(i32, (32, SIDE), 0), 15)
+    left = lax.broadcasted_iota(i32, (1, SIDE), 1) < RK
     ones = jnp.ones((8, SIDE), bf16)
+    dg = lambda p, q, dims: lax.dot_general(p, q, (dims, ((), ())), preferred_element_type=f32)
 
     def place(j):
         dst_at = lst[LIST + PER * own + j]
@@ -175,36 +177,65 @@
         z, cols = place(j)
         return pltpu.make_async_copy(b_all.at[z, :, cols], blocks.at[j], in_sems.at[j])
 
+    a_copies = [pltpu.make_async_copy(a, a_in.at[d], a_sems.at[d]) for d, a in enumerate((a0, a1, a2, a3))]
+    for copy in a_copies:
+        copy.start()
+
     @pl.loop(0, n)
     def _(j):
         fetch(j).start()
 
     g_sum[...] = jnp.zeros_like(g_sum)
-
-    @pl.loop(0, n)
-    def _(j):
-        a = split(jnp.concatenate([r[j, :RK] for r in a_in], axis=0))
-        c = jnp.concatenate([as_column(r[j, RK + 2 : RK + 3, :RK]) for r in a_in], axis=0)
-        for d in range(NO):
-            rows = pl.ds(pl.multiple_of(jnp.bitwise_and(own - d, NO - 1) * 32, 32), 32)
-            words = jnp.concatenate(
-                [jnp.broadcast_to(a_in[d][j, RK + i : RK + i + 1, :], (16, SIDE)) for i in range(2)], axis=0
-            ).astype(i32)
-            entries[rows, :] = jnp.bitwise_and(jnp.right_shift(words, shift), 1).astype(f32)
-        fetch(j).wait()
-        z, cols = place(j)
-        b_raw = blocks[j]
-        b = split(b_raw * c)
-        r = split(jax.nn.sigmoid(dot3(a, b, ((0,), (0,)))) - entries[...])
-        u = dot3(b, r, ((1,), (1,)))
-        g = dot3(a, r, ((1,), (0,)))
-        g_sum[z, :, cols] += g * c
-        along = lambda x: lax.dot_general(ones, x, (((1,), (1,)), ((), ())), preferred_element_type=f32)
-        h_high, h_low = split(b_raw * g)
-        h = along(h_high) + along(h_low)
-        for d in range(NO):
-            u_sum[d, j] = u[RK * d : RK * (d + 1)]
-            h_out[d][pl.ds(j, 1), :RK] = h[:1, RK * d : RK * (d + 1)]
+    for copy in a_copies:
+        copy.wait()
+
+    @pl.loop(0, jnp.right_shift(n + 1, 1))
+    def _(pair):
+        js = 2 * pair, 2 * pair + 1
+        fetch(js[0]).wait()
+
+        @pl.when(js[1] < n)
+        def _():
+            fetch(js[1]).wait()
+
+        terms = []
+        for half, j in enumerate(js):
+            a_high, a_low = split(jnp.concatenate([a_in[d, j, :RK] for d in range(NO)], axis=0))
+            c = jnp.concatenate([as_column(a_in[d, j, RK + 2 : RK + 3, :RK]) for d in range(NO)], axis=0)
+            for d in range(NO):
+                rows = pl.ds(pl.multiple_of(jnp.bitwise_and(own - d, NO - 1) * 32, 32), 32)
+                words = jnp.concatenate(
+                    [jnp.broadcast_to(a_in[d, j, RK + i : RK + i + 1, :], (16, SIDE)) for i in range(2)], axis=0
+                ).astype(i32)
+                entries[half, rows, :] = jnp.bitwise_and(jnp.right_shift(words, shift), 1).astype(f32)
+            b_raw = blocks[j]
+            b_high, b_low = split(b_raw * c)
+            logits = dot3((a_high, a_low), (b_high, b_low), ((0,), (0,)))
+            r_high, r_low = split(jax.nn.sigmoid(logits) - entries[half])
+            u = dg(
+                jnp.concatenate([b_high, b_low], axis=1), jnp.concatenate([r_high, r_high], axis=1), ((1,), (1,))
+            ) + dg(b_high, r_low, ((1,), (1,)))
+            g = dg(
+                jnp.concatenate([a_high, a_low], axis=1), jnp.concatenate([r_high, r_high], axis=0), ((1,), (0,))
+            ) + dg(a_high, r_low, ((1,), (0,)))
+            h_high, h_low = split(b_raw * g)
+            h = (dg(ones, h_high, ((1,), (1,))) + dg(ones, h_low, ((1,), (1,))))[:1]
+            for d in range(NO):
+                u_sum[d, j] = u[RK * d : RK * (d + 1)]
+            for v in range(NO // 2):
+                x = h[:, SIDE * v : SIDE * (v + 1)]
+                y = jnp.concatenate([x[:, RK:], x[:, :RK]], axis=1)
+                h_out[2 * v][pl.ds(j, 1), :] = jnp.where(left, x, y)
+                h_out[2 * v + 1][pl.ds(j, 1), :] = jnp.where(left, y, x)
+            terms.append(g * c)
+
+        z, cols = place(js[0])
+        g_sum[z, :, cols] += terms[0]
+
+        @pl.when(js[1] < n)
+        def _():
+            z, cols = place(js[1])
+            g_sum[z, :, cols] += terms[1]
 
     copies = [pltpu.make_async_copy(g_sum.at[z], g_out.at[z], out_sems.at[z]) for z in range(NZ)]
     copies += [pltpu.make_async_copy(u_sum.at[d], u_out[d], out_sems.at[NZ + d]) for d in range(NO)]
@@ -223,14 +254,12 @@
             slot = lst[2 * LIST + k]
             g, i = jnp.right_shift(slot, 3), jnp.bitwise_and(slot, 7)
             cols = lane_block(jnp.right_shift(i, 1))
-            row = h[pl.ds(j, 1), :RK]
-            both = jnp.concatenate([row, row], axis=1)
-            hour[g, :, cols] = jnp.where(upper == jnp.bitwise_and(i, 1), both, hour[g, :, cols])
+            hour[g, :, cols] += jnp.where(upper == jnp.bitwise_and(i, 1), h[pl.ds(j, 1), :], 0.0)
 
         each_tile(scal[0], lst, d, work)
 
 
-def src_sum_kernel(scal, lst, u0, u1, u2, u3, hour_terms, keep, give):
+def src_sum_kernel(scal, lst, u0, u1, u2, u3, back, keep, give):
     own, x_at, c_at = scal[0], scal[1], scal[2]
     keep[...] = jnp.zeros_like(keep)
     give[...] = jnp.zeros_like(give)
@@ -261,9 +290,10 @@
         out[:, pl.ds(pl.multiple_of(to * PART, PART), PART)] = p[...]
 
 
-def hour_kernel(scal, hours, where, back, out):
+def hour_kernel(scal, hours, where, back, out, both):
     first_hour = scal[1]
-    out[...] = jnp.zeros_like(out)
+    both[...] = jnp.zeros_like(both)
+    upper = jnp.right_shift(lax.broadcasted_iota(i32, (1, SIDE), 1), 6)
 
     @pl.loop(0, TILE_CAP)
     def _(t):
@@ -271,11 +301,11 @@
 
         @pl.when(at >= 0)
         def _():
-            h = hours[t] - first_hour
             slot = jnp.bitwise_and(at, 7)
-            both = back[jnp.right_shift(at, 3), :, lane_block(jnp.right_shift(slot, 1))]
-            odd = jnp.broadcast_to(jnp.bitwise_and(slot, 1), (1, RK)) == 1
-            out[pl.ds(h, 1), :] += jnp.where(odd, both[:, RK:], both[:, :RK])
+            row = back[jnp.right_shift(at, 3), :, lane_block(jnp.right_shift(slot, 1))]
+            both[pl.ds(hours[t] - first_hour, 1), :] += jnp.where(upper == jnp.bitwise_and(slot, 1), row, 0.0)
+
+    out[...] = both[:, :RK] + both[:, RK:]
 
 
 def shape(*dims, dtype=f32):
@@ -355,11 +385,12 @@
             g_sum, *out = call(
                 tile_kernel,
                 (shape(NZ, RANK, PART),) + (shape(PER, RK, SIDE),) * NO + (shape(PER, SIDE),) * NO,
-                [SMEM] * 2 + [VMEM] * NO + [HBM], (at, lst, *a_in, b_all), out_specs=(HBM,) * (1 + NO) + (VMEM,) * NO,
+                [SMEM] * 2 + [HBM] * (NO + 1), (at, lst, *a_in, b_all), out_specs=(HBM,) * (1 + NO) + (VMEM,) * NO,
                 scratch=[
-                    pltpu.VMEM((PER, RANK, SIDE), f32), pltpu.VMEM((NZ, RANK, PART), f32),
-                    pltpu.VMEM((NO, PER, RK, SIDE), f32), pltpu.VMEM((SIDE, SIDE), f32),
-                    pltpu.SemaphoreType.DMA((PER,)), pltpu.SemaphoreType.DMA((NZ + NO,)),
+                    pltpu.VMEM((NO, PER, XROWS, SIDE), f32), pltpu.VMEM((PER, RANK, SIDE), f32),
+                    pltpu.VMEM((NZ, RANK, PART), f32), pltpu.VMEM((NO, PER, RK, SIDE), f32),
+                    pltpu.VMEM((2, SIDE, SIDE), f32), pltpu.SemaphoreType.DMA((NO,)), pltpu.SemaphoreType.DMA((PER,)),
+                    pltpu.SemaphoreType.DMA((NZ + NO,)),
                 ],
                 vmem=60,
             )
@@ -368,15 +399,17 @@
             hour_terms = call(hour_pack_kernel, shape(GROUPS, 1, 3 * SIDE), [SMEM] * 2 + [VMEM] * NO, (at, lst, *h))
             back = lax.all_to_all(hour_terms, SLAB, 0, 0)
             grad_hour = call(
-                hour_kernel, shape(*hour_factor.shape), [SMEM] * 3 + [VMEM], (scal, tile_hour, where, back)
+                hour_kernel, shape(*hour_factor.shape), [SMEM] * 3 + [VMEM], (scal, tile_hour, where, back),
+                scratch=[pltpu.VMEM((hour_factor.shape[0], SIDE), f32)],
             )
         with jax.named_scope("src_back"):
-            u = [hop(v, "own", NO, -d) for d, v in enumerate(out[:NO])]
+            u_out, _ = lax.optimization_barrier((out[:NO], h))
+            u = [hop(v, "own", NO, -d) for d, v in enumerate(u_out)]
             keep, give = call(
                 src_sum_kernel, (shape(NX, RK, STORED * SIDE),) * 2, [SMEM] * 2 + [VMEM] * NO + [ANY],
-                (at, lst, *u, hour_terms),
-            )
-            s, _ = lax.optimization_barrier((keep + hop(give, "c", NC, 1), back))
+                (at, lst, *u, back),
+            )
+            s = keep + hop(give, "c", NC, 1)
             top = hop(s[2, :half], "x", NX, 1)
             bottom = hop(s[2, half:], "x", NX, -1)
             one = hop(jnp.concatenate([s[1, :half] + top, s[1, half:]]), "x", NX, 1)

time: 209 us -> 191 us (0.914)
  waiting for transfers between devices: 87 us -> 62.3 us
  blocking collectives: 0 us -> 24.3 us
  Pallas kernels: 33.8 us -> 26.3 us
  starting transfers between devices: 48.7 us -> 44.2 us
  other arithmetic: 10.6 us -> 6.5 us
    all_to_all x0 -> x1, blocking collectives: none -> 24.3 us  [one_round(): back = lax.all_to_all(hour_terms, SLAB, 0, 0)]
    ppermute x29, waiting for transfers between devices: 70.7 us -> 53.2 us  [hop(): lax.ppermute(value, axis, [(i, (i + by) % size) for i in range(size)])]
    pallas_call x9, Pallas kernels: 33.8 us -> 26.3 us  [call(): pl.pallas_call(kernel, out_shape=out_shape, in_specs=in_specs, out_specs=...]
    all_to_all x1 -> x0, starting transfers between devices: 7.24 us -> none  [one_round(): back = lax.all_to_all(hour_terms, SLAB, 0, 0)]
    all_to_all x1 -> x0, waiting for transfers between devices: 7.23 us -> none  [one_round(): back = lax.all_to_all(hour_terms, SLAB, 0, 0)]
    add x1, other arithmetic: 3.31 us -> 0.25 us  [one_round(): s = keep + hop(give, 'c', NC, 1)]
    ppermute x29, starting transfers between devices: 31 us -> 33.7 us  [hop(): lax.ppermute(value, axis, [(i, (i + by) % size) for i in range(size)])]
    reshape x3, local copies, waits for them, and re-layouts: 0.39 us -> 2.67 us  [per_device(): told[:, 32 * i:32 * i + TILE_CAP].reshape(-1)]
  transfers between devices with their start and end apart: 33 -> 32, of which waited for: 17 -> 15; matrix products, arithmetic and copies ran while one was open for 7% -> 6% of each run, Pallas kernels for 9% -> 7%
where the time goes in v4:
time: 191 us; the launch traced here: 189 us
  waiting for transfers between devices  62.3 us (33%)
  starting transfers between devices  44.2 us (23%)
  Pallas kernels  26.3 us (14%)
  blocking collectives  24.3 us (13%)
  between operations  15.8 us (8%)
  local copies, waits for them, and re-layouts  8.31 us (4%)
  other arithmetic  6.5 us (3%)
    ppermute x29, waiting for transfers between devices, hop(): lax.ppermute(value, axis, [(i, (i + by) % size) for i in range(size)])  53.2 us
    ppermute x29, starting transfers between devices, hop(): lax.ppermute(value, axis, [(i, (i + by) % size) for i in range(size)])  33.7 us
    pallas_call x9, Pallas kernels, call(): pl.pallas_call(kernel, out_shape=out_shape, in_specs=in_specs, out_specs=...  26.3 us
    all_to_all x1, blocking collectives, one_round(): back = lax.all_to_all(hour_terms, SLAB, 0, 0)  24.3 us
    all_to_all x1, starting transfers between devices, one_round(): got = lax.all_to_all(sent, SLAB, 0, 0)  10.4 us
    all_to_all x1, waiting for transfers between devices, one_round(): got = lax.all_to_all(sent, SLAB, 0, 0)  9.03 us
  transfers between devices with their start and end apart: 32, of which 15 were waited for; matrix products, arithmetic and copies ran while one was open for 6% of the time, Pallas kernels for 7%

profile of v4, /device:TPU:32, one launch (start us, length us, event | category | flops | bytes accessed | tf_op | source)
XLA Modules:
  0.0 188.7 jit_solution(9561530702248732207)
XLA Ops:
  7.2 1.1 constant_dynamic-slice_fusion.4
  8.4 3.1 %collective-permute-start.31 = (f32[64,512]{1,0:T(8,128)S(1)}, f32[64,512]{1,0:T(8,128)S(1)}, u32[]{:S(2)}, u32[]{:S(2)}) collective-permute-start(f32[64,512]{1,0:T(8,128)S(1)} %get-tuple-element.504), channel_id=1, source_target_pairs={{0,3},{1,0},{2,1},{3,2},{4,7},{5,4},{6,5},{7,6},{8,11},{9,8},{10,9... | collective-permute-start | bytes 393224 | tf_op jit(solution)/shard_map/gather_dst/ppermute | solution.py:327
  12.1 1.0 collective-permute-start.29
  13.8 3.1 %slots.5 = (f32[64,16,128]{2,1,0:T(8,128)}, s32[30]{0:T(128)S(1)}) custom-call(s32[4]{0:T(128)S(1)} %pad_add_fusion.2.scal, s32[30]{0:T(128)} %src_ids.1, s32[30]{0:T(128)} %dst_ids.1, s32[30]{0:T(128)} %hours.15, s32[1024]{0:T(1024)} %src_place.1, s32[1024]{0:T(1024)} %dst_place.1, s32[30,8,128]{2,1,0:T(8,128)} %bits.1, f32[8,64]{1,0:T(8,128)} %hour_rows.1), custom_call_target="tpu_custom_call" | custom-call | tf_op jit(solution)/shard_map/slots/pallas_call | solution.py:318
  17.0 2.3 %collective-permute-done.30.p2 = f32[64,512]{1,0:T(8,128)S(1)} collective-permute-done((f32[64,512]{1,0:T(8,128)S(1)}, f32[64,512]{1,0:T(8,128)S(1)}, u32[]{:S(2)}, u32[]{:S(2)}) %collective-permute-start.30) | collective-permute-done | bytes 131104 | tf_op jit(solution)/shard_map/gather_dst/ppermute | solution.py:327
  19.3 1.4 collective-permute-done.29.p1
  20.7 0.8 gather_dst.5
  21.6 1.6 collective-permute-start.33
  23.2 1.7 collective-permute-start.32
  24.9 10.4 %all-to-all-start.2 = ((f32[64,16,128]{2,1,0:T(8,128)}), f32[64,16,128]{2,1,0:T(8,128)S(1)}, u32[]{:S(2)}, u32[]{:S(2)}) async-start(f32[64,16,128]{2,1,0:T(8,128)} %get-tuple-element.392), calls=%async_computation.3 | async-start | bytes 1048576 | tf_op jit(solution)/shard_map/slots/all_to_all | solution.py:359
  35.6 1.2 collective-permute-done.33.a30
  37.8 3.0 %collective-permute-start.35 = (f32[32,2048]{1,0:T(8,128)S(1)}, f32[32,2048]{1,0:T(8,128)}, u32[]{:S(2)}, u32[]{:S(2)}) collective-permute-start(f32[32,2048]{1,0:T(8,128)S(1)} %slice.192), channel_id=1, source_target_pairs={{0,24},{8,0},{16,8},{24,16},{1,25},{9,1},{17,9},{25,17},{2,26},{10... | collective-permute-start | bytes 786440 | tf_op jit(solution)/shard_map/gather_src/ppermute | solution.py:327
  40.8 6.8 %collective-permute-done.34.a2t0 = f32[32,2048]{1,0:T(8,128)S(1)} collective-permute-done((f32[32,2048]{1,0:T(8,128)S(1)}, f32[32,2048]{1,0:T(8,128)S(1)}, u32[]{:S(2)}, u32[]{:S(2)}) %collective-permute-start.34) | collective-permute-done | bytes 262176 | tf_op jit(solution)/shard_map/gather_src/ppermute | solution.py:327
  47.6 1.4 collective-permute-done.35.a2b0
  49.1 9.0 %all-to-all-done.2.got = f32[64,16,128]{2,1,0:T(8,128)S(1)} async-done(((f32[64,16,128]{2,1,0:T(8,128)}), f32[64,16,128]{2,1,0:T(8,128)S(1)}, u32[]{:S(2)}, u32[]{:S(2)}) %all-to-all-start.2) | async-done | bytes 524320 | tf_op jit(solution)/shard_map/slots/all_to_all | solution.py:359
  58.1 3.5 %list.2.lst = s32[200]{0:T(256)S(1)} custom-call(s32[4]{0:T(128)S(1)} %pad_add_fusion.3.scal, f32[64,16,128]{2,1,0:T(8,128)S(1)} %all-to-all-done.2.got), custom_call_target="tpu_custom_call" | custom-call | tf_op jit(solution)/shard_map/list/pallas_call | solution.py:318
  61.7 2.4 %src_exchange.5 = (f32[16,72,128]{2,1,0:T(8,128)S(1)}, f32[16,72,128]{2,1,0:T(8,128)S(1)}, f32[16,72,128]{2,1,0:T(8,128)S(1)}, f32[16,72,128]{2,1,0:T(8,128)S(1)}) custom-call(s32[4]{0:T(128)S(1)} %pad_add_fusion.3.scal, s32[200]{0:T(256)S(1)} %list.2.lst, f32[1024,128]{1,0:T(8,128)S(1)} %bitcast.103, f32[64,2048]{1,0:T(8,128)} %a00, ...), custom_call_target="tpu_custom_call" | custom-call | tf_op jit(solution)/shard_map/src_exchange/pallas_call | solution.py:318
  64.1 0.8 copy-done.6
  64.9 2.0 %collective-permute-start.42 = (f32[16,72,128]{2,1,0:T(8,128)S(1)}, f32[16,72,128]{2,1,0:T(8,128)S(1)}, u32[]{:S(2)}, u32[]{:S(2)}) collective-permute-start(f32[16,72,128]{2,1,0:T(8,128)S(1)} %get-tuple-element.401), channel_id=1, source_target_pairs={{0,2},{1,3},{2,0},{3,1},{4,6},{5,7},{6,4},{7,5},{8,10},{9,11},{10,... | collective-permute-start | bytes 1769480 | tf_op jit(solution)/shard_map/src_exchange/ppermute | solution.py:327
  67.0 1.3 collective-permute-start.43
  68.2 26.6 %collective-permute-done.41.a1 = f32[16,72,128]{2,1,0:T(8,128)S(1)} collective-permute-done((f32[16,72,128]{2,1,0:T(8,128)S(1)}, f32[16,72,128]{2,1,0:T(8,128)S(1)}, u32[]{:S(2)}, u32[]{:S(2)}) %collective-permute-start.41) | collective-permute-done | bytes 589856 | tf_op jit(solution)/shard_map/src_exchange/ppermute | solution.py:327
  96.3 11.3 %tiles.5 = (f32[8,256,512]{2,1,0:T(8,128)}, f32[16,64,128]{2,1,0:T(8,128)}, f32[16,64,128]{2,1,0:T(8,128)}, f32[16,64,128]{2,1,0:T(8,128)}, f32[16,64,128]{2,1,0...) custom-call(s32[4]{0:T(128)} %copy-done.11, s32[200]{0:T(256)} %copy-done.9, ...), custom_call_target="tpu_custom_call" | custom-call | tf_op jit(solution)/shard_map/tiles/pallas_call | solution.py:318
  108.3 2.1 %collective-permute-start.46 = (f32[16,128]{1,0:T(8,128)S(1)}, f32[16,128]{1,0:T(8,128)S(1)}, u32[]{:S(2)}, u32[]{:S(2)}) collective-permute-start(f32[16,128]{1,0:T(8,128)S(1)} %copy-done.41), channel_id=1, source_target_pairs={{0,1},{1,2},{2,3},{3,0},{4,5},{5,6},{6,7},{7,4},{8,9},{9,10},{10,1... | collective-permute-start | bytes 24584 | tf_op jit(solution)/shard_map/hours/ppermute | solution.py:327
  110.4 1.5 collective-permute-done.44.h1
  111.9 1.5 collective-permute-done.45.h2
  113.5 1.2 collective-permute-done.46.h3
  114.6 2.0 %collective-permute-start.47 = (f32[16,64,128]{2,1,0:T(8,128)}, f32[16,64,128]{2,1,0:T(8,128)S(1)}, u32[]{:S(2)}, u32[]{:S(2)}) collective-permute-start(f32[16,64,128]{2,1,0:T(8,128)} %get-tuple-element.412), channel_id=1, source_target_pairs={{0,3},{1,0},{2,1},{3,2},{4,7},{5,4},{6,5},{7,6},{8,11},{9,8},{10,9... | collective-permute-start | bytes 1572872 | tf_op jit(solution)/shard_map/src_back/ppermute | solution.py:327
  116.6 0.9 collective-permute-start.48
  118.4 24.3 %all_to_all.22.back = f32[64,1,384]{2,1,0:T(1,128)S(1)} all-to-all(f32[64,1,384]{2,1,0:T(1,128)S(1)} %hours.13), channel_id=1, replica_groups=mesh['z'=8,'x'=4,'c'=2,'own'=4] {'z','x','c'}, dimensions={0} | all-to-all | bytes 196608 | tf_op jit(solution)/shard_map/hours/all_to_all | solution.py:400
  142.7 1.3 src_back.5
  144.5 3.8 %collective-permute-done.50 = f32[4,64,2048]{2,1,0:T(8,128)S(1)} collective-permute-done((f32[4,64,2048]{2,1,0:T(8,128)S(1)}, f32[4,64,2048]{2,1,0:T(8,128)S(1)}, u32[]{:S(2)}, u32[]{:S(2)}) %collective-permute-start.50) | collective-permute-done | bytes 2097184 | tf_op jit(solution)/shard_map/src_back/ppermute | solution.py:327
  150.0 2.5 %collective-permute-start.53 = (f32[32,2048]{1,0:T(8,128)S(1)}, f32[32,2048]{1,0:T(8,128)S(1)}, u32[]{:S(2)}, u32[]{:S(2)}) collective-permute-start(f32[32,2048]{1,0:T(8,128)S(1)} %get-tuple-element.497), channel_id=1, source_target_pairs={{0,24},{8,0},{16,8},{24,16},{1,25},{9,1},{17,9},{25,17},{2,26},{10... | collective-permute-start | bytes 786440 | tf_op jit(solution)/shard_map/src_back/ppermute | solution.py:327
  152.5 1.4 slice_sign_fusion
  154.0 0.9 reshape.209
  154.9 0.9 reshape.207
  155.8 0.9 reshape.208
  156.7 2.6 %collective-permute-done.51 = f32[32,2048]{1,0:T(8,128)S(1)} collective-permute-done((f32[32,2048]{1,0:T(8,128)}, f32[32,2048]{1,0:T(8,128)S(1)}, u32[]{:S(2)}, u32[]{:S(2)}) %collective-permute-start.51) | collective-permute-done | bytes 262176 | tf_op jit(solution)/shard_map/src_back/ppermute | solution.py:327
  159.4 2.8 %collective-permute-start.54 = (f32[64,2048]{1,0:T(8,128)S(1)}, f32[64,2048]{1,0:T(8,128)}, u32[]{:S(2)}, u32[]{:S(2)}) collective-permute-start(f32[64,2048]{1,0:T(8,128)S(1)} %pad_maximum_fusion.3), channel_id=1, source_target_pairs={{0,24},{8,0},{16,8},{24,16},{1,25},{9,1},{17,9},{25,17},{2,26},{10... | collective-permute-start | bytes 1572872 | tf_op jit(solution)/shard_map/src_back/ppermute | solution.py:327
  162.2 0.8 pad_maximum_fusion.2
  165.5 1.7 hours.14
  167.3 1.2 slice_bitcast_fusion.18
  168.5 1.4 collective-permute-start.57
  169.9 2.8 %collective-permute-start.56 = (f32[64,512]{1,0:T(8,128)S(1)}, f32[64,512]{1,0:T(8,128)S(1)}, u32[]{:S(2)}, u32[]{:S(2)}) collective-permute-start(f32[64,512]{1,0:T(8,128)S(1)} %get-tuple-element.501), channel_id=1, source_target_pairs={{0,2},{1,3},{2,0},{3,1},{4,6},{5,7},{6,4},{7,5},{8,10},{9,11},{10,... | collective-permute-start | bytes 393224 | tf_op jit(solution)/shard_map/dst_back/ppermute | solution.py:327
  172.7 2.5 %collective-permute-start.55 = (f32[64,512]{1,0:T(8,128)S(1)}, f32[64,512]{1,0:T(8,128)S(1)}, u32[]{:S(2)}, u32[]{:S(2)}) collective-permute-start(f32[64,512]{1,0:T(8,128)S(1)} %get-tuple-element.502), channel_id=1, source_target_pairs={{0,3},{1,0},{2,1},{3,2},{4,7},{5,4},{6,5},{7,6},{8,11},{9,8},{10,9... | collective-permute-start | bytes 393224 | tf_op jit(solution)/shard_map/dst_back/ppermute | solution.py:327
  175.2 2.1 %collective-permute-done.52 = f32[64,2048]{1,0:T(8,128)} collective-permute-done((f32[64,2048]{1,0:T(8,128)}, f32[64,2048]{1,0:T(8,128)}, u32[]{:S(2)}, u32[]{:S(2)}) %collective-permute-start.52) | collective-permute-done | bytes 524320 | tf_op jit(solution)/shard_map/src_back/ppermute | solution.py:327
  177.4 2.1 %fusion.11 = f32[64,2048]{1,0:T(8,128)} fusion(f32[64,2048]{1,0:T(8,128)} %collective-permute-done.54, f32[64,2048]{1,0:T(8,128)} %collective-permute-done.52, f32[4,64,2048]{2,1,0:T(8,128)S(1)} %add.201), kind=kLoop, calls=%fused_computation.38 | loop fusion | flops 262144 | bytes 2097152 | tf_op jit(solution)/shard_map/src_back/add | solution.py:417
  179.5 1.4 dst_back.5
  180.9 0.9 while.18
  (99 shorter events, 9.2 us)
Async XLA Ops:
  7.2 88.3 %all-gather.7.cloned.1.call-start = ((), (), s32[]{:S(2)}) async-start(), calls=%async_computation.7 | async-start | bytes 4718592 | tf_op jit(solution)/shard_map/gather_dst/all_gather | solution.py:357
  8.4 8.7 %collective-permute-start.31 = (f32[64,512]{1,0:T(8,128)S(1)}, f32[64,512]{1,0:T(8,128)S(1)}, u32[]{:S(2)}, u32[]{:S(2)}) collective-permute-start(f32[64,512]{1,0:T(8,128)S(1)} %get-tuple-element.504), channel_id=1, source_target_pairs={{0,3},{1,0},{2,1},{3,2},{4,7},{5,4},{6,5},{7,6},{8,11},{9,8},{10,9... | collective-permute-start | bytes 393224 | tf_op jit(solution)/shard_map/gather_dst/ppermute | solution.py:327
  11.5 7.9 %collective-permute-start.30 = (f32[64,512]{1,0:T(8,128)S(1)}, f32[64,512]{1,0:T(8,128)S(1)}, u32[]{:S(2)}, u32[]{:S(2)}) collective-permute-start(f32[64,512]{1,0:T(8,128)S(1)} %get-tuple-element.505), channel_id=1, source_target_pairs={{0,2},{1,3},{2,0},{3,1},{4,6},{5,7},{6,4},{7,5},{8,10},{9,11},{10,... | collective-permute-start | bytes 393224 | tf_op jit(solution)/shard_map/gather_dst/ppermute | solution.py:327
  12.1 8.6 %collective-permute-start.29 = (f32[64,512]{1,0:T(8,128)S(1)}, f32[64,512]{1,0:T(8,128)S(1)}, u32[]{:S(2)}, u32[]{:S(2)}) collective-permute-start(f32[64,512]{1,0:T(8,128)S(1)} %get-tuple-element.506), channel_id=1, source_target_pairs={{0,1},{1,2},{2,3},{3,0},{4,5},{5,6},{6,7},{7,4},{8,9},{9,10},{10,1... | collective-permute-start | bytes 393224 | tf_op jit(solution)/shard_map/gather_dst/ppermute | solution.py:327
  21.6 15.2 %collective-permute-start.33 = (f32[64,2048]{1,0:T(8,128)}, f32[64,2048]{1,0:T(8,128)S(1)}, u32[]{:S(2)}, u32[]{:S(2)}) collective-permute-start(f32[64,2048]{1,0:T(8,128)} %a00), channel_id=1, source_target_pairs={{0,8},{8,16},{16,24},{24,0},{1,9},{9,17},{17,25},{25,1},{2,10},{10... | collective-permute-start | bytes 1572872 | tf_op jit(solution)/shard_map/gather_src/ppermute | solution.py:327
  23.2 14.1 %collective-permute-start.32 = (f32[64,2048]{1,0:T(8,128)}, f32[64,2048]{1,0:T(8,128)S(1)}, u32[]{:S(2)}, u32[]{:S(2)}) collective-permute-start(f32[64,2048]{1,0:T(8,128)} %a00), channel_id=1, source_target_pairs={{0,24},{8,0},{16,8},{24,16},{1,25},{9,1},{17,9},{25,17},{2,26},{10... | collective-permute-start | bytes 1572872 | tf_op jit(solution)/shard_map/gather_src/ppermute | solution.py:327
  24.9 33.2 %all-to-all-start.2 = ((f32[64,16,128]{2,1,0:T(8,128)}), f32[64,16,128]{2,1,0:T(8,128)S(1)}, u32[]{:S(2)}, u32[]{:S(2)}) async-start(f32[64,16,128]{2,1,0:T(8,128)} %get-tuple-element.392), calls=%async_computation.3 | async-start | bytes 1048576 | tf_op jit(solution)/shard_map/slots/all_to_all | solution.py:359
  35.3 132.0 %reduce-scatter.3.cloned.1.call-start = ((), (), s32[]{:S(2)}) async-start(), calls=%async_computation.6 | async-start | bytes 4718592 | tf_op jit(solution)/shard_map/dst_back/reduce_scatter | solution.py:419
  35.3 26.3 %collective-permute-start.36 = (f32[64,2048]{1,0:T(8,128)}, f32[64,2048]{1,0:T(8,128)S(1)}, u32[]{:S(2)}, u32[]{:S(2)}) collective-permute-start(f32[64,2048]{1,0:T(8,128)} %a00), channel_id=1, source_target_pairs={{0,4},{4,0},{1,5},{5,1},{2,6},{6,2},{3,7},{7,3},{8,12},{12,8},{9,1... | collective-permute-start | bytes 1572872 | tf_op jit(solution)/shard_map/gather_src/ppermute | solution.py:327
  36.8 10.8 %collective-permute-start.34 = (f32[32,2048]{1,0:T(8,128)S(1)}, f32[32,2048]{1,0:T(8,128)S(1)}, u32[]{:S(2)}, u32[]{:S(2)}) collective-permute-start(f32[32,2048]{1,0:T(8,128)S(1)} %slice.191), channel_id=1, source_target_pairs={{0,8},{8,16},{16,24},{24,0},{1,9},{9,17},{17,25},{25,1},{2,10},{10... | collective-permute-start | bytes 786440 | tf_op jit(solution)/shard_map/gather_src/ppermute | solution.py:327
  37.2 24.4 %collective-permute-start.38 = (f32[64,2048]{1,0:T(8,128)S(1)}, f32[64,2048]{1,0:T(8,128)S(1)}, u32[]{:S(2)}, u32[]{:S(2)}) collective-permute-start(f32[64,2048]{1,0:T(8,128)S(1)} %collective-permute-done.33.a30), channel_id=1, source_target_pairs={{0,4},{4,0},{1,5},{5,1},{2,6},{6,2},{3,7},{7,3},{8,12},{12,8},{9,1... | collective-permute-start | bytes 1572872 | tf_op jit(solution)/shard_map/gather_src/ppermute | solution.py:327
  37.2 24.4 %collective-permute-start.37 = (f32[64,2048]{1,0:T(8,128)S(1)}, f32[64,2048]{1,0:T(8,128)S(1)}, u32[]{:S(2)}, u32[]{:S(2)}) collective-permute-start(f32[64,2048]{1,0:T(8,128)S(1)} %collective-permute-done.32.a10), channel_id=1, source_target_pairs={{0,4},{4,0},{1,5},{5,1},{2,6},{6,2},{3,7},{7,3},{8,12},{12,8},{9,1... | collective-permute-start | bytes 1572872 | tf_op jit(solution)/shard_map/gather_src/ppermute | solution.py:327
  37.8 11.2 %collective-permute-start.35 = (f32[32,2048]{1,0:T(8,128)S(1)}, f32[32,2048]{1,0:T(8,128)}, u32[]{:S(2)}, u32[]{:S(2)}) collective-permute-start(f32[32,2048]{1,0:T(8,128)S(1)} %slice.192), channel_id=1, source_target_pairs={{0,24},{8,0},{16,8},{24,16},{1,25},{9,1},{17,9},{25,17},{2,26},{10... | collective-permute-start | bytes 786440 | tf_op jit(solution)/shard_map/gather_src/ppermute | solution.py:327
  47.6 14.0 %collective-permute-start.39 = (f32[32,2048]{1,0:T(8,128)S(1)}, f32[32,2048]{1,0:T(8,128)}, u32[]{:S(2)}, u32[]{:S(2)}) collective-permute-start(f32[32,2048]{1,0:T(8,128)S(1)} %collective-permute-done.34.a2t0), channel_id=1, source_target_pairs={{0,4},{4,0},{1,5},{5,1},{2,6},{6,2},{3,7},{7,3},{8,12},{12,8},{9,1... | collective-permute-start | bytes 786440 | tf_op jit(solution)/shard_map/gather_src/ppermute | solution.py:327
  49.0 12.7 %collective-permute-start.40 = (f32[32,2048]{1,0:T(8,128)}, f32[32,2048]{1,0:T(8,128)}, u32[]{:S(2)}, u32[]{:S(2)}) collective-permute-start(f32[32,2048]{1,0:T(8,128)} %collective-permute-done.35.a2b0), channel_id=1, source_target_pairs={{0,4},{4,0},{1,5},{5,1},{2,6},{6,2},{3,7},{7,3},{8,12},{12,8},{9,1... | collective-permute-start | bytes 786440 | tf_op jit(solution)/shard_map/gather_src/ppermute | solution.py:327
  49.1 15.0 %copy-start.11 = (s32[4]{0:T(128)}, s32[4]{0:T(128)S(1)}, u32[]{:S(2)}) copy-start(s32[4]{0:T(128)S(1)} %pad_add_fusion.3.scal) | copy-start | bytes 52
  64.9 29.9 %collective-permute-start.41 = (f32[16,72,128]{2,1,0:T(8,128)S(1)}, f32[16,72,128]{2,1,0:T(8,128)S(1)}, u32[]{:S(2)}, u32[]{:S(2)}) collective-permute-start(f32[16,72,128]{2,1,0:T(8,128)S(1)} %get-tuple-element.400), channel_id=1, source_target_pairs={{0,1},{1,2},{2,3},{3,0},{4,5},{5,6},{6,7},{7,4},{8,9},{9,10},{10,1... | collective-permute-start | bytes 1769480 | tf_op jit(solution)/shard_map/src_exchange/ppermute | solution.py:327
  64.9 29.9 %collective-permute-start.42 = (f32[16,72,128]{2,1,0:T(8,128)S(1)}, f32[16,72,128]{2,1,0:T(8,128)S(1)}, u32[]{:S(2)}, u32[]{:S(2)}) collective-permute-start(f32[16,72,128]{2,1,0:T(8,128)S(1)} %get-tuple-element.401), channel_id=1, source_target_pairs={{0,2},{1,3},{2,0},{3,1},{4,6},{5,7},{6,4},{7,5},{8,10},{9,11},{10,... | collective-permute-start | bytes 1769480 | tf_op jit(solution)/shard_map/src_exchange/ppermute | solution.py:327
  67.0 28.5 %collective-permute-start.43 = (f32[16,72,128]{2,1,0:T(8,128)S(1)}, f32[16,72,128]{2,1,0:T(8,128)S(1)}, u32[]{:S(2)}, u32[]{:S(2)}) collective-permute-start(f32[16,72,128]{2,1,0:T(8,128)S(1)} %get-tuple-element.402), channel_id=1, source_target_pairs={{0,3},{1,0},{2,1},{3,2},{4,7},{5,4},{6,5},{7,6},{8,11},{9,8},{10,9... | collective-permute-start | bytes 1769480 | tf_op jit(solution)/shard_map/src_exchange/ppermute | solution.py:327
  107.6 9.0 %copy-start.40 = (f32[16,64,128]{2,1,0:T(8,128)S(1)}, f32[16,64,128]{2,1,0:T(8,128)}, u32[]{:S(2)}) copy-start(f32[16,64,128]{2,1,0:T(8,128)} %get-tuple-element.413) | copy-start | bytes 1572868
  107.6 9.9 %copy-start.38 = (f32[16,64,128]{2,1,0:T(8,128)S(1)}, f32[16,64,128]{2,1,0:T(8,128)}, u32[]{:S(2)}) copy-start(f32[16,64,128]{2,1,0:T(8,128)} %get-tuple-element.414) | copy-start | bytes 1572868
  107.6 9.9 %copy-start.10 = (s32[200]{0:T(256)S(1)}, s32[200]{0:T(256)}, u32[]{:S(2)}) copy-start(s32[200]{0:T(256)} %copy-done.9) | copy-start | bytes 2404
  107.6 9.9 %copy-start.12 = (s32[4]{0:T(128)S(1)}, s32[4]{0:T(128)}, u32[]{:S(2)}) copy-start(s32[4]{0:T(128)} %copy-done.11) | copy-start | bytes 52
  107.7 9.9 %copy-start.13 = (f32[16,128]{1,0:T(8,128)S(1)}, f32[16,128]{1,0:T(8,128)}, u32[]{:S(2)}) copy-start(f32[16,128]{1,0:T(8,128)} %get-tuple-element.407.h0) | copy-start | bytes 24580
  107.7 35.0 %copy-start.7 = (f32[16,64,128]{2,1,0:T(8,128)S(1)}, f32[16,64,128]{2,1,0:T(8,128)}, u32[]{:S(2)}) copy-start(f32[16,64,128]{2,1,0:T(8,128)} %get-tuple-element.411.u0) | copy-start | bytes 1572868
  108.3 3.7 %collective-permute-start.44 = (f32[16,128]{1,0:T(8,128)S(1)}, f32[16,128]{1,0:T(8,128)S(1)}, u32[]{:S(2)}, u32[]{:S(2)}) collective-permute-start(f32[16,128]{1,0:T(8,128)S(1)} %copy-done.45), channel_id=1, source_target_pairs={{0,3},{1,0},{2,1},{3,2},{4,7},{5,4},{6,5},{7,6},{8,11},{9,8},{10,9... | collective-permute-start | bytes 24584 | tf_op jit(solution)/shard_map/hours/ppermute | solution.py:327
  108.3 5.2 %collective-permute-start.45 = (f32[16,128]{1,0:T(8,128)S(1)}, f32[16,128]{1,0:T(8,128)S(1)}, u32[]{:S(2)}, u32[]{:S(2)}) collective-permute-start(f32[16,128]{1,0:T(8,128)S(1)} %copy-done.43), channel_id=1, source_target_pairs={{0,2},{1,3},{2,0},{3,1},{4,6},{5,7},{6,4},{7,5},{8,10},{9,11},{10,... | collective-permute-start | bytes 24584 | tf_op jit(solution)/shard_map/hours/ppermute | solution.py:327
  108.3 6.3 %collective-permute-start.46 = (f32[16,128]{1,0:T(8,128)S(1)}, f32[16,128]{1,0:T(8,128)S(1)}, u32[]{:S(2)}, u32[]{:S(2)}) collective-permute-start(f32[16,128]{1,0:T(8,128)S(1)} %copy-done.41), channel_id=1, source_target_pairs={{0,1},{1,2},{2,3},{3,0},{4,5},{5,6},{6,7},{7,4},{8,9},{9,10},{10,1... | collective-permute-start | bytes 24584 | tf_op jit(solution)/shard_map/hours/ppermute | solution.py:327
  114.6 28.1 %collective-permute-start.47 = (f32[16,64,128]{2,1,0:T(8,128)}, f32[16,64,128]{2,1,0:T(8,128)S(1)}, u32[]{:S(2)}, u32[]{:S(2)}) collective-permute-start(f32[16,64,128]{2,1,0:T(8,128)} %get-tuple-element.412), channel_id=1, source_target_pairs={{0,3},{1,0},{2,1},{3,2},{4,7},{5,4},{6,5},{7,6},{8,11},{9,8},{10,9... | collective-permute-start | bytes 1572872 | tf_op jit(solution)/shard_map/src_back/ppermute | solution.py:327
  116.6 26.0 %collective-permute-start.48 = (f32[16,64,128]{2,1,0:T(8,128)S(1)}, f32[16,64,128]{2,1,0:T(8,128)S(1)}, u32[]{:S(2)}, u32[]{:S(2)}) collective-permute-start(f32[16,64,128]{2,1,0:T(8,128)S(1)} %copy-done.40), channel_id=1, source_target_pairs={{0,2},{1,3},{2,0},{3,1},{4,6},{5,7},{6,4},{7,5},{8,10},{9,11},{10,... | collective-permute-start | bytes 1572872 | tf_op jit(solution)/shard_map/src_back/ppermute | solution.py:327
  117.5 25.1 %collective-permute-start.49 = (f32[16,64,128]{2,1,0:T(8,128)S(1)}, f32[16,64,128]{2,1,0:T(8,128)S(1)}, u32[]{:S(2)}, u32[]{:S(2)}) collective-permute-start(f32[16,64,128]{2,1,0:T(8,128)S(1)} %copy-done.38), channel_id=1, source_target_pairs={{0,1},{1,2},{2,3},{3,0},{4,5},{5,6},{6,7},{7,4},{8,9},{9,10},{10,1... | collective-permute-start | bytes 1572872 | tf_op jit(solution)/shard_map/src_back/ppermute | solution.py:327
  144.0 4.2 %collective-permute-start.50 = (f32[4,64,2048]{2,1,0:T(8,128)S(1)}, f32[4,64,2048]{2,1,0:T(8,128)S(1)}, u32[]{:S(2)}, u32[]{:S(2)}) collective-permute-start(f32[4,64,2048]{2,1,0:T(8,128)S(1)} %get-tuple-element.416), channel_id=1, source_target_pairs={{0,4},{4,0},{1,5},{5,1},{2,6},{6,2},{3,7},{7,3},{8,12},{12,8},{9,1... | collective-permute-start | bytes 6291464 | tf_op jit(solution)/shard_map/src_back/ppermute | solution.py:327
  149.3 16.1 %copy-start.31 = (s32[30]{0:T(128)S(1)}, s32[30]{0:T(128)}, u32[]{:S(2)}) copy-start(s32[30]{0:T(128)} %hours.15) | copy-start | bytes 364
  149.3 10.0 %collective-permute-start.51 = (f32[32,2048]{1,0:T(8,128)}, f32[32,2048]{1,0:T(8,128)S(1)}, u32[]{:S(2)}, u32[]{:S(2)}) collective-permute-start(f32[32,2048]{1,0:T(8,128)} %get-tuple-element.496), channel_id=1, source_target_pairs={{0,8},{8,16},{16,24},{24,0},{1,9},{9,17},{17,25},{25,1},{2,10},{10... | collective-permute-start | bytes 786440 | tf_op jit(solution)/shard_map/src_back/ppermute | solution.py:327
  150.0 9.3 %collective-permute-start.53 = (f32[32,2048]{1,0:T(8,128)S(1)}, f32[32,2048]{1,0:T(8,128)S(1)}, u32[]{:S(2)}, u32[]{:S(2)}) collective-permute-start(f32[32,2048]{1,0:T(8,128)S(1)} %get-tuple-element.497), channel_id=1, source_target_pairs={{0,24},{8,0},{16,8},{24,16},{1,25},{9,1},{17,9},{25,17},{2,26},{10... | collective-permute-start | bytes 786440 | tf_op jit(solution)/shard_map/src_back/ppermute | solution.py:327
  159.3 6.0 %copy-start.30 = (s32[64,30]{1,0:T(8,128)S(1)}, s32[64,30]{1,0:T(8,128)}, u32[]{:S(2)}) copy-start(s32[64,30]{1,0:T(8,128)} %get-tuple-element.508) | copy-start | bytes 23044
  159.4 15.8 %collective-permute-start.54 = (f32[64,2048]{1,0:T(8,128)S(1)}, f32[64,2048]{1,0:T(8,128)}, u32[]{:S(2)}, u32[]{:S(2)}) collective-permute-start(f32[64,2048]{1,0:T(8,128)S(1)} %pad_maximum_fusion.3), channel_id=1, source_target_pairs={{0,24},{8,0},{16,8},{24,16},{1,25},{9,1},{17,9},{25,17},{2,26},{10... | collective-permute-start | bytes 1572872 | tf_op jit(solution)/shard_map/src_back/ppermute | solution.py:327
  163.1 14.3 %collective-permute-start.52 = (f32[64,2048]{1,0:T(8,128)}, f32[64,2048]{1,0:T(8,128)}, u32[]{:S(2)}, u32[]{:S(2)}) collective-permute-start(f32[64,2048]{1,0:T(8,128)} %pad_maximum_fusion.2), channel_id=1, source_target_pairs={{0,8},{8,16},{16,24},{24,0},{1,9},{9,17},{17,25},{25,1},{2,10},{10... | collective-permute-start | bytes 1572872 | tf_op jit(solution)/shard_map/src_back/ppermute | solution.py:327
  167.2 13.7 %copy-start.22 = (s32[30,8,128]{2,1,0:T(8,128)S(1)}, s32[30,8,128]{2,1,0:T(8,128)}, u32[]{:S(2)}) copy-start(s32[30,8,128]{2,1,0:T(8,128)} %bits.1) | copy-start | bytes 368644
  167.2 13.7 %copy-start.27 = (s32[1024]{0:T(1024)S(1)}, s32[1024]{0:T(1024)}, u32[]{:S(2)}) copy-start(s32[1024]{0:T(1024)} %src_place.1) | copy-start | bytes 12292
  167.2 13.7 %copy-start.28 = (s32[1024]{0:T(1024)S(1)}, s32[1024]{0:T(1024)}, u32[]{:S(2)}) copy-start(s32[1024]{0:T(1024)} %dst_place.1) | copy-start | bytes 12292
  167.2 13.7 %copy-start.29 = (f32[8,64]{1,0:T(8,128)S(1)}, f32[8,64]{1,0:T(8,128)}, u32[]{:S(2)}) copy-start(f32[8,64]{1,0:T(8,128)} %hour_rows.1) | copy-start | bytes 6148
  167.2 13.7 %copy-start.32 = (s32[30]{0:T(128)S(1)}, s32[30]{0:T(128)}, u32[]{:S(2)}) copy-start(s32[30]{0:T(128)} %hours.15) | copy-start | bytes 364
  167.2 13.7 %copy-start.34 = (s32[30]{0:T(128)S(1)}, s32[30]{0:T(128)}, u32[]{:S(2)}) copy-start(s32[30]{0:T(128)} %src_ids.1) | copy-start | bytes 364
  167.2 13.7 %copy-start.36 = (s32[30]{0:T(128)S(1)}, s32[30]{0:T(128)}, u32[]{:S(2)}) copy-start(s32[30]{0:T(128)} %dst_ids.1) | copy-start | bytes 364
  168.5 11.0 %collective-permute-start.57 = (f32[64,512]{1,0:T(8,128)S(1)}, f32[64,512]{1,0:T(8,128)S(1)}, u32[]{:S(2)}, u32[]{:S(2)}) collective-permute-start(f32[64,512]{1,0:T(8,128)S(1)} %get-tuple-element.500), channel_id=1, source_target_pairs={{0,1},{1,2},{2,3},{3,0},{4,5},{5,6},{6,7},{7,4},{8,9},{9,10},{10,1... | collective-permute-start | bytes 393224 | tf_op jit(solution)/shard_map/dst_back/ppermute | solution.py:327
  169.9 9.6 %collective-permute-start.56 = (f32[64,512]{1,0:T(8,128)S(1)}, f32[64,512]{1,0:T(8,128)S(1)}, u32[]{:S(2)}, u32[]{:S(2)}) collective-permute-start(f32[64,512]{1,0:T(8,128)S(1)} %get-tuple-element.501), channel_id=1, source_target_pairs={{0,2},{1,3},{2,0},{3,1},{4,6},{5,7},{6,4},{7,5},{8,10},{9,11},{10,... | collective-permute-start | bytes 393224 | tf_op jit(solution)/shard_map/dst_back/ppermute | solution.py:327
  172.7 6.8 %collective-permute-start.55 = (f32[64,512]{1,0:T(8,128)S(1)}, f32[64,512]{1,0:T(8,128)S(1)}, u32[]{:S(2)}, u32[]{:S(2)}) collective-permute-start(f32[64,512]{1,0:T(8,128)S(1)} %get-tuple-element.502), channel_id=1, source_target_pairs={{0,3},{1,0},{2,1},{3,2},{4,7},{5,4},{6,5},{7,6},{8,11},{9,8},{10,9... | collective-permute-start | bytes 393224 | tf_op jit(solution)/shard_map/dst_back/ppermute | solution.py:327
  (8 other events, 8.1 us)
Sparse Core Ops, SparseCore 0:
  21.7 64.2 all-gather.6
  107.8 53.9 reduce-scatter.2
